TPU v7x, 256 devices: a whole 4x4x8 slice. The times are simulated.
256 devices in a mesh: chan: 128 (over x_hi, y, z, core), tile: 2 (over x_lo).
Axes of the slice: x: 4 (x_hi: 2, x_lo: 2; x = x_hi * 2 + x_lo), y: 4, z: 8, core: 2. Of those that a mesh axis runs over, the one named last changes fastest.
Arguments:
- raw_strain: bfloat16 [4096, 131072], P(('chan', 'tile')), may hold values from -6 to 6
- fir_taps: bfloat16 [128], replicated, may hold values from -0.5 to 0.5
- fan_band: int32 [4096, 256], P(None, 'tile'), may hold values from 0 to 7
- band_gain: float32 [8], replicated, may hold values from 0 to 1
Outputs:
- filtered: float32 [4096, 32768], P(('chan', 'tile'))
All inputs are finite; a program needn't handle non-finite values.
Results may differ from a plain program's by a relative error of at most 0.0003.
Values sent between devices are 32-bit elements; how exact they have to be, the bound alone decides.
No kernel may reach another device: no remote copies, remote signals or barrier semaphores. Data moves between devices by JAX's collectives and lax.ppermute only.
A program may use at most 64 MiB of HBM per device.

v0:
```python
import math

import jax
import jax.numpy as jnp
from jax import lax
from jax.sharding import PartitionSpec as P

K = 4096
ROOT = 64
WIN = 512
DEC = 4
BANDS = 8
HOP = 256
BINS = 256


def filter_matrix(fir_taps, out_block):
    tap_count = fir_taps.shape[0]
    span_len = tap_count + DEC * out_block
    period = span_len + DEC
    reversed_taps = fir_taps[::-1]
    lead_zero = jnp.zeros((1,), fir_taps.dtype)
    trail_zeros = jnp.zeros((period - tap_count - 1,), fir_taps.dtype)
    pattern = jnp.concatenate([lead_zero, reversed_taps, trail_zeros])
    repeated = jnp.tile(pattern, out_block)[: out_block * span_len]
    return repeated.reshape(out_block, span_len).T


def decimate(raw_strain, fir_taps):
    out_block = 128
    channels = raw_strain.shape[0]
    raw_len = raw_strain.shape[1]
    tap_count = fir_taps.shape[0]
    block_count = raw_len // (DEC * out_block)
    frames = raw_strain.reshape(channels, block_count, DEC * out_block)
    tail_rows = frames[:, :, DEC * out_block - tap_count :]
    tail_rows = jnp.concatenate([jnp.zeros_like(tail_rows[:, :1]), tail_rows[:, :-1]], axis=1)
    span_rows = jnp.concatenate([tail_rows, frames], axis=2)
    matrix = filter_matrix(fir_taps, out_block)
    result = jnp.einsum("cbs,so->cbo", span_rows, matrix, preferred_element_type=jnp.float32)
    return result.reshape(channels, block_count * out_block)


def time_tables():
    sample = lax.broadcasted_iota(jnp.int32, (WIN, BINS), 0)
    freq_index = lax.broadcasted_iota(jnp.int32, (WIN, BINS), 1)
    phase_angle = 2.0 * math.pi / WIN * (sample * freq_index % WIN).astype(jnp.float32)
    sine_taper = jnp.sin(math.pi * (lax.broadcasted_iota(jnp.float32, (WIN, 1), 0) + 0.5) / WIN)
    forward = jnp.concatenate([jnp.cos(phase_angle), -jnp.sin(phase_angle)], axis=1) * sine_taper
    weights = jnp.where(freq_index[:1] == 0, 1.0, 2.0) / WIN
    inverse = (
        jnp.concatenate([jnp.cos(phase_angle) * weights, -jnp.sin(phase_angle) * weights], axis=1)
        * sine_taper
    )
    return (forward, inverse.T)


def root_table(root_size, direction):
    row_index = lax.broadcasted_iota(jnp.int32, (root_size, root_size), 0)
    col_index = lax.broadcasted_iota(jnp.int32, (root_size, root_size), 1)
    phase_angle = (
        direction
        * 2.0
        * math.pi
        / root_size
        * (row_index * col_index % root_size).astype(jnp.float32)
    )
    cosine = jnp.cos(phase_angle)
    sine_part = jnp.sin(phase_angle)
    return jnp.stack(
        [jnp.stack([cosine, -sine_part], axis=-1), jnp.stack([sine_part, cosine], axis=-1)], axis=0
    )


def four_step(values, direction):
    root_size = values.shape[0]
    whole = root_size * root_size
    dft_table = root_table(root_size, direction)
    row_index = lax.broadcasted_iota(jnp.int32, (root_size, root_size), 0)
    col_index = lax.broadcasted_iota(jnp.int32, (root_size, root_size), 1)
    phase_angle = (
        direction * 2.0 * math.pi / whole * (row_index * col_index % whole).astype(jnp.float32)
    )
    turn_cos = jnp.cos(phase_angle)[:, :, None]
    turn_sin = jnp.sin(phase_angle)[:, :, None]
    section_one = jnp.einsum("rcas,absf->cbrf", dft_table, values, precision=lax.Precision.HIGHEST)
    real_part = section_one[:, :, 0] * turn_cos - section_one[:, :, 1] * turn_sin
    imag_part = section_one[:, :, 0] * turn_sin + section_one[:, :, 1] * turn_cos
    turned = jnp.stack([real_part, imag_part], axis=2)
    return jnp.einsum("rdbs,cbsf->dcrf", dft_table, turned, precision=lax.Precision.HIGHEST)


def margin_add(window_out):
    channels = window_out.shape[0]
    window_count = window_out.shape[1]
    lower_half = jnp.pad(window_out[:, :, :HOP], ((0, 0), (0, 1), (0, 0)))
    upper_half = jnp.pad(window_out[:, :, HOP:], ((0, 0), (1, 0), (0, 0)))
    return (lower_half + upper_half).reshape(channels, (window_count + 1) * HOP)


def local_frames(decimated, rim_width):
    local_ch = decimated.shape[0]
    total_len = decimated.shape[1]
    padded = jnp.pad(decimated, ((0, 0), (rim_width, rim_width)))
    pieces = padded.reshape(local_ch, total_len // HOP + 1, HOP)
    return jnp.concatenate([pieces[:, :-1], pieces[:, 1:]], axis=2)


def body(raw_strain, fir_taps, fan_band, band_gain):
    chan_count = lax.axis_size("chan")
    tile_count = lax.axis_size("tile")
    rim_width = HOP // 2
    decimated = decimate(raw_strain, fir_taps)
    local_ch = decimated.shape[0]
    total_len = decimated.shape[1]
    half_bins = BINS // tile_count
    forward, inverse = time_tables()
    frames = local_frames(decimated, rim_width)
    frames = lax.all_to_all(frames, "chan", split_axis=1, concat_axis=0, tiled=True)
    spectra = jnp.einsum("cws,sq->cwq", frames, forward, precision=lax.Precision.HIGHEST)
    spectra = spectra.reshape(frames.shape[0], frames.shape[1], 2, tile_count, half_bins)
    group_ch = spectra.shape[0]
    window_count = spectra.shape[1]
    received = lax.all_to_all(spectra, "tile", split_axis=3, concat_axis=0, tiled=True)
    ordered = received.reshape(tile_count, chan_count, local_ch, window_count, 2, half_bins)
    ordered = jnp.transpose(ordered, (1, 0, 2, 4, 3, 5)).reshape(
        ROOT, ROOT, 2, window_count * half_bins
    )
    spectrum = four_step(ordered, -1.0)
    bin_gains = jnp.zeros(fan_band.shape, jnp.float32)
    for band_index in range(BANDS):
        bin_gains = bin_gains + jnp.where(fan_band == band_index, band_gain[band_index], 0.0)
    shaped = spectrum.reshape(K, 2, window_count, half_bins) * bin_gains[:, None, None, :]
    restored = four_step(shaped.reshape(ROOT, ROOT, 2, window_count * half_bins), 1.0) * (1.0 / K)
    restored = restored.reshape(chan_count, tile_count, local_ch, 2, window_count, half_bins)
    restored = jnp.transpose(restored, (1, 0, 2, 4, 3, 5)).reshape(
        tile_count * group_ch, window_count, 2, 1, half_bins
    )
    returned = lax.all_to_all(restored, "tile", split_axis=0, concat_axis=3, tiled=True)
    returned = returned.reshape(group_ch, window_count, 2 * BINS)
    window_out = jnp.einsum("cwq,qs->cws", returned, inverse, precision=lax.Precision.HIGHEST)
    merged = lax.all_to_all(window_out, "chan", split_axis=0, concat_axis=1, tiled=True)
    summed = margin_add(merged)
    filtered = summed[:, rim_width : rim_width + total_len]
    return filtered


def solution(mesh):
    return jax.shard_map(
        body,
        mesh=mesh,
        in_specs=(P(("chan", "tile"), None), P(), P(None, "tile"), P()),
        out_specs=P(("chan", "tile"), None),
        check_vma=False,
    )
```

profile of v0, /device:TPU:1, one launch (start us, length us, event | category | flops | bytes accessed | tf_op | source)
XLA Modules:
  0.0 435.2 jit_solution(18079353609252254075)
XLA Ops:
  1.4 3.6 copy.59
  12.3 4.4 %copy.30 = f32[16,128,512]{2,0,1:T(8,128)} copy(f32[16,128,512]{2,1,0:T(8,128)S(1)} %pad_maximum_fusion) | data formatting | bytes 8388608 | tf_op jit(solution)/shard_map/concatenate | solution.py:106
  16.7 17.3 %all-to-all-start = ((f32[16,128,512]{2,0,1:T(8,128)}), f32[16,128,512]{2,0,1:T(8,128)}, u32[]{:S(2)}, u32[]{:S(2)}) async-start(f32[16,128,512]{2,0,1:T(8,128)} %copy.30), calls=%async_computation | async-start | bytes 8388608 | tf_op jit(solution)/shard_map/all_to_all | solution.py:119
  36.3 94.2 %all-to-all-done = f32[16,128,512]{2,0,1:T(8,128)} async-done(((f32[16,128,512]{2,0,1:T(8,128)}), f32[16,128,512]{2,0,1:T(8,128)}, u32[]{:S(2)}, u32[]{:S(2)}) %all-to-all-start) | async-done | bytes 4194336 | tf_op jit(solution)/shard_map/all_to_all | solution.py:119
  130.5 8.6 %convolution_bitcast_fusion.1 = f32[2048,1,2,2,128]{4,0,3,2,1:T(8,128)S(1)} fusion(f32[2048,512,1,1]{1,0,3,2:T(8,128)} %bitcast.4, f32[2,2,128,512]{3,2,1,0:T(8,128)S(1)} %bitcast.129), kind=kOutput, calls=%fused_computation.23 | convolution fusion | flops 6442450944 | bytes 9437184 | tf_op jit(solution)/shard_map/cws,sq->cwq/dot_general | solution.py:120
  139.0 2.3 copy.31
  141.3 6.3 %all-to-all-start.1 = ((f32[2048,1,2,2,128]{4,0,2,1,3:T(8,128)}), f32[2048,1,2,2,128]{4,0,2,1,3:T(8,128)}, u32[]{:S(2)}, u32[]{:S(2)}) async-start(f32[2048,1,2,2,128]{4,0,2,1,3:T(8,128)} %copy.31), calls=%async_computation.1 | async-start | bytes 8388608 | tf_op jit(solution)/shard_map/all_to_all | solution.py:124
  148.3 6.6 %select_add_fusion = f32[4096,128]{1,0:T(8,128)S(1)} fusion(s32[4096,128]{1,0:T(8,128)S(1)} %copy-done, f32[]{:T(128)} %bitcast.32, f32[]{:T(128)} %bitcast.31, f32[]{:T(128)} %bitcast.30, f32[]{:T(128)} %bitcast.29, f32[]{:T(128)} %bitcast.28, f32[]{:T(128)} %bitcast.27, f32[]{:T(128)} %bitcast.26, f32[]{:T(128)} %bitcast.25), kind=kLoop, calls=%fused_computation.32 | loop fusion | flops 12058624 | bytes 4194336 | tf_op jit(solution)/shard_map/add | solution.py:132
  157.0 36.5 %all-to-all-done.1 = f32[2048,1,2,2,128]{4,0,2,1,3:T(8,128)} async-done(((f32[2048,1,2,2,128]{4,0,2,1,3:T(8,128)}), f32[2048,1,2,2,128]{4,0,2,1,3:T(8,128)}, u32[]{:S(2)}, u32[]{:S(2)}) %all-to-all-start.1) | async-done | bytes 4194336 | tf_op jit(solution)/shard_map/all_to_all | solution.py:124
  193.5 2.8 copy.32
  196.3 6.5 %fusion.17 = f32[64,64,2,128]{3,0,2,1:T(8,128)S(1)} fusion(f32[64,64,2,128,1]{3,1,0,2,4:T(8,128)S(1)} %bitcast.118, f32[1,64,64,2]{2,1,3,0:T(8,128)S(1)} %get-tuple-element.16, f32[1,64,64,2]{2,1,3,0:T(8,128)S(1)} %get-tuple-element.15), kind=kOutput, calls=%fused_computation.26 | convolution fusion | flops 1610629120 | bytes 8454144 | tf_op jit(solution)/shard_map/rcas,absf->cbrf/dot_general | solution.py:86
  205.0 6.3 %fusion.12 = f32[64,128,2,64,1]{1,3,4,2,0:T(8,128)S(1)} fusion(f32[64,64,2,128,1]{3,0,2,1,4:T(8,128)S(1)} %maximum_bitcast_fusion, f32[1,64,64,2]{2,1,3,0:T(8,128)S(1)} %get-tuple-element.16, f32[1,64,64,2]{2,1,3,0:T(8,128)S(1)} %get-tuple-element.15), kind=kOutput, calls=%fused_computation.17 | convolution fusion | flops 1610629120 | bytes 8454144 | tf_op jit(solution)/shard_map/rdbs,cbsf->dcrf/dot_general | solution.py:90
  211.3 4.3 fusion.20
  217.9 6.3 %fusion.9 = f32[64,64,2,128]{3,0,2,1:T(8,128)S(1)} fusion(f32[64,64,2,128,1]{3,0,2,1,4:T(8,128)S(1)} %maximum_bitcast_fusion.1, f32[1,64,64,2]{2,1,3,0:T(8,128)S(1)} %get-tuple-element.14, f32[1,64,64,2]{2,1,3,0:T(8,128)S(1)} %get-tuple-element.13), kind=kOutput, calls=%fused_computation.14 | convolution fusion | flops 1611677696 | bytes 8454144 | tf_op jit(solution)/shard_map/rdbs,cbsf->dcrf/dot_general | solution.py:90
  224.2 2.4 copy.37
  227.0 16.6 %copy.39 = f32[4096,1,2,1,128]{4,2,3,1,0:T(2,128)} copy(f32[4096,1,2,1,128]{4,0,2,3,1:T(8,128)S(1)} %bitcast.120) | data formatting | bytes 8388608 | tf_op jit(solution)/shard_map/reshape | solution.py:136
  243.6 5.6 %all-to-all-start.2 = ((f32[4096,1,2,1,128]{4,2,3,1,0:T(2,128)}), f32[4096,1,2,1,128]{4,2,3,1,0:T(2,128)}, u32[]{:S(2)}, u32[]{:S(2)}) async-start(f32[4096,1,2,1,128]{4,2,3,1,0:T(2,128)} %copy.39), calls=%async_computation.2 | async-start | bytes 8388608 | tf_op jit(solution)/shard_map/all_to_all | solution.py:139
  251.4 42.9 %all-to-all-done.2 = f32[4096,1,2,1,128]{4,2,3,1,0:T(2,128)} async-done(((f32[4096,1,2,1,128]{4,2,3,1,0:T(2,128)}), f32[4096,1,2,1,128]{4,2,3,1,0:T(2,128)}, u32[]{:S(2)}, u32[]{:S(2)}) %all-to-all-start.2) | async-done | bytes 4194336 | tf_op jit(solution)/shard_map/all_to_all | solution.py:139
  294.3 4.4 %copy.40 = f32[4096,1,2,1,128]{4,0,2,3,1:T(8,128)} copy(f32[4096,1,2,1,128]{4,2,3,1,0:T(2,128)} %all-to-all-done.2) | data formatting | bytes 8388608 | tf_op jit(solution)/shard_map/all_to_all | solution.py:139
  298.7 5.4 %copy.41 = f32[2048,1,2,2,1,128]{0,5,3,2,4,1:T(8,128)} copy(f32[2048,1,2,2,1,128]{5,0,3,2,4,1:T(8,128)} %bitcast.121) | data formatting | bytes 8388608 | tf_op jit(solution)/shard_map/all_to_all | solution.py:139
  304.1 8.5 %convolution_bitcast_fusion = f32[2048,1,512]{2,0,1:T(8,128)S(1)} fusion(f32[2048,512]{0,1:T(8,128)} %bitcast.116, f32[512,256]{0,1:T(8,128)S(1)} %get-tuple-element.18, f32[512,256]{0,1:T(8,128)S(1)} %get-tuple-element.17, f32[512]{0:T(512)S(1)} %multiply_sine_fusion.4), kind=kOutput, calls=%fused_computation.22 | convolution fusion | flops 6442975232 | bytes 9439232 | tf_op jit(solution)/shard_map/cwq,qs->cws/dot_general | solution.py:141
  312.7 8.0 %copy.42 = f32[2048,1,512]{2,1,0:T(1,128)S(1)} copy(f32[2048,1,512]{2,0,1:T(8,128)S(1)} %convolution_bitcast_fusion) | data formatting | bytes 8388608 | tf_op jit(solution)/shard_map/cwq,qs->cws/dot_general | solution.py:141
  320.7 109.0 %all_to_all.63 = f32[2048,1,512]{2,1,0:T(1,128)S(1)} all-to-all(f32[2048,1,512]{2,1,0:T(1,128)S(1)} %copy.42), channel_id=1, replica_groups=mesh['chan'=128,'tile'=2] {'chan'}, dimensions={0} | all-to-all | bytes 8388608 | tf_op jit(solution)/shard_map/all_to_all | solution.py:142
  429.7 2.4 copy.74
  (42 shorter events, 23.5 us)
Async XLA Ops:
  16.7 113.8 %all-to-all-start = ((f32[16,128,512]{2,0,1:T(8,128)}), f32[16,128,512]{2,0,1:T(8,128)}, u32[]{:S(2)}, u32[]{:S(2)}) async-start(f32[16,128,512]{2,0,1:T(8,128)} %copy.30), calls=%async_computation | async-start | bytes 8388608 | tf_op jit(solution)/shard_map/all_to_all | solution.py:119
  141.3 6.3 %copy-start.1 = (f32[8]{0:T(128)S(1)}, f32[8]{0:T(128)}, u32[]{:S(2)}) copy-start(f32[8]{0:T(128)} %param.7) | copy-start | bytes 100
  141.3 7.0 %copy-start = (s32[4096,128]{1,0:T(8,128)S(1)}, s32[4096,128]{1,0:T(8,128)}, u32[]{:S(2)}) copy-start(s32[4096,128]{1,0:T(8,128)} %param.6) | copy-start | bytes 6291460
  141.3 52.2 %all-to-all-start.1 = ((f32[2048,1,2,2,128]{4,0,2,1,3:T(8,128)}), f32[2048,1,2,2,128]{4,0,2,1,3:T(8,128)}, u32[]{:S(2)}, u32[]{:S(2)}) async-start(f32[2048,1,2,2,128]{4,0,2,1,3:T(8,128)} %copy.31), calls=%async_computation.1 | async-start | bytes 8388608 | tf_op jit(solution)/shard_map/all_to_all | solution.py:124
  243.6 50.6 %all-to-all-start.2 = ((f32[4096,1,2,1,128]{4,2,3,1,0:T(2,128)}), f32[4096,1,2,1,128]{4,2,3,1,0:T(2,128)}, u32[]{:S(2)}, u32[]{:S(2)}) async-start(f32[4096,1,2,1,128]{4,2,3,1,0:T(2,128)} %copy.39), calls=%async_computation.2 | async-start | bytes 8388608 | tf_op jit(solution)/shard_map/all_to_all | solution.py:139
where the time goes:
time: 443 us; the launch traced here: 435 us
  waiting for transfers between devices  174 us (39%)
  blocking collectives  109 us (25%)
  local copies, waits for them, and re-layouts  63.7 us (14%)
  matrix products  42.2 us (10%)
  starting transfers between devices  29.2 us (7%)
  other arithmetic  17.1 us (4%)
    all_to_all x1, blocking collectives, body(): lax.all_to_all(window_out, 'chan', split_axis=0, concat_axis=1, tiled=True)  109 us
    all_to_all x1, waiting for transfers between devices, body(): lax.all_to_all(frames, 'chan', split_axis=1, concat_axis=0, tiled=True)  94.2 us
    all_to_all x1, waiting for transfers between devices, body(): lax.all_to_all(restored, 'tile', split_axis=0, concat_axis=3, tiled=True)  42.9 us
    all_to_all x1, waiting for transfers between devices, body(): lax.all_to_all(spectra, 'tile', split_axis=3, concat_axis=0, tiled=True)  36.5 us
    all_to_all x1, starting transfers between devices, body(): lax.all_to_all(frames, 'chan', split_axis=1, concat_axis=0, tiled=True)  17.3 us
    reshape x1, local copies, waits for them, and re-layouts, body(): jnp.transpose(restored, (1, 0, 2, 4, 3, 5))  16.6 us
    dot_general x2, matrix products, four_step(): jnp.einsum('rdbs,cbsf->dcrf', dft_table, turned, precision=lax.Precision....  12.6 us
    dot_general x2, matrix products, four_step(): jnp.einsum('rcas,absf->cbrf', dft_table, values, precision=lax.Precision....  10.9 us
  transfers between devices with their start and end apart: 3, of which 3 were waited for; matrix products, arithmetic and copies ran while one was open for 3% of the time, Pallas kernels for 0%

commit v1 on v0

v1 whole, which is shorter than its diff:
```python
import math

import jax
import jax.numpy as jnp
import numpy as np
from jax import lax
from jax.experimental import pallas as pl
from jax.experimental.pallas import tpu as pltpu
from jax.sharding import PartitionSpec as P
import ml_dtypes

K = 4096
ROOT = 64
WIN = 512
TAPS = 128
DEC = 4
BANDS = 8
HOP = 256
BINS = 256
BLK = 128
SLOTS = 32
HALF = 16
AXES = ("chan", "tile")
F32 = jnp.float32
BF16 = jnp.bfloat16
BIG = 60 * 1024 * 1024


def two(table):
    table = np.asarray(table, np.float32)
    hi = table.astype(ml_dtypes.bfloat16)
    lo = (table - hi.astype(np.float32)).astype(ml_dtypes.bfloat16)
    return hi, lo


def left_operand(table):
    hi, lo = two(table)
    return np.concatenate([hi, hi, lo], axis=-1)


def own_first(table, axis):
    other = np.roll(table, -HALF, axis=axis)
    return np.stack([table, other], axis=0)


def spatial_tables():
    c1 = np.arange(ROOT)
    slot = np.arange(SLOTS)[:, None]
    angle = 2 * np.pi / ROOT * (slot * c1 % ROOT)
    re, im = np.cos(angle), np.sin(angle)
    im[0] = -((-1.0) ** c1)
    first = np.stack([re, -im], axis=0)
    first = own_first(first, 1).reshape(2, ROOT, ROOT)
    c0 = np.arange(ROOT)[None, :]
    k2 = np.arange(ROOT)[:, None]
    second = np.zeros((SLOTS, 2, ROOT, 2, ROOT))
    inverse = np.zeros((SLOTS, 2, ROOT, 2, ROOT))
    for s in range(SLOTS):
        phase = 2 * np.pi / K * ((s + ROOT * k2) * c0 % K)
        co, si = np.cos(phase), np.sin(phase)
        if s:
            second[s, 0, :, 0], second[s, 0, :, 1] = co, si
            second[s, 1, :, 0], second[s, 1, :, 1] = -si, co
            inverse[s, 0, :, 0], inverse[s, 0, :, 1] = co.T, -si.T
            inverse[s, 1, :, 0], inverse[s, 1, :, 1] = si.T, co.T
            continue
        n = ROOT // 2
        second[0, 0, :n, 0], second[0, 1, :n, 0] = co[:n], -si[:n]
        second[0, 1, 0, 0] = (-1.0) ** c0[0]
        inverse[0, 0, :, 0, :n], inverse[0, 0, :, 1, :n] = co[:n].T, -si[:n].T
        inverse[0, 0, :, 0, 0] = 0.5
        inverse[0, 0, :, 1, 0] = 0.5 * (-1.0) ** c0[0]
        phase = 2 * np.pi / K * ((n + ROOT * k2[:n]) * c0 % K)
        co, si = np.cos(phase), np.sin(phase)
        second[0, 0, n:, 1], second[0, 1, n:, 1] = co, -si
        inverse[0, 1, :, 0, n:], inverse[0, 1, :, 1, n:] = co.T, -si.T
    second = second.reshape(SLOTS, BLK, BLK)
    inverse = inverse.reshape(SLOTS, BLK, BLK) / K
    last = np.swapaxes(first, 1, 2)
    return (left_operand(first), left_operand(second), left_operand(inverse), left_operand(last))


def temporal_tables():
    s = np.arange(WIN)[:, None]
    f = np.arange(BINS)[None, :]
    angle = 2 * np.pi / WIN * (s * f % WIN)
    taper = np.sin(np.pi * (s + 0.5) / WIN)
    forward = np.concatenate([np.cos(angle), np.sin(angle)], axis=1) * taper
    weight = np.where(f == 0, 1.0, 2.0) / WIN
    backward = np.concatenate([np.cos(angle) * weight, np.sin(angle) * weight], axis=1) * taper
    return np.stack(two(forward)), np.stack(two(backward.T))


def chip_of(j):
    row, i = divmod(j, 4)
    z, q = divmod(row, 4)
    x = i if row % 2 == 0 else 3 - i
    y = q if z % 2 == 0 else 3 - q
    return x, y, z


def device_of(j, core):
    x, y, z = chip_of(j)
    return (((x // 2 * 4 + y) * 8 + z) * 2 + core) * 2 + x % 2


def permutes(windows):
    partner = [(device_of(j, c), device_of(j, 1 - c)) for j in range(windows) for c in (0, 1)]
    same, cross = [], []
    for j in range(windows - 1):
        same.append((device_of(j + 1, 0), device_of(j, 0)))
        same.append((device_of(j, 1), device_of(j + 1, 1)))
        cross.append((device_of(j + 1, 0), device_of(j, 1)))
        cross.append((device_of(j, 1), device_of(j + 1, 0)))
    return partner, same, cross


def flipped(pairs):
    return [(b, a) for a, b in pairs]


def split(value):
    hi = value.astype(BF16)
    return hi, (value - hi.astype(F32)).astype(BF16)


def stacked(value):
    hi, lo = split(value)
    return jnp.concatenate([hi, lo, hi], axis=0)


def dot(a, b):
    return jnp.dot(a, b, preferred_element_type=F32)


def plane_slot(b):
    j, core = divmod(b, 2)
    row, i = divmod(j, 4)
    x = i if row % 2 == 0 else 3 - i
    return x // 2, row, core, x % 2


def decimate_kernel(taps_ref, tail_ref, cur_ref, out_ref, band_ref):
    plane = pl.program_id(0)
    span = TAPS + DEC * BLK

    @pl.when(plane == 0)
    def _():
        i = lax.broadcasted_iota(jnp.int32, (TAPS, TAPS), 0)
        j = lax.broadcasted_iota(jnp.int32, (TAPS, TAPS), 1)
        mirror = (i + j == TAPS - 1).astype(BF16)
        mirrored = dot(taps_ref[...], mirror)
        rows = jnp.broadcast_to(mirrored[:1], (BLK, TAPS))
        wide = jnp.concatenate([rows, jnp.zeros((BLK, span - TAPS), F32)], axis=1)
        band_ref[...] = pltpu.roll(wide, 1, 1, stride=DEC, stride_axis=0).astype(BF16)

    tail = jnp.where(plane == 0, jnp.zeros_like(tail_ref[...]), tail_ref[...])
    blocks = cur_ref.shape[1] // (DEC * BLK)
    band = band_ref[...]
    group = 8
    for b0 in range(0, blocks, group):
        spans = []
        for b in range(b0, b0 + group):
            start = b * DEC * BLK
            if b == 0:
                spans.append(jnp.concatenate([tail, cur_ref[:, : DEC * BLK]], axis=1))
            else:
                spans.append(cur_ref[:, start - TAPS : start + DEC * BLK])
        result = lax.dot_general(
            jnp.concatenate(spans, axis=0), band, (((1,), (1,)), ((), ())), preferred_element_type=F32
        )
        for n in range(group):
            xh, row, core, xl = plane_slot(b0 + n)
            y = jnp.where(plane % 2 == 0, row, 3 - row)
            out_ref[xh, y, 0, core, xl] = result[n * 16 : (n + 1) * 16]


def decimate(raw, taps):
    channels, length = raw.shape
    planes = 8
    width = length // planes
    taps = jnp.broadcast_to(taps[None, :], (16, TAPS))
    return pl.pallas_call(
        decimate_kernel,
        grid=(planes,),
        in_specs=[
            pl.BlockSpec((16, TAPS), lambda g: (0, 0)),
            pl.BlockSpec((channels, TAPS), lambda g: (0, jnp.maximum(g * (width // TAPS) - 1, 0))),
            pl.BlockSpec((channels, width), lambda g: (0, g)),
        ],
        out_specs=pl.BlockSpec((2, 4, 1, 2, 2, channels, BLK), lambda g: (0, 0, g, 0, 0, 0, 0)),
        out_shape=jax.ShapeDtypeStruct((2, 4, planes, 2, 2, channels, BLK), F32),
        scratch_shapes=[pltpu.VMEM((BLK, TAPS + DEC * BLK), BF16)],
        compiler_params=pltpu.CompilerParams(vmem_limit_bytes=BIG),
        name="decimate",
    )(taps, raw, raw)


def unplane_kernel(in_ref, out_ref):
    plane = pl.program_id(0)
    for b in range(32):
        xh, row, core, xl = plane_slot(b)
        y = jnp.where(plane % 2 == 0, row, 3 - row)
        out_ref[:, b * BLK : (b + 1) * BLK] = in_ref[xh, y, 0, core, xl]


def unplane(blocks):
    planes = blocks.shape[2]
    channels = blocks.shape[5]
    return pl.pallas_call(
        unplane_kernel,
        grid=(planes,),
        in_specs=[pl.BlockSpec((2, 4, 1, 2, 2, channels, BLK), lambda g: (0, 0, g, 0, 0, 0, 0))],
        out_specs=pl.BlockSpec((channels, 32 * BLK), lambda g: (0, g)),
        out_shape=jax.ShapeDtypeStruct((channels, planes * 32 * BLK), F32),
        compiler_params=pltpu.CompilerParams(vmem_limit_bytes=BIG),
        name="unplane",
    )(blocks)


def forward_kernel(where_ref, x_ref, first_ref, second_ref, out_ref, mid_ref):
    core = where_ref[0]
    first = first_ref[core]
    for c0 in range(0, ROOT, 2):
        one = stacked(x_ref[pl.ds(c0, ROOT, stride=ROOT), :])
        two_ = stacked(x_ref[pl.ds(c0 + 1, ROOT, stride=ROOT), :])
        y = dot(first, jnp.concatenate([one, two_], axis=1))
        mid_ref[c0 * ROOT : (c0 + 1) * ROOT, :] = y[:, :BLK]
        mid_ref[(c0 + 1) * ROOT : (c0 + 2) * ROOT, :] = y[:, BLK:]
    for s in range(SLOTS):
        re = mid_ref[pl.ds(s, ROOT, stride=ROOT), :]
        im = mid_ref[pl.ds(SLOTS + s, ROOT, stride=ROOT), :]
        table = second_ref[lax.rem(s + HALF * core, SLOTS)]
        out_ref[s] = dot(table, stacked(jnp.concatenate([re, im], axis=0)))


def forward_space(where, x, first, second):
    return pl.pallas_call(
        forward_kernel,
        in_specs=[pl.BlockSpec(memory_space=pltpu.SMEM)] + [pl.BlockSpec(memory_space=pltpu.VMEM)] * 3,
        out_specs=pl.BlockSpec(memory_space=pltpu.VMEM),
        out_shape=jax.ShapeDtypeStruct((SLOTS, BLK, BLK), F32),
        scratch_shapes=[pltpu.VMEM((K, BLK), F32)],
        compiler_params=pltpu.CompilerParams(vmem_limit_bytes=BIG),
        name="forward_space",
    )(where, x, first, second)


def inverse_kernel(where_ref, own_ref, halo_ref, part_ref, cross_ref, inv_ref, last_ref, out_ref, mid_ref):
    core = where_ref[0]
    for s in range(SLOTS):
        if s < HALF:
            z = own_ref[s] + halo_ref[s]
        else:
            z = part_ref[s - HALF] + cross_ref[s - HALF]
        table = inv_ref[lax.rem(s + HALF * core, SLOTS)]
        u = dot(table, stacked(z))
        mid_ref[pl.ds(s, ROOT, stride=ROOT), :] = u[:ROOT]
        mid_ref[pl.ds(SLOTS + s, ROOT, stride=ROOT), :] = u[ROOT:]
    last = last_ref[core]
    for c0 in range(0, ROOT, 2):
        one = stacked(mid_ref[c0 * ROOT : (c0 + 1) * ROOT, :])
        two_ = stacked(mid_ref[(c0 + 1) * ROOT : (c0 + 2) * ROOT, :])
        y = dot(last, jnp.concatenate([one, two_], axis=1))
        out_ref[pl.ds(c0, ROOT, stride=ROOT), :] = y[:, :BLK]
        out_ref[pl.ds(c0 + 1, ROOT, stride=ROOT), :] = y[:, BLK:]


def inverse_space(where, own, halo, part, cross, inv, last):
    return pl.pallas_call(
        inverse_kernel,
        in_specs=[pl.BlockSpec(memory_space=pltpu.SMEM)] + [pl.BlockSpec(memory_space=pltpu.VMEM)] * 6,
        out_specs=pl.BlockSpec(memory_space=pltpu.VMEM),
        out_shape=jax.ShapeDtypeStruct((K, BLK), F32),
        scratch_shapes=[pltpu.VMEM((K, BLK), F32)],
        compiler_params=pltpu.CompilerParams(vmem_limit_bytes=BIG),
        name="inverse_space",
    )(where, own, halo, part, cross, inv, last)


def gains_kernel(where_ref, gain_ref, band_ref, out_ref):
    core = where_ref[0]
    n = ROOT // 2
    i = lax.broadcasted_iota(jnp.int32, (ROOT, ROOT), 0)
    j = lax.broadcasted_iota(jnp.int32, (ROOT, ROOT), 1)
    mirror = (i + j == ROOT - 1).astype(BF16)
    source = jnp.where(i == 0, 0, jnp.where(i < n, n - i, n + ROOT - 1 - i))
    mirror0 = (j == source).astype(BF16)

    def rows(k1, k2, count):
        return band_ref[pl.ds(k1 + ROOT * k2, count, stride=ROOT), :]

    def exact(perm, bands):
        return dot(perm, bands.astype(F32).astype(BF16))

    def pick(bands):
        total = jnp.zeros(bands.shape, F32)
        for b in range(BANDS):
            total = jnp.where(bands == b, gain_ref[b], total)
        return total

    def put(s, plus, minus):
        gp, gm = pick(plus.astype(F32)), pick(minus)
        out_ref[0, s] = gp + gm
        out_ref[1, s] = gp - gm

    for s in range(HALF):
        if s:
            k1 = s + HALF * core
            put(s, rows(k1, 0, ROOT), exact(mirror, rows(ROOT - k1, 0, ROOT)))
            continue

        @pl.when(core == 0)
        def _():
            plus = jnp.concatenate([rows(0, 0, n), rows(n, 0, n)], axis=0)
            minus = jnp.concatenate([rows(0, n, n), rows(n, n, n)], axis=0)
            put(0, plus, exact(mirror0, minus))

        @pl.when(core != 0)
        def _():
            put(0, rows(HALF, 0, ROOT), exact(mirror, rows(ROOT - HALF, 0, ROOT)))


def gains(where, band_gain, fan_band):
    return pl.pallas_call(
        gains_kernel,
        in_specs=[pl.BlockSpec(memory_space=pltpu.SMEM)] * 2 + [pl.BlockSpec(memory_space=pltpu.VMEM)],
        out_specs=pl.BlockSpec(memory_space=pltpu.VMEM),
        out_shape=jax.ShapeDtypeStruct((2, HALF, ROOT, BLK), F32),
        compiler_params=pltpu.CompilerParams(vmem_limit_bytes=BIG),
        name="gains",
    )(where, band_gain, fan_band)


def time_kernel(where_ref, own_ref, part_ref, same_ref, cross_ref, mine_ref, theirs_ref, fwd_ref, bwd_ref, out_ref):
    core, xl = where_ref[0], where_ref[1]
    step = pl.program_id(0)
    slots = own_ref.shape[0]
    rows = slots * BLK
    even = core == 0

    def flat(ref):
        return ref[...].reshape(rows, BLK)

    own, part, same, cross = flat(own_ref), flat(part_ref), flat(same_ref), flat(cross_ref)
    x = jnp.concatenate(
        [
            jnp.where(even, cross, same),
            jnp.where(even, own, part),
            jnp.where(even, part, own),
            jnp.where(even, same, cross),
        ],
        axis=1,
    )
    hi, lo = split(x)
    fwd_hi = fwd_ref[0]
    v = dot(hi, fwd_hi) + dot(lo, fwd_hi) + dot(hi, fwd_ref[1])
    pieces = []
    for s in range(slots):
        p = v[s * BLK : s * BLK + ROOT]
        q = v[s * BLK + ROOT : (s + 1) * BLK]
        a, d = p[:, :BINS], p[:, BINS:]
        c, b = q[:, :BINS], q[:, BINS:]

        def wide(kind):
            mine, theirs = mine_ref[kind, s], theirs_ref[kind, s]
            low = jnp.where(xl == 0, mine, theirs)
            high = jnp.where(xl == 0, theirs, mine)
            return jnp.concatenate([low, high], axis=1)

        gs, gd = wide(0), wide(1)
        gr = gi = gs
        if s == 0:
            row = lax.broadcasted_iota(jnp.int32, (ROOT, BINS), 0)
            pair = (row == 0) & (step == 0) & even
            gr = jnp.where(pair, gs + gd, gs)
            gi = jnp.where(pair, gs - gd, gs)
            gd = jnp.where(pair, 0.0, gd)
        pieces.append(jnp.concatenate([gr * a + gd * b, gr * d - gd * c], axis=1))
        pieces.append(jnp.concatenate([gi * c - gd * d, gd * a + gi * b], axis=1))
    hi, lo = split(jnp.concatenate(pieces, axis=0))
    bwd_hi = bwd_ref[0]
    z = dot(hi, bwd_hi) + dot(lo, bwd_hi) + dot(hi, bwd_ref[1])
    places = [
        jnp.where(even, 3, 2),
        jnp.where(even, 0, 1),
        jnp.where(even, 1, 0),
        jnp.where(even, 2, 3),
    ]
    for n in range(4):
        out_ref[places[n]] = z[:, n * BLK : (n + 1) * BLK].reshape(slots, BLK, BLK)


def time_filter(where, own, part, same, cross, mine, theirs, fwd, bwd):
    total = own.shape[0]
    slots = 4
    data = pl.BlockSpec((slots, BLK, BLK), lambda g: (g, 0, 0))
    gain = pl.BlockSpec((2, slots, ROOT, BLK), lambda g: (0, g, 0, 0))
    table = pl.BlockSpec((2, WIN, WIN), lambda g: (0, 0, 0))
    return pl.pallas_call(
        time_kernel,
        grid=(total // slots,),
        in_specs=[pl.BlockSpec(memory_space=pltpu.SMEM)] + [data] * 4 + [gain] * 2 + [table] * 2,
        out_specs=pl.BlockSpec((4, slots, BLK, BLK), lambda g: (0, g, 0, 0)),
        out_shape=jax.ShapeDtypeStruct((4, total, BLK, BLK), F32),
        compiler_params=pltpu.CompilerParams(vmem_limit_bytes=BIG),
        name="time_filter",
    )(where, own, part, same, cross, mine, theirs, fwd, bwd)


def body(raw_strain, fir_taps, fan_band, band_gain):
    where = jnp.stack([lax.axis_index("chan") % 2, lax.axis_index("tile")]).astype(jnp.int32)
    first, second, inverse, last = (jnp.asarray(t) for t in spatial_tables())
    fwd, bwd = (jnp.asarray(t) for t in temporal_tables())
    partner, same, cross = permutes(raw_strain.shape[1] // DEC // HOP)

    mine = gains(where, band_gain, fan_band)
    theirs = lax.ppermute(mine, "tile", [(0, 1), (1, 0)])

    blocks = decimate(raw_strain, fir_taps)
    shape = blocks.shape
    blocks = blocks.reshape((256,) + shape[5:])
    blocks = lax.all_to_all(blocks, AXES, 0, 0, tiled=True)
    waves = forward_space(where, blocks.reshape(K, BLK), first, second)
    own, other = waves[:HALF], waves[HALF:]
    from_partner = lax.ppermute(other, AXES, partner)
    from_same = lax.ppermute(own, AXES, same)
    from_cross = lax.ppermute(other, AXES, cross)
    z = time_filter(where, own, from_partner, from_same, from_cross, mine, theirs, fwd, bwd)
    back_partner = lax.ppermute(z[1], AXES, partner)
    back_same = lax.ppermute(z[2], AXES, flipped(same))
    back_cross = lax.ppermute(z[3], AXES, flipped(cross))
    filtered = inverse_space(where, z[0], back_same, back_partner, back_cross, inverse, last)
    filtered = lax.all_to_all(filtered.reshape(256, 16, BLK), AXES, 0, 0, tiled=True)
    return unplane(filtered.reshape(shape))


def solution(mesh):
    return jax.shard_map(
        body,
        mesh=mesh,
        in_specs=(P(AXES, None), P(), P(None, "tile"), P()),
        out_specs=P(AXES, None),
        check_vma=False,
    )
```

time: 443 us -> 232 us (0.52); the launches traced: 435 us -> 232 us
  waiting for transfers between devices: 174 us -> 87.1 us
  local copies, waits for them, and re-layouts: 63.7 us -> 8.78 us
  blocking collectives: 109 us -> 61 us
  Pallas kernels: 0 us -> 44.6 us
  matrix products: 42.2 us -> 0 us
  other arithmetic: 17.1 us -> 0.55 us
    all_to_all x3 -> x1, waiting for transfers between devices: 174 us -> 45.9 us  [body(): blocks = lax.all_to_all(blocks, AXES, 0, 0, tiled=True)]
    all_to_all x1, blocking collectives: 109 us -> 61 us  [body(): lax.all_to_all(filtered.reshape(256, 16, BLK), AXES, 0, 0, tiled=True)]
    pallas_call x0 -> x6, Pallas kernels: none -> 44.6 us  [the longest x1 11 us: time_filter(): pl.pallas_call(time_kernel, grid=(total // slots,), in_specs=[pl.BlockSpe...]
    dot_general x7 -> x0, matrix products: 42.2 us -> none  [the longest x2 12.6 us: four_step(): jnp.einsum('rdbs,cbsf->dcrf', dft_table, turned, precision=lax.Precision....]
    ppermute x0 -> x7, waiting for transfers between devices: none -> 41.2 us  [the longest x1 18.9 us: body(): back_cross = lax.ppermute(z[3], AXES, flipped(cross))]
    reshape x3 -> x0, local copies, waits for them, and re-layouts: 18.5 us -> none  [the longest x1 16.6 us: body(): jnp.transpose(restored, (1, 0, 2, 4, 3, 5))]
    ppermute x0 -> x7, starting transfers between devices: none -> 13.8 us  [the longest x1 4.09 us: body(): back_cross = lax.ppermute(z[3], AXES, flipped(cross))]
    all_to_all x3 -> x1, starting transfers between devices: 29.2 us -> 15.7 us  [body(): blocks = lax.all_to_all(blocks, AXES, 0, 0, tiled=True)]
  transfers between devices with their start and end apart: 3 -> 8, of which waited for: 3 -> 5; matrix products, arithmetic and copies ran while one was open for 3% -> 1% of each run, Pallas kernels for 0% -> 5%
where the time goes in v1:
time: 232 us
  waiting for transfers between devices  87.1 us (38%)
  blocking collectives  61 us (26%)
  Pallas kernels  44.6 us (19%)
  starting transfers between devices  29.4 us (13%)
  local copies, waits for them, and re-layouts  8.78 us (4%)
    all_to_all x1, blocking collectives, body(): lax.all_to_all(filtered.reshape(256, 16, BLK), AXES, 0, 0, tiled=True)  61 us
    all_to_all x1, waiting for transfers between devices, body(): blocks = lax.all_to_all(blocks, AXES, 0, 0, tiled=True)  45.9 us
    ppermute x1, waiting for transfers between devices, body(): back_cross = lax.ppermute(z[3], AXES, flipped(cross))  18.9 us
    all_to_all x1, starting transfers between devices, body(): blocks = lax.all_to_all(blocks, AXES, 0, 0, tiled=True)  15.7 us
    pallas_call x1, Pallas kernels, time_filter(): pl.pallas_call(time_kernel, grid=(total // slots,), in_specs=[pl.BlockSpe...  11 us
    ppermute x1, waiting for transfers between devices, body(): from_same = lax.ppermute(own, AXES, same)  9.71 us
    ppermute x1, waiting for transfers between devices, body(): from_cross = lax.ppermute(other, AXES, cross)  9.35 us
    pallas_call x1, Pallas kernels, inverse_space(): pl.pallas_call(inverse_kernel, in_specs=[pl.BlockSpec(memory_space=pltpu....  8.56 us
  transfers between devices with their start and end apart: 8, of which 5 were waited for; matrix products, arithmetic and copies ran while one was open for 1% of the time, Pallas kernels for 5%

profile of v1, /device:TPU:1, one launch (start us, length us, event | category | flops | bytes accessed | tf_op | source)
XLA Modules:
  0.0 231.6 jit_solution(14170862857099755353)
XLA Ops:
  0.0 1.2 broadcast_in_dim.2.taps_ref
  1.2 7.7 %decimate.1 = f32[2,4,8,2,2,16,128]{6,5,4,3,2,1,0:T(8,128)} custom-call(bf16[16,128]{1,0:T(8,128)(2,1)} %broadcast_in_dim.2.taps_ref, bf16[16,131072]{1,0:T(8,128)(2,1)} %cur_ref.1, bf16[16,131072]{1,0:T(8,128)(2,1)} %cur_ref.1), custom_call_target="tpu_custom_call" | custom-call | tf_op jit(solution)/shard_map/decimate/pallas_call | solution.py:183
  9.0 15.7 %all-to-all-start = ((f32[256,16,128]{2,1,0:T(8,128)}), f32[256,16,128]{2,1,0:T(8,128)S(1)}, u32[]{:S(2)}, u32[]{:S(2)}) async-start(f32[256,16,128]{2,1,0:T(8,128)} %bitcast.14), calls=%async_computation | async-start | bytes 4194304 | tf_op jit(solution)/shard_map/all_to_all | solution.py:423
  24.7 0.6 pad_add_fusion.where_ref
  25.2 4.0 %gains.1.mine_ref = f32[2,16,64,128]{3,2,1,0:T(8,128)} custom-call(s32[2]{0:T(128)} %pad_add_fusion.where_ref, f32[8]{0:T(128)} %gain_ref.1, s32[4096,128]{1,0:T(8,128)} %band_ref.1), custom_call_target="tpu_custom_call" | custom-call | tf_op jit(solution)/shard_map/gains/pallas_call | solution.py:325
  29.2 1.4 collective-permute-start.3
  30.6 45.9 %all-to-all-done = f32[256,16,128]{2,1,0:T(8,128)S(1)} async-done(((f32[256,16,128]{2,1,0:T(8,128)}), f32[256,16,128]{2,1,0:T(8,128)S(1)}, u32[]{:S(2)}, u32[]{:S(2)}) %all-to-all-start) | async-done | bytes 2097184 | tf_op jit(solution)/shard_map/all_to_all | solution.py:423
  76.5 1.3 copy-done
  77.8 7.7 %forward_space.1 = f32[32,128,128]{2,1,0:T(8,128)} custom-call(s32[2]{0:T(128)} %pad_add_fusion.where_ref, f32[4096,128]{1,0:T(8,128)} %bitcast.17, bf16[2,64,192]{2,1,0:T(8,128)(2,1)} %constant.33.clone.first_ref, bf16[32,128,384]{2,1,0:T(8,128)(2,1)} %constant.34.clone.second_ref), custom_call_target="tpu_custom_call" | custom-call | tf_op jit(solution)/shard_map/forward_space/pallas_call | solution.py:238
  85.5 1.7 fusion
  87.2 2.9 %collective-permute-start.2 = (f32[16,128,128]{2,1,0:T(8,128)S(1)}, f32[16,128,128]{2,1,0:T(8,128)S(1)}, u32[]{:S(2)}, u32[]{:S(2)}) collective-permute-start(f32[16,128,128]{2,1,0:T(8,128)S(1)} %get-tuple-element.9), channel_id=1, source_target_pairs={{1,2},{2,1},{128,3},{3,128},{129,130},{130,129},{161,131},{131,161... | collective-permute-start | bytes 3145736 | tf_op jit(solution)/shard_map/ppermute | solution.py:428
  90.2 3.8 %collective-permute-start.1 = (f32[16,128,128]{2,1,0:T(8,128)S(1)}, f32[16,128,128]{2,1,0:T(8,128)}, u32[]{:S(2)}, u32[]{:S(2)}) collective-permute-start(f32[16,128,128]{2,1,0:T(8,128)S(1)} %get-tuple-element.10.own_ref), channel_id=1, source_target_pairs={{1,0},{2,3},{128,1},{3,130},{129,128},{130,131},{161,129},{131,163... | collective-permute-start | bytes 3145736 | tf_op jit(solution)/shard_map/ppermute | solution.py:427
  94.0 9.4 %collective-permute-done.2.cross_ref = f32[16,128,128]{2,1,0:T(8,128)S(1)} collective-permute-done((f32[16,128,128]{2,1,0:T(8,128)S(1)}, f32[16,128,128]{2,1,0:T(8,128)S(1)}, u32[]{:S(2)}, u32[]{:S(2)}) %collective-permute-start.2) | collective-permute-done | bytes 1048608 | tf_op jit(solution)/shard_map/ppermute | solution.py:428
  103.4 9.7 %collective-permute-done.1.same_ref = f32[16,128,128]{2,1,0:T(8,128)} collective-permute-done((f32[16,128,128]{2,1,0:T(8,128)S(1)}, f32[16,128,128]{2,1,0:T(8,128)}, u32[]{:S(2)}, u32[]{:S(2)}) %collective-permute-start.1) | collective-permute-done | bytes 1048608 | tf_op jit(solution)/shard_map/ppermute | solution.py:427
  113.1 11.0 %time_filter.1 = f32[4,16,128,128]{3,2,1,0:T(8,128)} custom-call(s32[2]{0:T(128)} %pad_add_fusion.where_ref, f32[16,128,128]{2,1,0:T(8,128)} %copy-done.1, f32[16,128,128]{2,1,0:T(8,128)} %collective-permute-done.part_ref, f32[16,128,128]{2,1,0:T(8,128)} %collective-permute-done.1.same_ref, f32[16,128,128]{2,1,0:T(8,128)} %copy-done.3, ...), custom_call_target="tpu_custom_call" | custom-call | tf_op jit(solution)/shard_map/time_filter/pallas_call | solution.py:400
  124.1 3.5 %slice_bitcast_fusion = (f32[16,128,128]{2,1,0:T(8,128)S(1)}, f32[16,128,128]{2,1,0:T(8,128)S(1)}, f32[16,128,128]{2,1,0:T(8,128)S(1)}, f32[16,128,128]{2,1,0:T(8,128)}) fusion(f32[4,16,128,128]{3,2,1,0:T(8,128)} %time_filter.1), kind=kLoop, calls=%fused_computation | loop fusion | bytes 8388608 | tf_op jit(solution)/shard_map/squeeze | solution.py:432
  127.6 4.1 %collective-permute-start.6 = (f32[16,128,128]{2,1,0:T(8,128)S(1)}, f32[16,128,128]{2,1,0:T(8,128)S(1)}, u32[]{:S(2)}, u32[]{:S(2)}) collective-permute-start(f32[16,128,128]{2,1,0:T(8,128)S(1)} %get-tuple-element.5), channel_id=1, source_target_pairs={{2,1},{1,2},{3,128},{128,3},{130,129},{129,130},{131,161},{161,131... | collective-permute-start | bytes 3145736 | tf_op jit(solution)/shard_map/ppermute | solution.py:432
  131.7 1.5 collective-permute-start.4
  133.2 18.9 %collective-permute-done.6.cross_ref = f32[16,128,128]{2,1,0:T(8,128)S(1)} collective-permute-done((f32[16,128,128]{2,1,0:T(8,128)S(1)}, f32[16,128,128]{2,1,0:T(8,128)S(1)}, u32[]{:S(2)}, u32[]{:S(2)}) %collective-permute-start.6) | collective-permute-done | bytes 1048608 | tf_op jit(solution)/shard_map/ppermute | solution.py:432
  152.1 3.2 %collective-permute-done.4.halo_ref = f32[16,128,128]{2,1,0:T(8,128)S(1)} collective-permute-done((f32[16,128,128]{2,1,0:T(8,128)S(1)}, f32[16,128,128]{2,1,0:T(8,128)S(1)}, u32[]{:S(2)}, u32[]{:S(2)}) %collective-permute-start.4) | collective-permute-done | bytes 1048608 | tf_op jit(solution)/shard_map/ppermute | solution.py:431
  155.4 1.0 copy-done.6
  156.3 8.6 %inverse_space.1 = f32[4096,128]{1,0:T(8,128)} custom-call(s32[2]{0:T(128)} %pad_add_fusion.where_ref, f32[16,128,128]{2,1,0:T(8,128)} %get-tuple-element.8.own_ref, f32[16,128,128]{2,1,0:T(8,128)} %copy-done.6, f32[16,128,128]{2,1,0:T(8,128)} %copy-done.5, f32[16,128,128]{2,1,0:T(8,128)} %copy-done.4, bf16[32,128,384]{2,1,0:T(8,128)(2,1)} %constant.35.clone.inv_ref, ...), custom_call_target="tpu_custom_call" | custom-call | tf_op jit(solution)/shard_map/inverse_space/pallas_call | solution.py:270
  164.9 61.0 %all_to_all.10 = f32[256,16,128]{2,1,0:T(8,128)} all-to-all(f32[256,16,128]{2,1,0:T(8,128)} %bitcast.15), channel_id=1, replica_groups=mesh['chan'=128,'tile'=2] {'chan','tile'}, dimensions={0} | all-to-all | bytes 4194304 | tf_op jit(solution)/shard_map/all_to_all | solution.py:434
  225.9 5.6 %unplane.1 = f32[16,32768]{1,0:T(8,128)} custom-call(f32[2,4,8,2,2,16,128]{6,5,4,3,2,1,0:T(8,128)} %bitcast.16), custom_call_target="tpu_custom_call" | custom-call | tf_op jit(solution)/shard_map/unplane/pallas_call | solution.py:210
  (17 shorter events, 0.2 us)
Async XLA Ops:
  9.0 67.5 %all-to-all-start = ((f32[256,16,128]{2,1,0:T(8,128)}), f32[256,16,128]{2,1,0:T(8,128)S(1)}, u32[]{:S(2)}, u32[]{:S(2)}) async-start(f32[256,16,128]{2,1,0:T(8,128)} %bitcast.14), calls=%async_computation | async-start | bytes 4194304 | tf_op jit(solution)/shard_map/all_to_all | solution.py:423
  29.2 64.8 %collective-permute-start.3 = (f32[2,16,64,128]{3,2,1,0:T(8,128)}, f32[2,16,64,128]{3,2,1,0:T(8,128)S(1)}, u32[]{:S(2)}, u32[]{:S(2)}) collective-permute-start(f32[2,16,64,128]{3,2,1,0:T(8,128)} %gains.1.mine_ref), channel_id=1, source_target_pairs={{0,1},{1,0},{2,3},{3,2},{4,5},{5,4},{6,7},{7,6},{8,9},{9,8},{10,11... | collective-permute-start | bytes 3145736 | tf_op jit(solution)/shard_map/ppermute | solution.py:418
  76.5 1.3 copy-start
  87.2 25.8 %copy-start.1 = (f32[16,128,128]{2,1,0:T(8,128)}, f32[16,128,128]{2,1,0:T(8,128)S(1)}, u32[]{:S(2)}) copy-start(f32[16,128,128]{2,1,0:T(8,128)S(1)} %get-tuple-element.10.own_ref) | copy-start | bytes 3145732
  87.2 16.1 %collective-permute-start.2 = (f32[16,128,128]{2,1,0:T(8,128)S(1)}, f32[16,128,128]{2,1,0:T(8,128)S(1)}, u32[]{:S(2)}, u32[]{:S(2)}) collective-permute-start(f32[16,128,128]{2,1,0:T(8,128)S(1)} %get-tuple-element.9), channel_id=1, source_target_pairs={{1,2},{2,1},{128,3},{3,128},{129,130},{130,129},{161,131},{131,161... | collective-permute-start | bytes 3145736 | tf_op jit(solution)/shard_map/ppermute | solution.py:428
  90.1 13.2 %collective-permute-start = (f32[16,128,128]{2,1,0:T(8,128)S(1)}, f32[16,128,128]{2,1,0:T(8,128)}, u32[]{:S(2)}, u32[]{:S(2)}) collective-permute-start(f32[16,128,128]{2,1,0:T(8,128)S(1)} %get-tuple-element.9), channel_id=1, source_target_pairs={{0,2},{2,0},{1,3},{3,1},{128,130},{130,128},{129,131},{131,129},{1... | collective-permute-start | bytes 3145736 | tf_op jit(solution)/shard_map/ppermute | solution.py:426
  90.2 22.9 %collective-permute-start.1 = (f32[16,128,128]{2,1,0:T(8,128)S(1)}, f32[16,128,128]{2,1,0:T(8,128)}, u32[]{:S(2)}, u32[]{:S(2)}) collective-permute-start(f32[16,128,128]{2,1,0:T(8,128)S(1)} %get-tuple-element.10.own_ref), channel_id=1, source_target_pairs={{1,0},{2,3},{128,1},{3,130},{129,128},{130,131},{161,129},{131,163... | collective-permute-start | bytes 3145736 | tf_op jit(solution)/shard_map/ppermute | solution.py:427
  94.0 19.1 %copy-start.2 = (f32[2,16,64,128]{3,2,1,0:T(8,128)}, f32[2,16,64,128]{3,2,1,0:T(8,128)S(1)}, u32[]{:S(2)}) copy-start(f32[2,16,64,128]{3,2,1,0:T(8,128)S(1)} %collective-permute-done.3.theirs_ref) | copy-start | bytes 3145732
  103.3 9.7 %copy-start.3 = (f32[16,128,128]{2,1,0:T(8,128)}, f32[16,128,128]{2,1,0:T(8,128)S(1)}, u32[]{:S(2)}) copy-start(f32[16,128,128]{2,1,0:T(8,128)S(1)} %collective-permute-done.2.cross_ref) | copy-start | bytes 3145732
  127.6 24.6 %collective-permute-start.6 = (f32[16,128,128]{2,1,0:T(8,128)S(1)}, f32[16,128,128]{2,1,0:T(8,128)S(1)}, u32[]{:S(2)}, u32[]{:S(2)}) collective-permute-start(f32[16,128,128]{2,1,0:T(8,128)S(1)} %get-tuple-element.5), channel_id=1, source_target_pairs={{2,1},{1,2},{3,128},{128,3},{130,129},{129,130},{131,161},{161,131... | collective-permute-start | bytes 3145736 | tf_op jit(solution)/shard_map/ppermute | solution.py:432
  131.6 20.5 %collective-permute-start.5 = (f32[16,128,128]{2,1,0:T(8,128)S(1)}, f32[16,128,128]{2,1,0:T(8,128)S(1)}, u32[]{:S(2)}, u32[]{:S(2)}) collective-permute-start(f32[16,128,128]{2,1,0:T(8,128)S(1)} %get-tuple-element.6), channel_id=1, source_target_pairs={{0,2},{2,0},{1,3},{3,1},{128,130},{130,128},{129,131},{131,129},{1... | collective-permute-start | bytes 3145736 | tf_op jit(solution)/shard_map/ppermute | solution.py:430
  131.7 23.6 %collective-permute-start.4 = (f32[16,128,128]{2,1,0:T(8,128)S(1)}, f32[16,128,128]{2,1,0:T(8,128)S(1)}, u32[]{:S(2)}, u32[]{:S(2)}) collective-permute-start(f32[16,128,128]{2,1,0:T(8,128)S(1)} %get-tuple-element.7), channel_id=1, source_target_pairs={{0,1},{3,2},{1,128},{130,3},{128,129},{131,130},{129,161},{163,131... | collective-permute-start | bytes 3145736 | tf_op jit(solution)/shard_map/ppermute | solution.py:431
  152.1 3.2 %copy-start.4 = (f32[16,128,128]{2,1,0:T(8,128)}, f32[16,128,128]{2,1,0:T(8,128)S(1)}, u32[]{:S(2)}) copy-start(f32[16,128,128]{2,1,0:T(8,128)S(1)} %collective-permute-done.6.cross_ref) | copy-start | bytes 3145732
  152.1 3.2 %copy-start.5 = (f32[16,128,128]{2,1,0:T(8,128)}, f32[16,128,128]{2,1,0:T(8,128)S(1)}, u32[]{:S(2)}) copy-start(f32[16,128,128]{2,1,0:T(8,128)S(1)} %collective-permute-done.5.part_ref) | copy-start | bytes 3145732
  155.4 1.0 copy-start.6

commit v2 on v1

--- a/solution.py
+++ b/solution.py
@@ -1,4 +1,4 @@
-import math
+import functools
 
 import jax
 import jax.numpy as jnp
@@ -20,10 +20,21 @@
 BLK = 128
 SLOTS = 32
 HALF = 16
+CHUNKS = 2
+WIDTH = HALF // CHUNKS
+PART = 2 * WIDTH
 AXES = ("chan", "tile")
 F32 = jnp.float32
 BF16 = jnp.bfloat16
-BIG = 60 * 1024 * 1024
+MIB = 1024 * 1024
+
+
+def params(mib):
+    return pltpu.CompilerParams(vmem_limit_bytes=mib * MIB)
+
+
+VMEM = pl.BlockSpec(memory_space=pltpu.VMEM)
+SMEM = pl.BlockSpec(memory_space=pltpu.SMEM)
 
 
 def two(table):
@@ -38,19 +49,24 @@
     return np.concatenate([hi, hi, lo], axis=-1)
 
 
-def own_first(table, axis):
-    other = np.roll(table, -HALF, axis=axis)
-    return np.stack([table, other], axis=0)
+def slot_order(core):
+    width = HALF // CHUNKS
+    order = []
+    for g in range(CHUNKS):
+        order += [(i + HALF * core) % SLOTS for i in range(g * width, (g + 1) * width)]
+        order += [(i + HALF * (1 - core)) % SLOTS for i in range(g * width, (g + 1) * width)]
+    return np.array(order)
 
 
 def spatial_tables():
     c1 = np.arange(ROOT)
     slot = np.arange(SLOTS)[:, None]
     angle = 2 * np.pi / ROOT * (slot * c1 % ROOT)
-    re, im = np.cos(angle), np.sin(angle)
-    im[0] = -((-1.0) ** c1)
-    first = np.stack([re, -im], axis=0)
-    first = own_first(first, 1).reshape(2, ROOT, ROOT)
+    re, im = np.cos(angle), -np.sin(angle)
+    im[0] = (-1.0) ** c1
+    first = np.stack([re, im], axis=0)
+    first = np.stack([first[:, slot_order(core)] for core in (0, 1)])
+    first = first.reshape(2, 2, CHUNKS, SLOTS // CHUNKS, ROOT).swapaxes(1, 2).reshape(2, ROOT, ROOT)
     c0 = np.arange(ROOT)[None, :]
     k2 = np.arange(ROOT)[:, None]
     second = np.zeros((SLOTS, 2, ROOT, 2, ROOT))
@@ -149,15 +165,16 @@
         i = lax.broadcasted_iota(jnp.int32, (TAPS, TAPS), 0)
         j = lax.broadcasted_iota(jnp.int32, (TAPS, TAPS), 1)
         mirror = (i + j == TAPS - 1).astype(BF16)
-        mirrored = dot(taps_ref[...], mirror)
-        rows = jnp.broadcast_to(mirrored[:1], (BLK, TAPS))
-        wide = jnp.concatenate([rows, jnp.zeros((BLK, span - TAPS), F32)], axis=1)
-        band_ref[...] = pltpu.roll(wide, 1, 1, stride=DEC, stride_axis=0).astype(BF16)
+        rows = jnp.broadcast_to(taps_ref[...].astype(F32), (BLK, TAPS))
+        mirrored = dot(rows.astype(BF16), mirror)
+        wide = jnp.concatenate([mirrored, jnp.zeros((BLK, span - TAPS), F32)], axis=1)
+        wide = pltpu.roll(wide, 1, 1, stride=DEC, stride_axis=0)
+        band_ref[...] = wide.T.astype(BF16)
 
     tail = jnp.where(plane == 0, jnp.zeros_like(tail_ref[...]), tail_ref[...])
     blocks = cur_ref.shape[1] // (DEC * BLK)
     band = band_ref[...]
-    group = 8
+    group = 16
     for b0 in range(0, blocks, group):
         spans = []
         for b in range(b0, b0 + group):
@@ -166,9 +183,7 @@
                 spans.append(jnp.concatenate([tail, cur_ref[:, : DEC * BLK]], axis=1))
             else:
                 spans.append(cur_ref[:, start - TAPS : start + DEC * BLK])
-        result = lax.dot_general(
-            jnp.concatenate(spans, axis=0), band, (((1,), (1,)), ((), ())), preferred_element_type=F32
-        )
+        result = dot(jnp.concatenate(spans, axis=0), band)
         for n in range(group):
             xh, row, core, xl = plane_slot(b0 + n)
             y = jnp.where(plane % 2 == 0, row, 3 - row)
@@ -179,29 +194,30 @@
     channels, length = raw.shape
     planes = 8
     width = length // planes
-    taps = jnp.broadcast_to(taps[None, :], (16, TAPS))
     return pl.pallas_call(
         decimate_kernel,
         grid=(planes,),
         in_specs=[
-            pl.BlockSpec((16, TAPS), lambda g: (0, 0)),
+            pl.BlockSpec((1, TAPS), lambda g: (0, 0)),
             pl.BlockSpec((channels, TAPS), lambda g: (0, jnp.maximum(g * (width // TAPS) - 1, 0))),
             pl.BlockSpec((channels, width), lambda g: (0, g)),
         ],
         out_specs=pl.BlockSpec((2, 4, 1, 2, 2, channels, BLK), lambda g: (0, 0, g, 0, 0, 0, 0)),
         out_shape=jax.ShapeDtypeStruct((2, 4, planes, 2, 2, channels, BLK), F32),
-        scratch_shapes=[pltpu.VMEM((BLK, TAPS + DEC * BLK), BF16)],
-        compiler_params=pltpu.CompilerParams(vmem_limit_bytes=BIG),
+        scratch_shapes=[pltpu.VMEM((TAPS + DEC * BLK, BLK), BF16)],
+        compiler_params=params(12),
         name="decimate",
-    )(taps, raw, raw)
+    )(taps.reshape(1, TAPS), raw, raw)
 
 
 def unplane_kernel(in_ref, out_ref):
-    plane = pl.program_id(0)
-    for b in range(32):
-        xh, row, core, xl = plane_slot(b)
-        y = jnp.where(plane % 2 == 0, row, 3 - row)
-        out_ref[:, b * BLK : (b + 1) * BLK] = in_ref[xh, y, 0, core, xl]
+    planes = in_ref.shape[2]
+    for plane in range(planes):
+        for b in range(32):
+            xh, row, core, xl = plane_slot(b)
+            y = row if plane % 2 == 0 else 3 - row
+            start = (plane * 32 + b) * BLK
+            out_ref[:, start : start + BLK] = in_ref[xh, y, plane, core, xl]
 
 
 def unplane(blocks):
@@ -209,73 +225,129 @@
     channels = blocks.shape[5]
     return pl.pallas_call(
         unplane_kernel,
-        grid=(planes,),
-        in_specs=[pl.BlockSpec((2, 4, 1, 2, 2, channels, BLK), lambda g: (0, 0, g, 0, 0, 0, 0))],
-        out_specs=pl.BlockSpec((channels, 32 * BLK), lambda g: (0, g)),
+        in_specs=[VMEM],
+        out_specs=VMEM,
         out_shape=jax.ShapeDtypeStruct((channels, planes * 32 * BLK), F32),
-        compiler_params=pltpu.CompilerParams(vmem_limit_bytes=BIG),
+        compiler_params=params(8),
         name="unplane",
     )(blocks)
 
 
-def forward_kernel(where_ref, x_ref, first_ref, second_ref, out_ref, mid_ref):
+def real_slot(core, chunk, i):
+    s = chunk * WIDTH + i % WIDTH + (HALF if i >= WIDTH else 0)
+    return lax.rem(s + HALF * core, SLOTS)
+
+
+def second_stage(core, chunk, mid_ref, second_ref, own_ref, other_ref):
+    for i in range(PART):
+        re = mid_ref[pl.ds(i, ROOT, stride=2 * PART), :]
+        im = mid_ref[pl.ds(PART + i, ROOT, stride=2 * PART), :]
+        table = second_ref[real_slot(core, chunk, i)]
+        wave = dot(table, stacked(jnp.concatenate([re, im], axis=0)))
+        if i < WIDTH:
+            own_ref[i] = wave
+        else:
+            other_ref[i - WIDTH] = wave
+
+
+def forward_kernel(where_ref, x_ref, first_ref, second_ref, own_ref, other_ref, *rest):
+    later, mid_ref = rest[:-1], rest[-1]
     core = where_ref[0]
     first = first_ref[core]
+    rows = 2 * PART
     for c0 in range(0, ROOT, 2):
         one = stacked(x_ref[pl.ds(c0, ROOT, stride=ROOT), :])
         two_ = stacked(x_ref[pl.ds(c0 + 1, ROOT, stride=ROOT), :])
         y = dot(first, jnp.concatenate([one, two_], axis=1))
-        mid_ref[c0 * ROOT : (c0 + 1) * ROOT, :] = y[:, :BLK]
-        mid_ref[(c0 + 1) * ROOT : (c0 + 2) * ROOT, :] = y[:, BLK:]
-    for s in range(SLOTS):
-        re = mid_ref[pl.ds(s, ROOT, stride=ROOT), :]
-        im = mid_ref[pl.ds(SLOTS + s, ROOT, stride=ROOT), :]
-        table = second_ref[lax.rem(s + HALF * core, SLOTS)]
-        out_ref[s] = dot(table, stacked(jnp.concatenate([re, im], axis=0)))
+        for g, ref in enumerate((mid_ref,) + later):
+            ref[c0 * rows : (c0 + 1) * rows, :] = y[g * rows : (g + 1) * rows, :BLK]
+            ref[(c0 + 1) * rows : (c0 + 2) * rows, :] = y[g * rows : (g + 1) * rows, BLK:]
+    second_stage(core, 0, mid_ref, second_ref, own_ref, other_ref)
 
 
 def forward_space(where, x, first, second):
+    wave = jax.ShapeDtypeStruct((WIDTH, BLK, BLK), F32)
+    middle = jax.ShapeDtypeStruct((K // CHUNKS, BLK), F32)
     return pl.pallas_call(
         forward_kernel,
-        in_specs=[pl.BlockSpec(memory_space=pltpu.SMEM)] + [pl.BlockSpec(memory_space=pltpu.VMEM)] * 3,
-        out_specs=pl.BlockSpec(memory_space=pltpu.VMEM),
-        out_shape=jax.ShapeDtypeStruct((SLOTS, BLK, BLK), F32),
-        scratch_shapes=[pltpu.VMEM((K, BLK), F32)],
-        compiler_params=pltpu.CompilerParams(vmem_limit_bytes=BIG),
+        in_specs=[SMEM] + [VMEM] * 3,
+        out_specs=[VMEM] * (1 + CHUNKS),
+        out_shape=[wave] * 2 + [middle] * (CHUNKS - 1),
+        scratch_shapes=[pltpu.VMEM((K // CHUNKS, BLK), F32)],
+        compiler_params=params(14),
         name="forward_space",
     )(where, x, first, second)
 
 
-def inverse_kernel(where_ref, own_ref, halo_ref, part_ref, cross_ref, inv_ref, last_ref, out_ref, mid_ref):
+def forward_more_kernel(chunk, where_ref, mid_ref, second_ref, own_ref, other_ref):
+    second_stage(where_ref[0], chunk, mid_ref, second_ref, own_ref, other_ref)
+
+
+def forward_more(chunk, where, middle, second):
+    wave = jax.ShapeDtypeStruct((WIDTH, BLK, BLK), F32)
+    return pl.pallas_call(
+        functools.partial(forward_more_kernel, chunk),
+        in_specs=[SMEM] + [VMEM] * 2,
+        out_specs=[VMEM] * 2,
+        out_shape=[wave] * 2,
+        compiler_params=params(12),
+        name="forward_more",
+    )(where, middle, second)
+
+
+def inverse_stage(core, chunk, own_ref, halo_ref, part_ref, cross_ref, inv_ref, mid_ref):
+    for i in range(PART):
+        if i < WIDTH:
+            z = own_ref[i] + halo_ref[i]
+        else:
+            z = part_ref[i - WIDTH] + cross_ref[i - WIDTH]
+        u = dot(inv_ref[real_slot(core, chunk, i)], stacked(z))
+        mid_ref[pl.ds(i, ROOT, stride=2 * PART), :] = u[:ROOT]
+        mid_ref[pl.ds(PART + i, ROOT, stride=2 * PART), :] = u[ROOT:]
+
+
+def inverse_more_kernel(chunk, where_ref, own_ref, halo_ref, part_ref, cross_ref, inv_ref, mid_ref):
+    inverse_stage(where_ref[0], chunk, own_ref, halo_ref, part_ref, cross_ref, inv_ref, mid_ref)
+
+
+def inverse_more(chunk, where, waves, inv):
+    return pl.pallas_call(
+        functools.partial(inverse_more_kernel, chunk),
+        in_specs=[SMEM] + [VMEM] * 5,
+        out_specs=VMEM,
+        out_shape=jax.ShapeDtypeStruct((K // CHUNKS, BLK), F32),
+        compiler_params=params(12),
+        name="inverse_more",
+    )(where, *waves, inv)
+
+
+def inverse_kernel(where_ref, own_ref, halo_ref, part_ref, cross_ref, inv_ref, last_ref, *rest):
+    earlier, out_ref, mid_ref = rest[:-2], rest[-2], rest[-1]
     core = where_ref[0]
-    for s in range(SLOTS):
-        if s < HALF:
-            z = own_ref[s] + halo_ref[s]
-        else:
-            z = part_ref[s - HALF] + cross_ref[s - HALF]
-        table = inv_ref[lax.rem(s + HALF * core, SLOTS)]
-        u = dot(table, stacked(z))
-        mid_ref[pl.ds(s, ROOT, stride=ROOT), :] = u[:ROOT]
-        mid_ref[pl.ds(SLOTS + s, ROOT, stride=ROOT), :] = u[ROOT:]
+    inverse_stage(core, CHUNKS - 1, own_ref, halo_ref, part_ref, cross_ref, inv_ref, mid_ref)
     last = last_ref[core]
+    rows = 2 * PART
+    refs = earlier + (mid_ref,)
+
+    def column(c0):
+        return stacked(jnp.concatenate([ref[c0 * rows : (c0 + 1) * rows, :] for ref in refs], axis=0))
+
     for c0 in range(0, ROOT, 2):
-        one = stacked(mid_ref[c0 * ROOT : (c0 + 1) * ROOT, :])
-        two_ = stacked(mid_ref[(c0 + 1) * ROOT : (c0 + 2) * ROOT, :])
-        y = dot(last, jnp.concatenate([one, two_], axis=1))
+        y = dot(last, jnp.concatenate([column(c0), column(c0 + 1)], axis=1))
         out_ref[pl.ds(c0, ROOT, stride=ROOT), :] = y[:, :BLK]
         out_ref[pl.ds(c0 + 1, ROOT, stride=ROOT), :] = y[:, BLK:]
 
 
-def inverse_space(where, own, halo, part, cross, inv, last):
+def inverse_space(where, waves, earlier, inv, last):
     return pl.pallas_call(
         inverse_kernel,
-        in_specs=[pl.BlockSpec(memory_space=pltpu.SMEM)] + [pl.BlockSpec(memory_space=pltpu.VMEM)] * 6,
-        out_specs=pl.BlockSpec(memory_space=pltpu.VMEM),
+        in_specs=[SMEM] + [VMEM] * (6 + len(earlier)),
+        out_specs=VMEM,
         out_shape=jax.ShapeDtypeStruct((K, BLK), F32),
-        scratch_shapes=[pltpu.VMEM((K, BLK), F32)],
-        compiler_params=pltpu.CompilerParams(vmem_limit_bytes=BIG),
+        scratch_shapes=[pltpu.VMEM((K // CHUNKS, BLK), F32)],
+        compiler_params=params(14),
         name="inverse_space",
-    )(where, own, halo, part, cross, inv, last)
+    )(where, *waves, inv, last, *earlier)
 
 
 def gains_kernel(where_ref, gain_ref, band_ref, out_ref):
@@ -324,15 +396,17 @@
 def gains(where, band_gain, fan_band):
     return pl.pallas_call(
         gains_kernel,
-        in_specs=[pl.BlockSpec(memory_space=pltpu.SMEM)] * 2 + [pl.BlockSpec(memory_space=pltpu.VMEM)],
-        out_specs=pl.BlockSpec(memory_space=pltpu.VMEM),
+        in_specs=[SMEM] * 2 + [VMEM],
+        out_specs=VMEM,
         out_shape=jax.ShapeDtypeStruct((2, HALF, ROOT, BLK), F32),
-        compiler_params=pltpu.CompilerParams(vmem_limit_bytes=BIG),
+        compiler_params=params(8),
         name="gains",
     )(where, band_gain, fan_band)
 
 
-def time_kernel(where_ref, own_ref, part_ref, same_ref, cross_ref, mine_ref, theirs_ref, fwd_ref, bwd_ref, out_ref):
+def time_kernel(first_chunk, where_ref, *refs):
+    own_ref, part_ref, same_ref, cross_ref, mine_ref, theirs_ref, fwd_ref, bwd_ref = refs[:8]
+    out_refs = refs[8:]
     core, xl = where_ref[0], where_ref[1]
     step = pl.program_id(0)
     slots = own_ref.shape[0]
@@ -370,7 +444,7 @@
 
         gs, gd = wide(0), wide(1)
         gr = gi = gs
-        if s == 0:
+        if s == 0 and first_chunk:
             row = lax.broadcasted_iota(jnp.int32, (ROOT, BINS), 0)
             pair = (row == 0) & (step == 0) & even
             gr = jnp.where(pair, gs + gd, gs)
@@ -381,31 +455,32 @@
     hi, lo = split(jnp.concatenate(pieces, axis=0))
     bwd_hi = bwd_ref[0]
     z = dot(hi, bwd_hi) + dot(lo, bwd_hi) + dot(hi, bwd_ref[1])
-    places = [
-        jnp.where(even, 3, 2),
-        jnp.where(even, 0, 1),
-        jnp.where(even, 1, 0),
-        jnp.where(even, 2, 3),
+    before, low, high, after = (z[:, n * BLK : (n + 1) * BLK] for n in range(4))
+    outs = [
+        jnp.where(even, low, high),
+        jnp.where(even, high, low),
+        jnp.where(even, after, before),
+        jnp.where(even, before, after),
     ]
-    for n in range(4):
-        out_ref[places[n]] = z[:, n * BLK : (n + 1) * BLK].reshape(slots, BLK, BLK)
-
-
-def time_filter(where, own, part, same, cross, mine, theirs, fwd, bwd):
-    total = own.shape[0]
+    for out_ref, value in zip(out_refs, outs):
+        out_ref[...] = value.reshape(slots, BLK, BLK)
+
+
+def time_filter(chunk, where, waves, mine, theirs, fwd, bwd):
     slots = 4
+    steps = WIDTH // slots
     data = pl.BlockSpec((slots, BLK, BLK), lambda g: (g, 0, 0))
-    gain = pl.BlockSpec((2, slots, ROOT, BLK), lambda g: (0, g, 0, 0))
+    gain = pl.BlockSpec((2, slots, ROOT, BLK), lambda g: (0, chunk * steps + g, 0, 0))
     table = pl.BlockSpec((2, WIN, WIN), lambda g: (0, 0, 0))
     return pl.pallas_call(
-        time_kernel,
-        grid=(total // slots,),
-        in_specs=[pl.BlockSpec(memory_space=pltpu.SMEM)] + [data] * 4 + [gain] * 2 + [table] * 2,
-        out_specs=pl.BlockSpec((4, slots, BLK, BLK), lambda g: (0, g, 0, 0)),
-        out_shape=jax.ShapeDtypeStruct((4, total, BLK, BLK), F32),
-        compiler_params=pltpu.CompilerParams(vmem_limit_bytes=BIG),
+        functools.partial(time_kernel, chunk == 0),
+        grid=(steps,),
+        in_specs=[SMEM] + [data] * 4 + [gain] * 2 + [table] * 2,
+        out_specs=[data] * 4,
+        out_shape=[jax.ShapeDtypeStruct((WIDTH, BLK, BLK), F32)] * 4,
+        compiler_params=params(24),
         name="time_filter",
-    )(where, own, part, same, cross, mine, theirs, fwd, bwd)
+    )(where, *waves, mine, theirs, fwd, bwd)
 
 
 def body(raw_strain, fir_taps, fan_band, band_gain):
@@ -421,16 +496,24 @@
     shape = blocks.shape
     blocks = blocks.reshape((256,) + shape[5:])
     blocks = lax.all_to_all(blocks, AXES, 0, 0, tiled=True)
-    waves = forward_space(where, blocks.reshape(K, BLK), first, second)
-    own, other = waves[:HALF], waves[HALF:]
-    from_partner = lax.ppermute(other, AXES, partner)
-    from_same = lax.ppermute(own, AXES, same)
-    from_cross = lax.ppermute(other, AXES, cross)
-    z = time_filter(where, own, from_partner, from_same, from_cross, mine, theirs, fwd, bwd)
-    back_partner = lax.ppermute(z[1], AXES, partner)
-    back_same = lax.ppermute(z[2], AXES, flipped(same))
-    back_cross = lax.ppermute(z[3], AXES, flipped(cross))
-    filtered = inverse_space(where, z[0], back_same, back_partner, back_cross, inverse, last)
+    own, other, *middle = forward_space(where, blocks.reshape(K, BLK), first, second)
+    received = []
+    for g in range(CHUNKS):
+        if g:
+            own, other = forward_more(g, where, middle[g - 1], second)
+        from_partner = lax.ppermute(other, AXES, partner)
+        from_same = lax.ppermute(own, AXES, same)
+        from_cross = lax.ppermute(other, AXES, cross)
+        received.append((own, from_partner, from_same, from_cross))
+    returned = []
+    for g in range(CHUNKS):
+        own, part, halo, far = time_filter(g, where, received[g], mine, theirs, fwd, bwd)
+        back_partner = lax.ppermute(part, AXES, partner)
+        back_same = lax.ppermute(halo, AXES, flipped(same))
+        back_cross = lax.ppermute(far, AXES, flipped(cross))
+        returned.append((own, back_same, back_partner, back_cross))
+    earlier = [inverse_more(g, where, returned[g], inverse) for g in range(CHUNKS - 1)]
+    filtered = inverse_space(where, returned[-1], earlier, inverse, last)
     filtered = lax.all_to_all(filtered.reshape(256, 16, BLK), AXES, 0, 0, tiled=True)
     return unplane(filtered.reshape(shape))
 

time: 232 us -> 196 us (0.84)
  waiting for transfers between devices: 87.1 us -> 58.3 us
  Pallas kernels: 44.6 us -> 30.5 us
  starting transfers between devices: 29.4 us -> 41.7 us
  local copies, waits for them, and re-layouts: 8.78 us -> 4.62 us
    ppermute x3 -> x6, waiting for transfers between devices: 22.1 us -> 9.08 us  [the longest x2 4.6 us: body(): back_cross = lax.ppermute(far, AXES, flipped(cross))]
    pallas_call x5 -> x8, Pallas kernels: 36.8 us -> 25.5 us  [the longest x2 10.2 us: time_filter(): pl.pallas_call(functools.partial(time_kernel, chunk == 0), grid=(steps,),...]
    ppermute x1 -> x2, waiting for transfers between devices: 9.71 us -> 0.01 us  [body(): from_same = lax.ppermute(own, AXES, same)]
    ppermute x3 -> x6, starting transfers between devices: 5.65 us -> 12.5 us  [the longest x2 5.75 us: body(): back_cross = lax.ppermute(far, AXES, flipped(cross))]
    ppermute x1 -> x2, waiting for transfers between devices: 9.35 us -> 4.42 us  [body(): from_cross = lax.ppermute(other, AXES, cross)]
    squeeze x1 -> x0, local copies, waits for them, and re-layouts: 3.5 us -> none  [body(): back_cross = lax.ppermute(z[3], AXES, flipped(cross))]
    ppermute x1 -> x2, starting transfers between devices: 2.87 us -> 5.81 us  [body(): from_cross = lax.ppermute(other, AXES, cross)]
    pallas_call x1, Pallas kernels: 7.74 us -> 5 us  [decimate(): pl.pallas_call(decimate_kernel, grid=(planes,), in_specs=[pl.BlockSpec((1...]
  transfers between devices with their start and end apart: 8 -> 14, of which waited for: 5 -> 5; matrix products, arithmetic and copies ran while one was open for 1% -> 0% of each run, Pallas kernels for 5% -> 11%
where the time goes in v2:
time: 196 us; the launch traced here: 195 us
  blocking collectives  60 us (31%)
  waiting for transfers between devices  58.3 us (30%)
  starting transfers between devices  41.7 us (21%)
  Pallas kernels  30.5 us (16%)
  local copies, waits for them, and re-layouts  4.62 us (2%)
    all_to_all x1, blocking collectives, body(): lax.all_to_all(filtered.reshape(256, 16, BLK), AXES, 0, 0, tiled=True)  60 us
    all_to_all x1, waiting for transfers between devices, body(): blocks = lax.all_to_all(blocks, AXES, 0, 0, tiled=True)  44.8 us
    all_to_all x1, starting transfers between devices, body(): blocks = lax.all_to_all(blocks, AXES, 0, 0, tiled=True)  16.7 us
    pallas_call x2, Pallas kernels, time_filter(): pl.pallas_call(functools.partial(time_kernel, chunk == 0), grid=(steps,),...  10.2 us
    ppermute x2, starting transfers between devices, body(): from_cross = lax.ppermute(other, AXES, cross)  5.81 us
    ppermute x2, starting transfers between devices, body(): back_cross = lax.ppermute(far, AXES, flipped(cross))  5.75 us
    pallas_call x1, Pallas kernels, decimate(): pl.pallas_call(decimate_kernel, grid=(planes,), in_specs=[pl.BlockSpec((1...  5 us
    unnamed x20, local copies, waits for them, and re-layouts  4.62 us
  transfers between devices with their start and end apart: 14, of which 5 were waited for; matrix products, arithmetic and copies ran while one was open for 0% of the time, Pallas kernels for 11%

profile of v2, /device:TPU:1, one launch (start us, length us, event | category | flops | bytes accessed | tf_op | source)
XLA Modules:
  0.0 195.4 jit_solution(688947577814097188)
XLA Ops:
  0.0 2.2 %copy-done = bf16[16,131072]{1,0:T(8,128)(2,1)S(1)} copy-done((bf16[16,131072]{1,0:T(8,128)(2,1)S(1)}, bf16[16,131072]{1,0:T(8,128)(2,1)}, u32[]{:S(2)}) %copy-start) | copy-done | bytes 4194328
  2.8 5.0 %decimate.1 = f32[2,4,8,2,2,16,128]{6,5,4,3,2,1,0:T(8,128)} custom-call(bf16[1,128]{1,0:T(2,128)(2,1)S(1)} %bitcast.9, bf16[16,131072]{1,0:T(8,128)(2,1)S(1)} %copy-done, bf16[16,131072]{1,0:T(8,128)(2,1)S(1)} %copy-done), custom_call_target="tpu_custom_call" | custom-call | tf_op jit(solution)/shard_map/decimate/pallas_call | solution.py:197
  7.9 16.7 %all-to-all-start = ((f32[256,16,128]{2,1,0:T(8,128)}), f32[256,16,128]{2,1,0:T(8,128)}, u32[]{:S(2)}, u32[]{:S(2)}) async-start(f32[256,16,128]{2,1,0:T(8,128)} %bitcast.3), calls=%async_computation | async-start | bytes 4194304 | tf_op jit(solution)/shard_map/all_to_all | solution.py:498
  24.6 1.7 copy-done.5
  26.4 2.9 %gains.1.refs_4_ = f32[2,16,64,128]{3,2,1,0:T(8,128)} custom-call(s32[2]{0:T(128)S(1)} %pad_add_fusion.where_ref, f32[8]{0:T(128)S(1)} %copy-done.8, s32[4096,128]{1,0:T(8,128)S(1)} %copy-done.5), custom_call_target="tpu_custom_call" | custom-call | tf_op jit(solution)/shard_map/gains/pallas_call | solution.py:397
  30.7 44.8 %all-to-all-done = f32[256,16,128]{2,1,0:T(8,128)} async-done(((f32[256,16,128]{2,1,0:T(8,128)}), f32[256,16,128]{2,1,0:T(8,128)}, u32[]{:S(2)}, u32[]{:S(2)}) %all-to-all-start) | async-done | bytes 2097184 | tf_op jit(solution)/shard_map/all_to_all | solution.py:498
  75.5 4.0 %forward_space.1 = (f32[8,128,128]{2,1,0:T(8,128)S(1)}, f32[8,128,128]{2,1,0:T(8,128)S(1)}, f32[2048,128]{1,0:T(8,128)S(1)}) custom-call(s32[2]{0:T(128)S(1)} %pad_add_fusion.where_ref, f32[4096,128]{1,0:T(8,128)} %bitcast.4.x_ref, bf16[2,64,192]{2,1,0:T(8,128)(2,1)S(1)} %copy-done.7, bf16[32,128,384]{2,1,0:T(8,128)(2,1)S(1)} %copy-done.2), custom_call_target="tpu_custom_call" | custom-call | tf_op jit(solution)/shard_map/forward_space/pallas_call | solution.py:271
  80.8 1.9 collective-permute-start.8
  82.6 3.6 %collective-permute-start.9 = (f32[8,128,128]{2,1,0:T(8,128)S(1)}, f32[8,128,128]{2,1,0:T(8,128)S(1)}, u32[]{:S(2)}, u32[]{:S(2)}) collective-permute-start(f32[8,128,128]{2,1,0:T(8,128)S(1)} %get-tuple-element.26), channel_id=1, source_target_pairs={{1,2},{2,1},{128,3},{3,128},{129,130},{130,129},{161,131},{131,161... | collective-permute-start | bytes 1572872 | tf_op jit(solution)/shard_map/ppermute | solution.py:506
  86.3 1.6 forward_more.1
  88.0 2.2 %collective-permute-start.2 = (f32[8,128,128]{2,1,0:T(8,128)S(1)}, f32[8,128,128]{2,1,0:T(8,128)S(1)}, u32[]{:S(2)}, u32[]{:S(2)}) collective-permute-start(f32[8,128,128]{2,1,0:T(8,128)S(1)} %get-tuple-element.20), channel_id=1, source_target_pairs={{1,2},{2,1},{128,3},{3,128},{129,130},{130,129},{161,131},{131,161... | collective-permute-start | bytes 1572872 | tf_op jit(solution)/shard_map/ppermute | solution.py:506
  90.2 2.1 %collective-permute-start.1 = (f32[8,128,128]{2,1,0:T(8,128)S(1)}, f32[8,128,128]{2,1,0:T(8,128)S(1)}, u32[]{:S(2)}, u32[]{:S(2)}) collective-permute-start(f32[8,128,128]{2,1,0:T(8,128)S(1)} %get-tuple-element.19.refs_0_), channel_id=1, source_target_pairs={{1,0},{2,3},{128,1},{3,130},{129,128},{130,131},{161,129},{131,163... | collective-permute-start | bytes 1572872 | tf_op jit(solution)/shard_map/ppermute | solution.py:505
  92.4 4.4 %collective-permute-done.9.refs_3_ = f32[8,128,128]{2,1,0:T(8,128)S(1)} collective-permute-done((f32[8,128,128]{2,1,0:T(8,128)S(1)}, f32[8,128,128]{2,1,0:T(8,128)S(1)}, u32[]{:S(2)}, u32[]{:S(2)}) %collective-permute-start.9) | collective-permute-done | bytes 524320 | tf_op jit(solution)/shard_map/ppermute | solution.py:506
  96.8 5.1 %time_filter.3 = (f32[8,128,128]{2,1,0:T(8,128)S(1)}, f32[8,128,128]{2,1,0:T(8,128)S(1)}, f32[8,128,128]{2,1,0:T(8,128)S(1)}, f32[8,128,128]{2,1,0:T(8,128)S(1)}) custom-call(s32[2]{0:T(128)S(1)} %pad_add_fusion.where_ref, f32[8,128,128]{2,1,0:T(8,128)S(1)} %get-tuple-element.25.refs_0_, f32[8,128,128]{2,1,0:T(8,128)S(1)} %collective-permute-done.7.refs_1_, ...), custom_call_target="tpu_custom_call" | custom-call | tf_op jit(solution)/shard_map/time_filter/pallas_call | solution.py:475
  104.3 3.7 %collective-permute-start.12 = (f32[8,128,128]{2,1,0:T(8,128)S(1)}, f32[8,128,128]{2,1,0:T(8,128)S(1)}, u32[]{:S(2)}, u32[]{:S(2)}) collective-permute-start(f32[8,128,128]{2,1,0:T(8,128)S(1)} %get-tuple-element.30), channel_id=1, source_target_pairs={{2,1},{1,2},{3,128},{128,3},{130,129},{129,130},{131,161},{161,131... | collective-permute-start | bytes 1572872 | tf_op jit(solution)/shard_map/ppermute | solution.py:513
  108.1 5.1 %time_filter.2 = (f32[8,128,128]{2,1,0:T(8,128)S(1)}, f32[8,128,128]{2,1,0:T(8,128)S(1)}, f32[8,128,128]{2,1,0:T(8,128)S(1)}, f32[8,128,128]{2,1,0:T(8,128)S(1)}) custom-call(s32[2]{0:T(128)S(1)} %pad_add_fusion.where_ref, f32[8,128,128]{2,1,0:T(8,128)S(1)} %get-tuple-element.19.refs_0_, f32[8,128,128]{2,1,0:T(8,128)S(1)} %collective-permute-done.refs_1_, ...), custom_call_target="tpu_custom_call" | custom-call | tf_op jit(solution)/shard_map/time_filter/pallas_call | solution.py:475
  114.5 3.0 %collective-permute-start.5 = (f32[8,128,128]{2,1,0:T(8,128)S(1)}, f32[8,128,128]{2,1,0:T(8,128)S(1)}, u32[]{:S(2)}, u32[]{:S(2)}) collective-permute-start(f32[8,128,128]{2,1,0:T(8,128)S(1)} %get-tuple-element.23), channel_id=1, source_target_pairs={{0,2},{2,0},{1,3},{3,1},{128,130},{130,128},{129,131},{131,129},{1... | collective-permute-start | bytes 1572872 | tf_op jit(solution)/shard_map/ppermute | solution.py:511
  117.5 2.0 %collective-permute-start.6 = (f32[8,128,128]{2,1,0:T(8,128)S(1)}, f32[8,128,128]{2,1,0:T(8,128)S(1)}, u32[]{:S(2)}, u32[]{:S(2)}) collective-permute-start(f32[8,128,128]{2,1,0:T(8,128)S(1)} %get-tuple-element.24), channel_id=1, source_target_pairs={{2,1},{1,2},{3,128},{128,3},{130,129},{129,130},{131,161},{161,131... | collective-permute-start | bytes 1572872 | tf_op jit(solution)/shard_map/ppermute | solution.py:513
  120.9 1.9 inverse_more.1.rest_0_
  122.8 4.5 %collective-permute-done.4.halo_ref = f32[8,128,128]{2,1,0:T(8,128)S(1)} collective-permute-done((f32[8,128,128]{2,1,0:T(8,128)S(1)}, f32[8,128,128]{2,1,0:T(8,128)S(1)}, u32[]{:S(2)}, u32[]{:S(2)}) %collective-permute-start.4) | collective-permute-done | bytes 524320 | tf_op jit(solution)/shard_map/ppermute | solution.py:512
  127.3 3.2 %collective-permute-done.6.cross_ref = f32[8,128,128]{2,1,0:T(8,128)S(1)} collective-permute-done((f32[8,128,128]{2,1,0:T(8,128)S(1)}, f32[8,128,128]{2,1,0:T(8,128)S(1)}, u32[]{:S(2)}, u32[]{:S(2)}) %collective-permute-start.6) | collective-permute-done | bytes 524320 | tf_op jit(solution)/shard_map/ppermute | solution.py:513
  130.5 3.4 %inverse_space.1 = f32[4096,128]{1,0:T(8,128)S(1)} custom-call(s32[2]{0:T(128)S(1)} %pad_add_fusion.where_ref, f32[8,128,128]{2,1,0:T(8,128)S(1)} %get-tuple-element.21.own_ref, f32[8,128,128]{2,1,0:T(8,128)S(1)} %collective-permute-done.4.halo_ref, f32[8,128,128]{2,1,0:T(8,128)S(1)} %collective-permute-done.5.part_ref, ...), custom_call_target="tpu_custom_call" | custom-call | tf_op jit(solution)/shard_map/inverse_space/pallas_call | solution.py:342
  133.9 60.0 %all_to_all.10 = f32[256,16,128]{2,1,0:T(8,128)S(1)} all-to-all(f32[256,16,128]{2,1,0:T(8,128)S(1)} %bitcast.8), channel_id=1, replica_groups=mesh['chan'=128,'tile'=2] {'chan','tile'}, dimensions={0} | all-to-all | bytes 4194304 | tf_op jit(solution)/shard_map/all_to_all | solution.py:517
  194.0 1.5 unplane.1
  (35 shorter events, 8.6 us)
Async XLA Ops:
  0.0 2.2 %copy-start = (bf16[16,131072]{1,0:T(8,128)(2,1)S(1)}, bf16[16,131072]{1,0:T(8,128)(2,1)}, u32[]{:S(2)}) copy-start(bf16[16,131072]{1,0:T(8,128)(2,1)} %cur_ref.1) | copy-start | bytes 12582916
  2.2 0.7 copy-start.9
  7.8 16.8 %copy-start.8 = (f32[8]{0:T(128)S(1)}, f32[8]{0:T(128)}, u32[]{:S(2)}) copy-start(f32[8]{0:T(128)} %gain_ref.1) | copy-start | bytes 100
  7.8 67.6 %copy-start.7 = (bf16[2,64,192]{2,1,0:T(8,128)(2,1)S(1)}, bf16[2,64,192]{2,1,0:T(8,128)(2,1)}, u32[]{:S(2)}) copy-start(bf16[2,64,192]{2,1,0:T(8,128)(2,1)} %constant.33.clone.first_ref) | copy-start | bytes 147460
  7.9 67.6 %all-to-all-start = ((f32[256,16,128]{2,1,0:T(8,128)}), f32[256,16,128]{2,1,0:T(8,128)}, u32[]{:S(2)}, u32[]{:S(2)}) async-start(f32[256,16,128]{2,1,0:T(8,128)} %bitcast.3), calls=%async_computation | async-start | bytes 4194304 | tf_op jit(solution)/shard_map/all_to_all | solution.py:498
  24.5 51.0 %copy-start.2 = (bf16[32,128,384]{2,1,0:T(8,128)(2,1)S(1)}, bf16[32,128,384]{2,1,0:T(8,128)(2,1)}, u32[]{:S(2)}) copy-start(bf16[32,128,384]{2,1,0:T(8,128)(2,1)} %constant.34.clone.second_ref) | copy-start | bytes 9437188
  24.6 1.7 copy-start.5
  29.3 58.7 %collective-permute-start.3 = (f32[2,16,64,128]{3,2,1,0:T(8,128)}, f32[2,16,64,128]{3,2,1,0:T(8,128)}, u32[]{:S(2)}, u32[]{:S(2)}) collective-permute-start(f32[2,16,64,128]{3,2,1,0:T(8,128)} %gains.1.refs_4_), channel_id=1, source_target_pairs={{0,1},{1,0},{2,3},{3,2},{4,5},{5,4},{6,7},{7,6},{8,9},{9,8},{10,11... | collective-permute-start | bytes 3145736 | tf_op jit(solution)/shard_map/ppermute | solution.py:493
  79.5 10.7 %collective-permute-start.7 = (f32[8,128,128]{2,1,0:T(8,128)S(1)}, f32[8,128,128]{2,1,0:T(8,128)S(1)}, u32[]{:S(2)}, u32[]{:S(2)}) collective-permute-start(f32[8,128,128]{2,1,0:T(8,128)S(1)} %get-tuple-element.26), channel_id=1, source_target_pairs={{0,2},{2,0},{1,3},{3,1},{128,130},{130,128},{129,131},{131,129},{1... | collective-permute-start | bytes 1572872 | tf_op jit(solution)/shard_map/ppermute | solution.py:504
  80.8 11.6 %collective-permute-start.8 = (f32[8,128,128]{2,1,0:T(8,128)S(1)}, f32[8,128,128]{2,1,0:T(8,128)S(1)}, u32[]{:S(2)}, u32[]{:S(2)}) collective-permute-start(f32[8,128,128]{2,1,0:T(8,128)S(1)} %get-tuple-element.25.refs_0_), channel_id=1, source_target_pairs={{1,0},{2,3},{128,1},{3,130},{129,128},{130,131},{161,129},{131,163... | collective-permute-start | bytes 1572872 | tf_op jit(solution)/shard_map/ppermute | solution.py:505
  82.6 14.1 %collective-permute-start.9 = (f32[8,128,128]{2,1,0:T(8,128)S(1)}, f32[8,128,128]{2,1,0:T(8,128)S(1)}, u32[]{:S(2)}, u32[]{:S(2)}) collective-permute-start(f32[8,128,128]{2,1,0:T(8,128)S(1)} %get-tuple-element.26), channel_id=1, source_target_pairs={{1,2},{2,1},{128,3},{3,128},{129,130},{130,129},{161,131},{131,161... | collective-permute-start | bytes 1572872 | tf_op jit(solution)/shard_map/ppermute | solution.py:506
  86.2 10.5 %copy-start.3 = (bf16[2,512,512]{2,1,0:T(8,128)(2,1)S(1)}, bf16[2,512,512]{2,1,0:T(8,128)(2,1)}, u32[]{:S(2)}) copy-start(bf16[2,512,512]{2,1,0:T(8,128)(2,1)} %constant.37.clone.refs_6_) | copy-start | bytes 3145732
  86.3 10.5 %copy-start.4 = (bf16[2,512,512]{2,1,0:T(8,128)(2,1)S(1)}, bf16[2,512,512]{2,1,0:T(8,128)(2,1)}, u32[]{:S(2)}) copy-start(bf16[2,512,512]{2,1,0:T(8,128)(2,1)} %constant.38.clone.refs_7_) | copy-start | bytes 3145732
  87.9 16.5 %collective-permute-start = (f32[8,128,128]{2,1,0:T(8,128)S(1)}, f32[8,128,128]{2,1,0:T(8,128)S(1)}, u32[]{:S(2)}, u32[]{:S(2)}) collective-permute-start(f32[8,128,128]{2,1,0:T(8,128)S(1)} %get-tuple-element.20), channel_id=1, source_target_pairs={{0,2},{2,0},{1,3},{3,1},{128,130},{130,128},{129,131},{131,129},{1... | collective-permute-start | bytes 1572872 | tf_op jit(solution)/shard_map/ppermute | solution.py:504
  88.0 20.1 %collective-permute-start.2 = (f32[8,128,128]{2,1,0:T(8,128)S(1)}, f32[8,128,128]{2,1,0:T(8,128)S(1)}, u32[]{:S(2)}, u32[]{:S(2)}) collective-permute-start(f32[8,128,128]{2,1,0:T(8,128)S(1)} %get-tuple-element.20), channel_id=1, source_target_pairs={{1,2},{2,1},{128,3},{3,128},{129,130},{130,129},{161,131},{131,161... | collective-permute-start | bytes 1572872 | tf_op jit(solution)/shard_map/ppermute | solution.py:506
  90.2 17.9 %collective-permute-start.1 = (f32[8,128,128]{2,1,0:T(8,128)S(1)}, f32[8,128,128]{2,1,0:T(8,128)S(1)}, u32[]{:S(2)}, u32[]{:S(2)}) collective-permute-start(f32[8,128,128]{2,1,0:T(8,128)S(1)} %get-tuple-element.19.refs_0_), channel_id=1, source_target_pairs={{1,0},{2,3},{128,1},{3,130},{129,128},{130,131},{161,129},{131,163... | collective-permute-start | bytes 1572872 | tf_op jit(solution)/shard_map/ppermute | solution.py:505
  101.9 15.7 %collective-permute-start.10 = (f32[8,128,128]{2,1,0:T(8,128)S(1)}, f32[8,128,128]{2,1,0:T(8,128)S(1)}, u32[]{:S(2)}, u32[]{:S(2)}) collective-permute-start(f32[8,128,128]{2,1,0:T(8,128)S(1)} %get-tuple-element.28), channel_id=1, source_target_pairs={{0,1},{3,2},{1,128},{130,3},{128,129},{131,130},{129,161},{163,131... | collective-permute-start | bytes 1572872 | tf_op jit(solution)/shard_map/ppermute | solution.py:512
  103.2 16.4 %collective-permute-start.11 = (f32[8,128,128]{2,1,0:T(8,128)S(1)}, f32[8,128,128]{2,1,0:T(8,128)S(1)}, u32[]{:S(2)}, u32[]{:S(2)}) collective-permute-start(f32[8,128,128]{2,1,0:T(8,128)S(1)} %get-tuple-element.29), channel_id=1, source_target_pairs={{0,2},{2,0},{1,3},{3,1},{128,130},{130,128},{129,131},{131,129},{1... | collective-permute-start | bytes 1572872 | tf_op jit(solution)/shard_map/ppermute | solution.py:511
  104.3 16.6 %copy-start.1 = (bf16[32,128,384]{2,1,0:T(8,128)(2,1)S(1)}, bf16[32,128,384]{2,1,0:T(8,128)(2,1)}, u32[]{:S(2)}) copy-start(bf16[32,128,384]{2,1,0:T(8,128)(2,1)} %constant.35.clone.inv_ref) | copy-start | bytes 9437188
  104.3 16.6 %collective-permute-start.12 = (f32[8,128,128]{2,1,0:T(8,128)S(1)}, f32[8,128,128]{2,1,0:T(8,128)S(1)}, u32[]{:S(2)}, u32[]{:S(2)}) collective-permute-start(f32[8,128,128]{2,1,0:T(8,128)S(1)} %get-tuple-element.30), channel_id=1, source_target_pairs={{2,1},{1,2},{3,128},{128,3},{130,129},{129,130},{131,161},{161,131... | collective-permute-start | bytes 1572872 | tf_op jit(solution)/shard_map/ppermute | solution.py:513
  113.2 14.1 %collective-permute-start.4 = (f32[8,128,128]{2,1,0:T(8,128)S(1)}, f32[8,128,128]{2,1,0:T(8,128)S(1)}, u32[]{:S(2)}, u32[]{:S(2)}) collective-permute-start(f32[8,128,128]{2,1,0:T(8,128)S(1)} %get-tuple-element.22), channel_id=1, source_target_pairs={{0,1},{3,2},{1,128},{130,3},{128,129},{131,130},{129,161},{163,131... | collective-permute-start | bytes 1572872 | tf_op jit(solution)/shard_map/ppermute | solution.py:512
  114.5 12.8 %collective-permute-start.5 = (f32[8,128,128]{2,1,0:T(8,128)S(1)}, f32[8,128,128]{2,1,0:T(8,128)S(1)}, u32[]{:S(2)}, u32[]{:S(2)}) collective-permute-start(f32[8,128,128]{2,1,0:T(8,128)S(1)} %get-tuple-element.23), channel_id=1, source_target_pairs={{0,2},{2,0},{1,3},{3,1},{128,130},{130,128},{129,131},{131,129},{1... | collective-permute-start | bytes 1572872 | tf_op jit(solution)/shard_map/ppermute | solution.py:511
  117.5 13.0 %collective-permute-start.6 = (f32[8,128,128]{2,1,0:T(8,128)S(1)}, f32[8,128,128]{2,1,0:T(8,128)S(1)}, u32[]{:S(2)}, u32[]{:S(2)}) collective-permute-start(f32[8,128,128]{2,1,0:T(8,128)S(1)} %get-tuple-element.24), channel_id=1, source_target_pairs={{2,1},{1,2},{3,128},{128,3},{130,129},{129,130},{131,161},{161,131... | collective-permute-start | bytes 1572872 | tf_op jit(solution)/shard_map/ppermute | solution.py:513
  120.9 9.6 %copy-start.6 = (bf16[2,64,192]{2,1,0:T(8,128)(2,1)S(1)}, bf16[2,64,192]{2,1,0:T(8,128)(2,1)}, u32[]{:S(2)}) copy-start(bf16[2,64,192]{2,1,0:T(8,128)(2,1)} %constant.36.clone.last_ref) | copy-start | bytes 147460

commit v3 on v2

--- a/solution.py
+++ b/solution.py
@@ -35,6 +35,7 @@
 
 VMEM = pl.BlockSpec(memory_space=pltpu.VMEM)
 SMEM = pl.BlockSpec(memory_space=pltpu.SMEM)
+ANY = pl.BlockSpec(memory_space=pl.ANY)
 
 
 def two(table):
@@ -156,58 +157,69 @@
     return x // 2, row, core, x % 2
 
 
-def decimate_kernel(taps_ref, tail_ref, cur_ref, out_ref, band_ref):
-    plane = pl.program_id(0)
+def decimate_kernel(taps_ref, raw_ref, out_ref, cur_ref, band_ref, stage_ref, in_sems, out_sems):
+    planes = out_ref.shape[2]
     span = TAPS + DEC * BLK
-
-    @pl.when(plane == 0)
-    def _():
-        i = lax.broadcasted_iota(jnp.int32, (TAPS, TAPS), 0)
-        j = lax.broadcasted_iota(jnp.int32, (TAPS, TAPS), 1)
-        mirror = (i + j == TAPS - 1).astype(BF16)
-        rows = jnp.broadcast_to(taps_ref[...].astype(F32), (BLK, TAPS))
-        mirrored = dot(rows.astype(BF16), mirror)
-        wide = jnp.concatenate([mirrored, jnp.zeros((BLK, span - TAPS), F32)], axis=1)
-        wide = pltpu.roll(wide, 1, 1, stride=DEC, stride_axis=0)
-        band_ref[...] = wide.T.astype(BF16)
-
-    tail = jnp.where(plane == 0, jnp.zeros_like(tail_ref[...]), tail_ref[...])
-    blocks = cur_ref.shape[1] // (DEC * BLK)
+    width = raw_ref.shape[1] // planes
+    loads = []
+    for plane in range(planes):
+        part = pl.ds(plane * width, width)
+        loads.append(pltpu.make_async_copy(raw_ref.at[:, part], cur_ref.at[:, part], in_sems.at[plane]))
+        loads[-1].start()
+
+    i = lax.broadcasted_iota(jnp.int32, (TAPS, TAPS), 0)
+    j = lax.broadcasted_iota(jnp.int32, (TAPS, TAPS), 1)
+    mirror = (i + j == TAPS - 1).astype(BF16)
+    rows = jnp.broadcast_to(taps_ref[...].astype(F32), (BLK, TAPS))
+    mirrored = dot(rows.astype(BF16), mirror)
+    wide = jnp.concatenate([mirrored, jnp.zeros((BLK, span - TAPS), F32)], axis=1)
+    wide = pltpu.roll(wide, 1, 1, stride=DEC, stride_axis=0)
+    band_ref[...] = wide.T.astype(BF16)
+
+    blocks = width // (DEC * BLK)
+    group = 16
     band = band_ref[...]
-    group = 16
-    for b0 in range(0, blocks, group):
-        spans = []
-        for b in range(b0, b0 + group):
-            start = b * DEC * BLK
-            if b == 0:
-                spans.append(jnp.concatenate([tail, cur_ref[:, : DEC * BLK]], axis=1))
-            else:
-                spans.append(cur_ref[:, start - TAPS : start + DEC * BLK])
-        result = dot(jnp.concatenate(spans, axis=0), band)
-        for n in range(group):
-            xh, row, core, xl = plane_slot(b0 + n)
-            y = jnp.where(plane % 2 == 0, row, 3 - row)
-            out_ref[xh, y, 0, core, xl] = result[n * 16 : (n + 1) * 16]
+    stores = []
+    for plane in range(planes):
+        loads[plane].wait()
+        for b0 in range(0, blocks, group):
+            spans = []
+            for b in range(b0, b0 + group):
+                start = plane * width + b * DEC * BLK
+                if start == 0:
+                    tail = jnp.zeros((cur_ref.shape[0], TAPS), BF16)
+                    spans.append(jnp.concatenate([tail, cur_ref[:, : DEC * BLK]], axis=1))
+                else:
+                    spans.append(cur_ref[:, start - TAPS : start + DEC * BLK])
+            result = dot(jnp.concatenate(spans, axis=0), band)
+            for n in range(group):
+                xh, row, core, xl = plane_slot(b0 + n)
+                y = row if plane % 2 == 0 else 3 - row
+                stage_ref[plane, xh, y, core, xl] = result[n * 16 : (n + 1) * 16]
+        stores.append(pltpu.make_async_copy(stage_ref.at[plane], out_ref.at[:, :, plane], out_sems.at[plane]))
+        stores[-1].start()
+    for store in stores:
+        store.wait()
 
 
 def decimate(raw, taps):
     channels, length = raw.shape
     planes = 8
-    width = length // planes
     return pl.pallas_call(
         decimate_kernel,
-        grid=(planes,),
-        in_specs=[
-            pl.BlockSpec((1, TAPS), lambda g: (0, 0)),
-            pl.BlockSpec((channels, TAPS), lambda g: (0, jnp.maximum(g * (width // TAPS) - 1, 0))),
-            pl.BlockSpec((channels, width), lambda g: (0, g)),
+        in_specs=[VMEM, ANY],
+        out_specs=ANY,
+        out_shape=jax.ShapeDtypeStruct((2, 4, planes, 2, 2, channels, BLK), F32),
+        scratch_shapes=[
+            pltpu.VMEM(raw.shape, BF16),
+            pltpu.VMEM((TAPS + DEC * BLK, BLK), BF16),
+            pltpu.VMEM((planes, 2, 4, 2, 2, channels, BLK), F32),
+            pltpu.SemaphoreType.DMA((planes,)),
+            pltpu.SemaphoreType.DMA((planes,)),
         ],
-        out_specs=pl.BlockSpec((2, 4, 1, 2, 2, channels, BLK), lambda g: (0, 0, g, 0, 0, 0, 0)),
-        out_shape=jax.ShapeDtypeStruct((2, 4, planes, 2, 2, channels, BLK), F32),
-        scratch_shapes=[pltpu.VMEM((TAPS + DEC * BLK, BLK), BF16)],
-        compiler_params=params(12),
+        compiler_params=params(60),
         name="decimate",
-    )(taps.reshape(1, TAPS), raw, raw)
+    )(taps.reshape(1, TAPS), raw)
 
 
 def unplane_kernel(in_ref, out_ref):

time: 196 us -> 193 us (0.985)
  local copies, waits for them, and re-layouts: 4.62 us -> 1.78 us
    unnamed x20 -> x16, local copies, waits for them, and re-layouts: 4.62 us -> 1.78 us
where the time goes in v3:
time: 193 us
  blocking collectives  59.9 us (31%)
  waiting for transfers between devices  58.3 us (30%)
  starting transfers between devices  41.8 us (22%)
  Pallas kernels  30.4 us (16%)
    all_to_all x1, blocking collectives, body(): lax.all_to_all(filtered.reshape(256, 16, BLK), AXES, 0, 0, tiled=True)  59.9 us
    all_to_all x1, waiting for transfers between devices, body(): blocks = lax.all_to_all(blocks, AXES, 0, 0, tiled=True)  44.8 us
    all_to_all x1, starting transfers between devices, body(): blocks = lax.all_to_all(blocks, AXES, 0, 0, tiled=True)  16.7 us
    pallas_call x2, Pallas kernels, time_filter(): pl.pallas_call(functools.partial(time_kernel, chunk == 0), grid=(steps,),...  9.98 us
    ppermute x2, starting transfers between devices, body(): from_cross = lax.ppermute(other, AXES, cross)  5.81 us
    ppermute x2, starting transfers between devices, body(): back_cross = lax.ppermute(far, AXES, flipped(cross))  5.55 us
    pallas_call x1, Pallas kernels, decimate(): pl.pallas_call(decimate_kernel, in_specs=[VMEM, ANY], out_specs=ANY, out_...  5.11 us
    ppermute x2, waiting for transfers between devices, body(): back_cross = lax.ppermute(far, AXES, flipped(cross))  4.79 us
  transfers between devices with their start and end apart: 14, of which 5 were waited for; matrix products, arithmetic and copies ran while one was open for 0% of the time, Pallas kernels for 11%

profile of v3, /device:TPU:1, one launch (start us, length us, event | category | flops | bytes accessed | tf_op | source)
XLA Modules:
  0.0 192.6 jit_solution(15055342391915193643)
XLA Ops:
  0.0 5.1 %decimate.1 = f32[2,4,8,2,2,16,128]{6,5,4,3,2,1,0:T(8,128)} custom-call(bf16[1,128]{1,0:T(2,128)(2,1)} %bitcast.10, bf16[16,131072]{1,0:T(8,128)(2,1)} %raw_ref.1), custom_call_target="tpu_custom_call" | custom-call | tf_op jit(solution)/shard_map/decimate/pallas_call | solution.py:208
  5.1 16.7 %all-to-all-start = ((f32[256,16,128]{2,1,0:T(8,128)}), f32[256,16,128]{2,1,0:T(8,128)}, u32[]{:S(2)}, u32[]{:S(2)}) async-start(f32[256,16,128]{2,1,0:T(8,128)} %bitcast.9), calls=%async_computation | async-start | bytes 4194304 | tf_op jit(solution)/shard_map/all_to_all | solution.py:510
  21.9 1.7 copy-done.4
  23.7 2.9 %gains.1.refs_4_ = f32[2,16,64,128]{3,2,1,0:T(8,128)} custom-call(s32[2]{0:T(128)S(1)} %pad_add_fusion.where_ref, f32[8]{0:T(128)S(1)} %copy-done.7, s32[4096,128]{1,0:T(8,128)S(1)} %copy-done.4), custom_call_target="tpu_custom_call" | custom-call | tf_op jit(solution)/shard_map/gains/pallas_call | solution.py:409
  28.0 44.8 %all-to-all-done = f32[256,16,128]{2,1,0:T(8,128)} async-done(((f32[256,16,128]{2,1,0:T(8,128)}), f32[256,16,128]{2,1,0:T(8,128)}, u32[]{:S(2)}, u32[]{:S(2)}) %all-to-all-start) | async-done | bytes 2097184 | tf_op jit(solution)/shard_map/all_to_all | solution.py:510
  72.8 4.1 %forward_space.1 = (f32[8,128,128]{2,1,0:T(8,128)S(1)}, f32[8,128,128]{2,1,0:T(8,128)S(1)}, f32[2048,128]{1,0:T(8,128)S(1)}) custom-call(s32[2]{0:T(128)S(1)} %pad_add_fusion.where_ref, f32[4096,128]{1,0:T(8,128)} %bitcast.4.x_ref, bf16[2,64,192]{2,1,0:T(8,128)(2,1)S(1)} %copy-done.6, bf16[32,128,384]{2,1,0:T(8,128)(2,1)S(1)} %copy-done.1), custom_call_target="tpu_custom_call" | custom-call | tf_op jit(solution)/shard_map/forward_space/pallas_call | solution.py:283
  78.1 1.9 collective-permute-start.8
  80.0 3.6 %collective-permute-start.9 = (f32[8,128,128]{2,1,0:T(8,128)S(1)}, f32[8,128,128]{2,1,0:T(8,128)S(1)}, u32[]{:S(2)}, u32[]{:S(2)}) collective-permute-start(f32[8,128,128]{2,1,0:T(8,128)S(1)} %get-tuple-element.26), channel_id=1, source_target_pairs={{1,2},{2,1},{128,3},{3,128},{129,130},{130,129},{161,131},{131,161... | collective-permute-start | bytes 1572872 | tf_op jit(solution)/shard_map/ppermute | solution.py:518
  83.6 1.6 forward_more.1
  85.3 2.2 %collective-permute-start.2 = (f32[8,128,128]{2,1,0:T(8,128)S(1)}, f32[8,128,128]{2,1,0:T(8,128)S(1)}, u32[]{:S(2)}, u32[]{:S(2)}) collective-permute-start(f32[8,128,128]{2,1,0:T(8,128)S(1)} %get-tuple-element.20), channel_id=1, source_target_pairs={{1,2},{2,1},{128,3},{3,128},{129,130},{130,129},{161,131},{131,161... | collective-permute-start | bytes 1572872 | tf_op jit(solution)/shard_map/ppermute | solution.py:518
  87.5 2.1 %collective-permute-start.1 = (f32[8,128,128]{2,1,0:T(8,128)S(1)}, f32[8,128,128]{2,1,0:T(8,128)S(1)}, u32[]{:S(2)}, u32[]{:S(2)}) collective-permute-start(f32[8,128,128]{2,1,0:T(8,128)S(1)} %get-tuple-element.19.refs_0_), channel_id=1, source_target_pairs={{1,0},{2,3},{128,1},{3,130},{129,128},{130,131},{161,129},{131,163... | collective-permute-start | bytes 1572872 | tf_op jit(solution)/shard_map/ppermute | solution.py:517
  89.7 4.4 %collective-permute-done.9.refs_3_ = f32[8,128,128]{2,1,0:T(8,128)S(1)} collective-permute-done((f32[8,128,128]{2,1,0:T(8,128)S(1)}, f32[8,128,128]{2,1,0:T(8,128)S(1)}, u32[]{:S(2)}, u32[]{:S(2)}) %collective-permute-start.9) | collective-permute-done | bytes 524320 | tf_op jit(solution)/shard_map/ppermute | solution.py:518
  94.1 5.0 %time_filter.3 = (f32[8,128,128]{2,1,0:T(8,128)S(1)}, f32[8,128,128]{2,1,0:T(8,128)S(1)}, f32[8,128,128]{2,1,0:T(8,128)S(1)}, f32[8,128,128]{2,1,0:T(8,128)S(1)}) custom-call(s32[2]{0:T(128)S(1)} %pad_add_fusion.where_ref, f32[8,128,128]{2,1,0:T(8,128)S(1)} %get-tuple-element.25.refs_0_, f32[8,128,128]{2,1,0:T(8,128)S(1)} %collective-permute-done.7.refs_1_, ...), custom_call_target="tpu_custom_call" | custom-call | tf_op jit(solution)/shard_map/time_filter/pallas_call | solution.py:487
  101.8 3.6 %collective-permute-start.12 = (f32[8,128,128]{2,1,0:T(8,128)S(1)}, f32[8,128,128]{2,1,0:T(8,128)S(1)}, u32[]{:S(2)}, u32[]{:S(2)}) collective-permute-start(f32[8,128,128]{2,1,0:T(8,128)S(1)} %get-tuple-element.30), channel_id=1, source_target_pairs={{2,1},{1,2},{3,128},{128,3},{130,129},{129,130},{131,161},{161,131... | collective-permute-start | bytes 1572872 | tf_op jit(solution)/shard_map/ppermute | solution.py:525
  105.4 5.0 %time_filter.2 = (f32[8,128,128]{2,1,0:T(8,128)S(1)}, f32[8,128,128]{2,1,0:T(8,128)S(1)}, f32[8,128,128]{2,1,0:T(8,128)S(1)}, f32[8,128,128]{2,1,0:T(8,128)S(1)}) custom-call(s32[2]{0:T(128)S(1)} %pad_add_fusion.where_ref, f32[8,128,128]{2,1,0:T(8,128)S(1)} %get-tuple-element.19.refs_0_, f32[8,128,128]{2,1,0:T(8,128)S(1)} %collective-permute-done.refs_1_, ...), custom_call_target="tpu_custom_call" | custom-call | tf_op jit(solution)/shard_map/time_filter/pallas_call | solution.py:487
  111.7 3.2 %collective-permute-start.5 = (f32[8,128,128]{2,1,0:T(8,128)S(1)}, f32[8,128,128]{2,1,0:T(8,128)S(1)}, u32[]{:S(2)}, u32[]{:S(2)}) collective-permute-start(f32[8,128,128]{2,1,0:T(8,128)S(1)} %get-tuple-element.23), channel_id=1, source_target_pairs={{0,2},{2,0},{1,3},{3,1},{128,130},{130,128},{129,131},{131,129},{1... | collective-permute-start | bytes 1572872 | tf_op jit(solution)/shard_map/ppermute | solution.py:523
  114.9 2.0 %collective-permute-start.6 = (f32[8,128,128]{2,1,0:T(8,128)S(1)}, f32[8,128,128]{2,1,0:T(8,128)S(1)}, u32[]{:S(2)}, u32[]{:S(2)}) collective-permute-start(f32[8,128,128]{2,1,0:T(8,128)S(1)} %get-tuple-element.24), channel_id=1, source_target_pairs={{2,1},{1,2},{3,128},{128,3},{130,129},{129,130},{131,161},{161,131... | collective-permute-start | bytes 1572872 | tf_op jit(solution)/shard_map/ppermute | solution.py:525
  116.9 1.6 collective-permute-done.12.cross_ref
  118.5 1.9 inverse_more.1.rest_0_
  120.3 4.3 %collective-permute-done.4.halo_ref = f32[8,128,128]{2,1,0:T(8,128)S(1)} collective-permute-done((f32[8,128,128]{2,1,0:T(8,128)S(1)}, f32[8,128,128]{2,1,0:T(8,128)S(1)}, u32[]{:S(2)}, u32[]{:S(2)}) %collective-permute-start.4) | collective-permute-done | bytes 524320 | tf_op jit(solution)/shard_map/ppermute | solution.py:524
  124.6 3.2 %collective-permute-done.6.cross_ref = f32[8,128,128]{2,1,0:T(8,128)S(1)} collective-permute-done((f32[8,128,128]{2,1,0:T(8,128)S(1)}, f32[8,128,128]{2,1,0:T(8,128)S(1)}, u32[]{:S(2)}, u32[]{:S(2)}) %collective-permute-start.6) | collective-permute-done | bytes 524320 | tf_op jit(solution)/shard_map/ppermute | solution.py:525
  127.8 3.4 %inverse_space.1 = f32[4096,128]{1,0:T(8,128)S(1)} custom-call(s32[2]{0:T(128)S(1)} %pad_add_fusion.where_ref, f32[8,128,128]{2,1,0:T(8,128)S(1)} %get-tuple-element.21.own_ref, f32[8,128,128]{2,1,0:T(8,128)S(1)} %collective-permute-done.4.halo_ref, f32[8,128,128]{2,1,0:T(8,128)S(1)} %collective-permute-done.5.part_ref, ...), custom_call_target="tpu_custom_call" | custom-call | tf_op jit(solution)/shard_map/inverse_space/pallas_call | solution.py:354
  131.2 59.9 %all_to_all.10 = f32[256,16,128]{2,1,0:T(8,128)S(1)} all-to-all(f32[256,16,128]{2,1,0:T(8,128)S(1)} %bitcast.8), channel_id=1, replica_groups=mesh['chan'=128,'tile'=2] {'chan','tile'}, dimensions={0} | all-to-all | bytes 4194304 | tf_op jit(solution)/shard_map/all_to_all | solution.py:529
  191.1 1.5 unplane.1
  (31 shorter events, 6.8 us)
Async XLA Ops:
  5.1 16.8 %copy-start.7 = (f32[8]{0:T(128)S(1)}, f32[8]{0:T(128)}, u32[]{:S(2)}) copy-start(f32[8]{0:T(128)} %gain_ref.1) | copy-start | bytes 100
  5.1 67.7 %copy-start.6 = (bf16[2,64,192]{2,1,0:T(8,128)(2,1)S(1)}, bf16[2,64,192]{2,1,0:T(8,128)(2,1)}, u32[]{:S(2)}) copy-start(bf16[2,64,192]{2,1,0:T(8,128)(2,1)} %constant.33.clone.first_ref) | copy-start | bytes 147460
  5.1 67.6 %all-to-all-start = ((f32[256,16,128]{2,1,0:T(8,128)}), f32[256,16,128]{2,1,0:T(8,128)}, u32[]{:S(2)}, u32[]{:S(2)}) async-start(f32[256,16,128]{2,1,0:T(8,128)} %bitcast.9), calls=%async_computation | async-start | bytes 4194304 | tf_op jit(solution)/shard_map/all_to_all | solution.py:510
  21.8 51.0 %copy-start.1 = (bf16[32,128,384]{2,1,0:T(8,128)(2,1)S(1)}, bf16[32,128,384]{2,1,0:T(8,128)(2,1)}, u32[]{:S(2)}) copy-start(bf16[32,128,384]{2,1,0:T(8,128)(2,1)} %constant.34.clone.second_ref) | copy-start | bytes 9437188
  21.9 1.7 copy-start.4
  26.6 58.7 %collective-permute-start.3 = (f32[2,16,64,128]{3,2,1,0:T(8,128)}, f32[2,16,64,128]{3,2,1,0:T(8,128)}, u32[]{:S(2)}, u32[]{:S(2)}) collective-permute-start(f32[2,16,64,128]{3,2,1,0:T(8,128)} %gains.1.refs_4_), channel_id=1, source_target_pairs={{0,1},{1,0},{2,3},{3,2},{4,5},{5,4},{6,7},{7,6},{8,9},{9,8},{10,11... | collective-permute-start | bytes 3145736 | tf_op jit(solution)/shard_map/ppermute | solution.py:505
  76.9 10.7 %collective-permute-start.7 = (f32[8,128,128]{2,1,0:T(8,128)S(1)}, f32[8,128,128]{2,1,0:T(8,128)S(1)}, u32[]{:S(2)}, u32[]{:S(2)}) collective-permute-start(f32[8,128,128]{2,1,0:T(8,128)S(1)} %get-tuple-element.26), channel_id=1, source_target_pairs={{0,2},{2,0},{1,3},{3,1},{128,130},{130,128},{129,131},{131,129},{1... | collective-permute-start | bytes 1572872 | tf_op jit(solution)/shard_map/ppermute | solution.py:516
  78.1 11.6 %collective-permute-start.8 = (f32[8,128,128]{2,1,0:T(8,128)S(1)}, f32[8,128,128]{2,1,0:T(8,128)S(1)}, u32[]{:S(2)}, u32[]{:S(2)}) collective-permute-start(f32[8,128,128]{2,1,0:T(8,128)S(1)} %get-tuple-element.25.refs_0_), channel_id=1, source_target_pairs={{1,0},{2,3},{128,1},{3,130},{129,128},{130,131},{161,129},{131,163... | collective-permute-start | bytes 1572872 | tf_op jit(solution)/shard_map/ppermute | solution.py:517
  80.0 14.1 %collective-permute-start.9 = (f32[8,128,128]{2,1,0:T(8,128)S(1)}, f32[8,128,128]{2,1,0:T(8,128)S(1)}, u32[]{:S(2)}, u32[]{:S(2)}) collective-permute-start(f32[8,128,128]{2,1,0:T(8,128)S(1)} %get-tuple-element.26), channel_id=1, source_target_pairs={{1,2},{2,1},{128,3},{3,128},{129,130},{130,129},{161,131},{131,161... | collective-permute-start | bytes 1572872 | tf_op jit(solution)/shard_map/ppermute | solution.py:518
  83.6 10.5 %copy-start.2 = (bf16[2,512,512]{2,1,0:T(8,128)(2,1)S(1)}, bf16[2,512,512]{2,1,0:T(8,128)(2,1)}, u32[]{:S(2)}) copy-start(bf16[2,512,512]{2,1,0:T(8,128)(2,1)} %constant.37.clone.refs_6_) | copy-start | bytes 3145732
  83.6 10.5 %copy-start.3 = (bf16[2,512,512]{2,1,0:T(8,128)(2,1)S(1)}, bf16[2,512,512]{2,1,0:T(8,128)(2,1)}, u32[]{:S(2)}) copy-start(bf16[2,512,512]{2,1,0:T(8,128)(2,1)} %constant.38.clone.refs_7_) | copy-start | bytes 3145732
  85.2 16.6 %collective-permute-start = (f32[8,128,128]{2,1,0:T(8,128)S(1)}, f32[8,128,128]{2,1,0:T(8,128)S(1)}, u32[]{:S(2)}, u32[]{:S(2)}) collective-permute-start(f32[8,128,128]{2,1,0:T(8,128)S(1)} %get-tuple-element.20), channel_id=1, source_target_pairs={{0,2},{2,0},{1,3},{3,1},{128,130},{130,128},{129,131},{131,129},{1... | collective-permute-start | bytes 1572872 | tf_op jit(solution)/shard_map/ppermute | solution.py:516
  85.3 20.0 %collective-permute-start.2 = (f32[8,128,128]{2,1,0:T(8,128)S(1)}, f32[8,128,128]{2,1,0:T(8,128)S(1)}, u32[]{:S(2)}, u32[]{:S(2)}) collective-permute-start(f32[8,128,128]{2,1,0:T(8,128)S(1)} %get-tuple-element.20), channel_id=1, source_target_pairs={{1,2},{2,1},{128,3},{3,128},{129,130},{130,129},{161,131},{131,161... | collective-permute-start | bytes 1572872 | tf_op jit(solution)/shard_map/ppermute | solution.py:518
  87.5 17.8 %collective-permute-start.1 = (f32[8,128,128]{2,1,0:T(8,128)S(1)}, f32[8,128,128]{2,1,0:T(8,128)S(1)}, u32[]{:S(2)}, u32[]{:S(2)}) collective-permute-start(f32[8,128,128]{2,1,0:T(8,128)S(1)} %get-tuple-element.19.refs_0_), channel_id=1, source_target_pairs={{1,0},{2,3},{128,1},{3,130},{129,128},{130,131},{161,129},{131,163... | collective-permute-start | bytes 1572872 | tf_op jit(solution)/shard_map/ppermute | solution.py:517
  99.1 15.7 %collective-permute-start.10 = (f32[8,128,128]{2,1,0:T(8,128)S(1)}, f32[8,128,128]{2,1,0:T(8,128)S(1)}, u32[]{:S(2)}, u32[]{:S(2)}) collective-permute-start(f32[8,128,128]{2,1,0:T(8,128)S(1)} %get-tuple-element.28), channel_id=1, source_target_pairs={{0,1},{3,2},{1,128},{130,3},{128,129},{131,130},{129,161},{163,131... | collective-permute-start | bytes 1572872 | tf_op jit(solution)/shard_map/ppermute | solution.py:524
  100.4 16.4 %collective-permute-start.11 = (f32[8,128,128]{2,1,0:T(8,128)S(1)}, f32[8,128,128]{2,1,0:T(8,128)S(1)}, u32[]{:S(2)}, u32[]{:S(2)}) collective-permute-start(f32[8,128,128]{2,1,0:T(8,128)S(1)} %get-tuple-element.29), channel_id=1, source_target_pairs={{0,2},{2,0},{1,3},{3,1},{128,130},{130,128},{129,131},{131,129},{1... | collective-permute-start | bytes 1572872 | tf_op jit(solution)/shard_map/ppermute | solution.py:523
  101.8 16.7 %copy-start = (bf16[32,128,384]{2,1,0:T(8,128)(2,1)S(1)}, bf16[32,128,384]{2,1,0:T(8,128)(2,1)}, u32[]{:S(2)}) copy-start(bf16[32,128,384]{2,1,0:T(8,128)(2,1)} %constant.35.clone.inv_ref) | copy-start | bytes 9437188
  101.8 16.7 %collective-permute-start.12 = (f32[8,128,128]{2,1,0:T(8,128)S(1)}, f32[8,128,128]{2,1,0:T(8,128)S(1)}, u32[]{:S(2)}, u32[]{:S(2)}) collective-permute-start(f32[8,128,128]{2,1,0:T(8,128)S(1)} %get-tuple-element.30), channel_id=1, source_target_pairs={{2,1},{1,2},{3,128},{128,3},{130,129},{129,130},{131,161},{161,131... | collective-permute-start | bytes 1572872 | tf_op jit(solution)/shard_map/ppermute | solution.py:525
  110.4 14.3 %collective-permute-start.4 = (f32[8,128,128]{2,1,0:T(8,128)S(1)}, f32[8,128,128]{2,1,0:T(8,128)S(1)}, u32[]{:S(2)}, u32[]{:S(2)}) collective-permute-start(f32[8,128,128]{2,1,0:T(8,128)S(1)} %get-tuple-element.22), channel_id=1, source_target_pairs={{0,1},{3,2},{1,128},{130,3},{128,129},{131,130},{129,161},{163,131... | collective-permute-start | bytes 1572872 | tf_op jit(solution)/shard_map/ppermute | solution.py:524
  111.7 13.0 %collective-permute-start.5 = (f32[8,128,128]{2,1,0:T(8,128)S(1)}, f32[8,128,128]{2,1,0:T(8,128)S(1)}, u32[]{:S(2)}, u32[]{:S(2)}) collective-permute-start(f32[8,128,128]{2,1,0:T(8,128)S(1)} %get-tuple-element.23), channel_id=1, source_target_pairs={{0,2},{2,0},{1,3},{3,1},{128,130},{130,128},{129,131},{131,129},{1... | collective-permute-start | bytes 1572872 | tf_op jit(solution)/shard_map/ppermute | solution.py:523
  114.9 13.0 %collective-permute-start.6 = (f32[8,128,128]{2,1,0:T(8,128)S(1)}, f32[8,128,128]{2,1,0:T(8,128)S(1)}, u32[]{:S(2)}, u32[]{:S(2)}) collective-permute-start(f32[8,128,128]{2,1,0:T(8,128)S(1)} %get-tuple-element.24), channel_id=1, source_target_pairs={{2,1},{1,2},{3,128},{128,3},{130,129},{129,130},{131,161},{161,131... | collective-permute-start | bytes 1572872 | tf_op jit(solution)/shard_map/ppermute | solution.py:525
  118.4 9.4 %copy-start.5 = (bf16[2,64,192]{2,1,0:T(8,128)(2,1)S(1)}, bf16[2,64,192]{2,1,0:T(8,128)(2,1)}, u32[]{:S(2)}) copy-start(bf16[2,64,192]{2,1,0:T(8,128)(2,1)} %constant.36.clone.last_ref) | copy-start | bytes 147460

commit v4 on v3

--- a/solution.py
+++ b/solution.py
@@ -27,6 +27,8 @@
 F32 = jnp.float32
 BF16 = jnp.bfloat16
 MIB = 1024 * 1024
+WAVE = jax.ShapeDtypeStruct((WIDTH, BLK, BLK), F32)
+MIDDLE = jax.ShapeDtypeStruct((PART, BLK, BLK), F32)
 
 
 def params(mib):
@@ -50,24 +52,7 @@
     return np.concatenate([hi, hi, lo], axis=-1)
 
 
-def slot_order(core):
-    width = HALF // CHUNKS
-    order = []
-    for g in range(CHUNKS):
-        order += [(i + HALF * core) % SLOTS for i in range(g * width, (g + 1) * width)]
-        order += [(i + HALF * (1 - core)) % SLOTS for i in range(g * width, (g + 1) * width)]
-    return np.array(order)
-
-
 def spatial_tables():
-    c1 = np.arange(ROOT)
-    slot = np.arange(SLOTS)[:, None]
-    angle = 2 * np.pi / ROOT * (slot * c1 % ROOT)
-    re, im = np.cos(angle), -np.sin(angle)
-    im[0] = (-1.0) ** c1
-    first = np.stack([re, im], axis=0)
-    first = np.stack([first[:, slot_order(core)] for core in (0, 1)])
-    first = first.reshape(2, 2, CHUNKS, SLOTS // CHUNKS, ROOT).swapaxes(1, 2).reshape(2, ROOT, ROOT)
     c0 = np.arange(ROOT)[None, :]
     k2 = np.arange(ROOT)[:, None]
     second = np.zeros((SLOTS, 2, ROOT, 2, ROOT))
@@ -78,8 +63,8 @@
         if s:
             second[s, 0, :, 0], second[s, 0, :, 1] = co, si
             second[s, 1, :, 0], second[s, 1, :, 1] = -si, co
-            inverse[s, 0, :, 0], inverse[s, 0, :, 1] = co.T, -si.T
-            inverse[s, 1, :, 0], inverse[s, 1, :, 1] = si.T, co.T
+            inverse[s, 0, :, 0], inverse[s, 0, :, 1] = co.T / 2, -si.T / 2
+            inverse[s, 1, :, 0], inverse[s, 1, :, 1] = si.T / 2, co.T / 2
             continue
         n = ROOT // 2
         second[0, 0, :n, 0], second[0, 1, :n, 0] = co[:n], -si[:n]
@@ -93,8 +78,7 @@
         inverse[0, 1, :, 0, n:], inverse[0, 1, :, 1, n:] = co.T, -si.T
     second = second.reshape(SLOTS, BLK, BLK)
     inverse = inverse.reshape(SLOTS, BLK, BLK) / K
-    last = np.swapaxes(first, 1, 2)
-    return (left_operand(first), left_operand(second), left_operand(inverse), left_operand(last))
+    return left_operand(second), left_operand(inverse)
 
 
 def temporal_tables():
@@ -245,6 +229,51 @@
     )(blocks)
 
 
+def turn(value, k, n):
+    re, im = value
+    if 8 * abs(k) == n:
+        c = np.float32(np.sqrt(0.5))
+        return ((re - im) * c, (re + im) * c) if k > 0 else ((re + im) * c, (im - re) * c)
+    c, s = np.float32(np.cos(2 * np.pi * k / n)), np.float32(np.sin(2 * np.pi * k / n))
+    return re * c - im * s, re * s + im * c
+
+
+def real_forward(load, n, start, step):
+    if n == 2:
+        a, b = load(start), load(start + step)
+        return [a + b, a - b]
+    even = real_forward(load, n // 2, start, 2 * step)
+    odd = real_forward(load, n // 2, start + step, 2 * step)
+    half, quarter = n // 2, n // 4
+    out = [None] * (half + 1)
+    out[0], out[half] = even[0] + odd[0], even[0] - odd[0]
+    out[quarter] = (even[quarter], -odd[quarter])
+    for k in range(1, quarter):
+        re, im = turn(odd[k], -k, n)
+        er, ei = even[k]
+        out[k] = (er + re, ei + im)
+        out[half - k] = (er - re, im - ei)
+    return out
+
+
+def real_inverse(bins):
+    half = len(bins) - 1
+    if half == 1:
+        return [bins[0] + bins[1], bins[0] - bins[1]]
+    n, quarter = 2 * half, half // 2
+    even, odd = [bins[0] + bins[half]], [bins[0] - bins[half]]
+    for k in range(1, quarter):
+        (ar, ai), (br, bi) = bins[k], bins[half - k]
+        even.append((ar + br, ai - bi))
+        odd.append(turn((ar - br, ai + bi), k, n))
+    re, im = bins[quarter]
+    even.append(re + re)
+    odd.append(-(im + im))
+    out = [None] * n
+    out[0::2], out[1::2] = real_inverse(even), real_inverse(odd)
+    return out
+
+
 def real_slot(core, chunk, i):
     s = chunk * WIDTH + i % WIDTH + (HALF if i >= WIDTH else 0)
     return lax.rem(s + HALF * core, SLOTS)
@@ -252,43 +281,38 @@
 
 def second_stage(core, chunk, mid_ref, second_ref, own_ref, other_ref):
     for i in range(PART):
-        re = mid_ref[pl.ds(i, ROOT, stride=2 * PART), :]
-        im = mid_ref[pl.ds(PART + i, ROOT, stride=2 * PART), :]
-        table = second_ref[real_slot(core, chunk, i)]
-        wave = dot(table, stacked(jnp.concatenate([re, im], axis=0)))
+        s = real_slot(core, chunk, i)
+        wave = dot(second_ref[s], stacked(mid_ref[s]))
         if i < WIDTH:
             own_ref[i] = wave
         else:
             other_ref[i - WIDTH] = wave
 
 
-def forward_kernel(where_ref, x_ref, first_ref, second_ref, own_ref, other_ref, *rest):
-    later, mid_ref = rest[:-1], rest[-1]
-    core = where_ref[0]
-    first = first_ref[core]
-    rows = 2 * PART
-    for c0 in range(0, ROOT, 2):
-        one = stacked(x_ref[pl.ds(c0, ROOT, stride=ROOT), :])
-        two_ = stacked(x_ref[pl.ds(c0 + 1, ROOT, stride=ROOT), :])
-        y = dot(first, jnp.concatenate([one, two_], axis=1))
-        for g, ref in enumerate((mid_ref,) + later):
-            ref[c0 * rows : (c0 + 1) * rows, :] = y[g * rows : (g + 1) * rows, :BLK]
-            ref[(c0 + 1) * rows : (c0 + 2) * rows, :] = y[g * rows : (g + 1) * rows, BLK:]
-    second_stage(core, 0, mid_ref, second_ref, own_ref, other_ref)
-
-
-def forward_space(where, x, first, second):
-    wave = jax.ShapeDtypeStruct((WIDTH, BLK, BLK), F32)
-    middle = jax.ShapeDtypeStruct((K // CHUNKS, BLK), F32)
+def forward_kernel(where_ref, x_ref, second_ref, own_ref, other_ref, mid_ref):
+    def tile(t, carry):
+        rows = pl.ds(pl.multiple_of(t * 8, 8), 8)
+        rows_im = pl.ds(pl.multiple_of(ROOT + t * 8, 8), 8)
+        bins = real_forward(lambda c1: x_ref[c1, rows, :], ROOT, 0, 1)
+        mid_ref[0, rows, :] = bins[0]
+        mid_ref[0, rows_im, :] = bins[SLOTS]
+        for s in range(1, SLOTS):
+            mid_ref[s, rows, :], mid_ref[s, rows_im, :] = bins[s]
+        return carry
+
+    lax.fori_loop(0, ROOT // 8, tile, 0)
+    second_stage(where_ref[0], 0, mid_ref, second_ref, own_ref, other_ref)
+
+
+def forward_space(where, x, second):
     return pl.pallas_call(
         forward_kernel,
-        in_specs=[SMEM] + [VMEM] * 3,
-        out_specs=[VMEM] * (1 + CHUNKS),
-        out_shape=[wave] * 2 + [middle] * (CHUNKS - 1),
-        scratch_shapes=[pltpu.VMEM((K // CHUNKS, BLK), F32)],
+        in_specs=[SMEM] + [VMEM] * 2,
+        out_specs=[VMEM] * 3,
+        out_shape=[WAVE, WAVE, jax.ShapeDtypeStruct((SLOTS, BLK, BLK), F32)],
         compiler_params=params(14),
         name="forward_space",
-    )(where, x, first, second)
+    )(where, x.reshape(ROOT, ROOT, BLK), second)
 
 
 def forward_more_kernel(chunk, where_ref, mid_ref, second_ref, own_ref, other_ref):
@@ -296,12 +320,11 @@
 
 
 def forward_more(chunk, where, middle, second):
-    wave = jax.ShapeDtypeStruct((WIDTH, BLK, BLK), F32)
     return pl.pallas_call(
         functools.partial(forward_more_kernel, chunk),
         in_specs=[SMEM] + [VMEM] * 2,
         out_specs=[VMEM] * 2,
-        out_shape=[wave] * 2,
+        out_shape=[WAVE, WAVE],
         compiler_params=params(12),
         name="forward_more",
     )(where, middle, second)
@@ -313,9 +336,7 @@
             z = own_ref[i] + halo_ref[i]
         else:
             z = part_ref[i - WIDTH] + cross_ref[i - WIDTH]
-        u = dot(inv_ref[real_slot(core, chunk, i)], stacked(z))
-        mid_ref[pl.ds(i, ROOT, stride=2 * PART), :] = u[:ROOT]
-        mid_ref[pl.ds(PART + i, ROOT, stride=2 * PART), :] = u[ROOT:]
+        mid_ref[i] = dot(inv_ref[real_slot(core, chunk, i)], stacked(z))
 
 
 def inverse_more_kernel(chunk, where_ref, own_ref, halo_ref, part_ref, cross_ref, inv_ref, mid_ref):
@@ -327,39 +348,46 @@
         functools.partial(inverse_more_kernel, chunk),
         in_specs=[SMEM] + [VMEM] * 5,
         out_specs=VMEM,
-        out_shape=jax.ShapeDtypeStruct((K // CHUNKS, BLK), F32),
+        out_shape=MIDDLE,
         compiler_params=params(12),
         name="inverse_more",
     )(where, *waves, inv)
 
 
-def inverse_kernel(where_ref, own_ref, halo_ref, part_ref, cross_ref, inv_ref, last_ref, *rest):
+def inverse_kernel(where_ref, own_ref, halo_ref, part_ref, cross_ref, inv_ref, *rest):
     earlier, out_ref, mid_ref = rest[:-2], rest[-2], rest[-1]
     core = where_ref[0]
     inverse_stage(core, CHUNKS - 1, own_ref, halo_ref, part_ref, cross_ref, inv_ref, mid_ref)
-    last = last_ref[core]
-    rows = 2 * PART
     refs = earlier + (mid_ref,)
 
-    def column(c0):
-        return stacked(jnp.concatenate([ref[c0 * rows : (c0 + 1) * rows, :] for ref in refs], axis=0))
-
-    for c0 in range(0, ROOT, 2):
-        y = dot(last, jnp.concatenate([column(c0), column(c0 + 1)], axis=1))
-        out_ref[pl.ds(c0, ROOT, stride=ROOT), :] = y[:, :BLK]
-        out_ref[pl.ds(c0 + 1, ROOT, stride=ROOT), :] = y[:, BLK:]
-
-
-def inverse_space(where, waves, earlier, inv, last):
+    def tile(t, carry):
+        rows = pl.ds(pl.multiple_of(t * 8, 8), 8)
+        rows_im = pl.ds(pl.multiple_of(ROOT + t * 8, 8), 8)
+
+        def both(s):
+            ref = refs[s % HALF // WIDTH]
+            place = s % WIDTH + WIDTH * lax.rem(core + s // HALF, 2)
+            return ref[place, rows, :], ref[place, rows_im, :]
+
+        low, high = both(0)
+        values = real_inverse([low] + [both(s) for s in range(1, SLOTS)] + [high])
+        for c1 in range(ROOT):
+            out_ref[c1, rows, :] = values[c1]
+        return carry
+
+    lax.fori_loop(0, ROOT // 8, tile, 0)
+
+
+def inverse_space(where, waves, earlier, inv):
     return pl.pallas_call(
         inverse_kernel,
-        in_specs=[SMEM] + [VMEM] * (6 + len(earlier)),
+        in_specs=[SMEM] + [VMEM] * (5 + len(earlier)),
         out_specs=VMEM,
-        out_shape=jax.ShapeDtypeStruct((K, BLK), F32),
-        scratch_shapes=[pltpu.VMEM((K // CHUNKS, BLK), F32)],
+        out_shape=jax.ShapeDtypeStruct((ROOT, ROOT, BLK), F32),
+        scratch_shapes=[pltpu.VMEM(MIDDLE.shape, F32)],
         compiler_params=params(14),
         name="inverse_space",
-    )(where, *waves, inv, last, *earlier)
+    )(where, *waves, inv, *earlier)
 
 
 def gains_kernel(where_ref, gain_ref, band_ref, out_ref):
@@ -497,7 +525,7 @@
 
 def body(raw_strain, fir_taps, fan_band, band_gain):
     where = jnp.stack([lax.axis_index("chan") % 2, lax.axis_index("tile")]).astype(jnp.int32)
-    first, second, inverse, last = (jnp.asarray(t) for t in spatial_tables())
+    second, inverse = (jnp.asarray(t) for t in spatial_tables())
     fwd, bwd = (jnp.asarray(t) for t in temporal_tables())
     partner, same, cross = permutes(raw_strain.shape[1] // DEC // HOP)
 
@@ -508,11 +536,11 @@
     shape = blocks.shape
     blocks = blocks.reshape((256,) + shape[5:])
     blocks = lax.all_to_all(blocks, AXES, 0, 0, tiled=True)
-    own, other, *middle = forward_space(where, blocks.reshape(K, BLK), first, second)
+    own, other, middle = forward_space(where, blocks, second)
     received = []
     for g in range(CHUNKS):
         if g:
-            own, other = forward_more(g, where, middle[g - 1], second)
+            own, other = forward_more(g, where, middle, second)
         from_partner = lax.ppermute(other, AXES, partner)
         from_same = lax.ppermute(own, AXES, same)
         from_cross = lax.ppermute(other, AXES, cross)
@@ -525,7 +553,7 @@
         back_cross = lax.ppermute(far, AXES, flipped(cross))
         returned.append((own, back_same, back_partner, back_cross))
     earlier = [inverse_more(g, where, returned[g], inverse) for g in range(CHUNKS - 1)]
-    filtered = inverse_space(where, returned[-1], earlier, inverse, last)
+    filtered = inverse_space(where, returned[-1], earlier, inverse)
     filtered = lax.all_to_all(filtered.reshape(256, 16, BLK), AXES, 0, 0, tiled=True)
     return unplane(filtered.reshape(shape))
 

time: 193 us -> 191 us (0.990)
  Pallas kernels: 30.4 us -> 27.2 us
    ppermute x2, starting transfers between devices: 5.81 us -> 8.58 us  [body(): from_cross = lax.ppermute(other, AXES, cross)]
    ppermute x2, starting transfers between devices: 4.53 us -> 2.1 us  [body(): back_partner = lax.ppermute(part, AXES, partner)]
    pallas_call x2, Pallas kernels: 7.48 us -> 5.27 us  [the longest x1 3.12 us: forward_space(): pl.pallas_call(forward_kernel, in_specs=[SMEM] + [VMEM] * 2, out_specs=[V...]
  transfers between devices with their start and end apart: 14 -> 14, of which waited for: 5 -> 6; matrix products, arithmetic and copies ran while one was open for 0% -> 0% of each run, Pallas kernels for 11% -> 10%
where the time goes in v4:
time: 191 us; the launch traced here: 190 us
  blocking collectives  59.9 us (31%)
  waiting for transfers between devices  58.6 us (31%)
  starting transfers between devices  42.5 us (22%)
  Pallas kernels  27.2 us (14%)
    all_to_all x1, blocking collectives, body(): lax.all_to_all(filtered.reshape(256, 16, BLK), AXES, 0, 0, tiled=True)  59.9 us
    all_to_all x1, waiting for transfers between devices, body(): blocks = lax.all_to_all(blocks, AXES, 0, 0, tiled=True)  44.8 us
    all_to_all x1, starting transfers between devices, body(): blocks = lax.all_to_all(blocks, AXES, 0, 0, tiled=True)  16.7 us
    pallas_call x2, Pallas kernels, time_filter(): pl.pallas_call(functools.partial(time_kernel, chunk == 0), grid=(steps,),...  10.2 us
    ppermute x2, starting transfers between devices, body(): from_cross = lax.ppermute(other, AXES, cross)  8.58 us
    ppermute x2, starting transfers between devices, body(): back_cross = lax.ppermute(far, AXES, flipped(cross))  7.07 us
    ppermute x2, waiting for transfers between devices, body(): back_same = lax.ppermute(halo, AXES, flipped(same))  5.55 us
    pallas_call x1, Pallas kernels, decimate(): pl.pallas_call(decimate_kernel, in_specs=[VMEM, ANY], out_specs=ANY, out_...  5.11 us
  transfers between devices with their start and end apart: 14, of which 6 were waited for; matrix products, arithmetic and copies ran while one was open for 0% of the time, Pallas kernels for 10%

profile of v4, /device:TPU:1, one launch (start us, length us, event | category | flops | bytes accessed | tf_op | source)
XLA Modules:
  0.0 190.3 jit_solution(11514138698482110506)
XLA Ops:
  0.0 5.1 %decimate.1 = f32[2,4,8,2,2,16,128]{6,5,4,3,2,1,0:T(8,128)} custom-call(bf16[1,128]{1,0:T(2,128)(2,1)} %bitcast.10, bf16[16,131072]{1,0:T(8,128)(2,1)} %raw_ref.1), custom_call_target="tpu_custom_call" | custom-call | tf_op jit(solution)/shard_map/decimate/pallas_call | solution.py:192
  5.1 16.7 %all-to-all-start = ((f32[256,16,128]{2,1,0:T(8,128)}), f32[256,16,128]{2,1,0:T(8,128)}, u32[]{:S(2)}, u32[]{:S(2)}) async-start(f32[256,16,128]{2,1,0:T(8,128)} %bitcast.9), calls=%async_computation | async-start | bytes 4194304 | tf_op jit(solution)/shard_map/all_to_all | solution.py:538
  21.9 1.7 copy-done.4
  23.6 2.9 %gains.1.refs_4_ = f32[2,16,64,128]{3,2,1,0:T(8,128)} custom-call(s32[2]{0:T(128)S(1)} %pad_add_fusion.where_ref, f32[8]{0:T(128)S(1)} %copy-done.5, s32[4096,128]{1,0:T(8,128)S(1)} %copy-done.4), custom_call_target="tpu_custom_call" | custom-call | tf_op jit(solution)/shard_map/gains/pallas_call | solution.py:437
  26.6 1.4 collective-permute-start.3
  28.0 44.8 %all-to-all-done = f32[256,16,128]{2,1,0:T(8,128)} async-done(((f32[256,16,128]{2,1,0:T(8,128)}), f32[256,16,128]{2,1,0:T(8,128)}, u32[]{:S(2)}, u32[]{:S(2)}) %all-to-all-start) | async-done | bytes 2097184 | tf_op jit(solution)/shard_map/all_to_all | solution.py:538
  72.8 3.1 %forward_space.1 = (f32[8,128,128]{2,1,0:T(8,128)S(1)}, f32[8,128,128]{2,1,0:T(8,128)S(1)}, f32[32,128,128]{2,1,0:T(8,128)S(1)}) custom-call(s32[2]{0:T(128)S(1)} %pad_add_fusion.where_ref, f32[64,64,128]{2,1,0:T(8,128)} %bitcast.4.x_ref, bf16[32,128,384]{2,1,0:T(8,128)(2,1)S(1)} %copy-done.1), custom_call_target="tpu_custom_call" | custom-call | tf_op jit(solution)/shard_map/forward_space/pallas_call | solution.py:308
  75.9 1.9 collective-permute-start.8
  77.8 4.7 %collective-permute-start.9 = (f32[8,128,128]{2,1,0:T(8,128)S(1)}, f32[8,128,128]{2,1,0:T(8,128)S(1)}, u32[]{:S(2)}, u32[]{:S(2)}) collective-permute-start(f32[8,128,128]{2,1,0:T(8,128)S(1)} %get-tuple-element.26), channel_id=1, source_target_pairs={{1,2},{2,1},{128,3},{3,128},{129,130},{130,129},{161,131},{131,161... | collective-permute-start | bytes 1572872 | tf_op jit(solution)/shard_map/ppermute | solution.py:546
  83.8 2.0 %collective-permute-start.1 = (f32[8,128,128]{2,1,0:T(8,128)S(1)}, f32[8,128,128]{2,1,0:T(8,128)S(1)}, u32[]{:S(2)}, u32[]{:S(2)}) collective-permute-start(f32[8,128,128]{2,1,0:T(8,128)S(1)} %get-tuple-element.19.refs_0_), channel_id=1, source_target_pairs={{1,0},{2,3},{128,1},{3,130},{129,128},{130,131},{161,129},{131,163... | collective-permute-start | bytes 1572872 | tf_op jit(solution)/shard_map/ppermute | solution.py:545
  85.8 3.9 %collective-permute-start.2 = (f32[8,128,128]{2,1,0:T(8,128)S(1)}, f32[8,128,128]{2,1,0:T(8,128)S(1)}, u32[]{:S(2)}, u32[]{:S(2)}) collective-permute-start(f32[8,128,128]{2,1,0:T(8,128)S(1)} %get-tuple-element.20), channel_id=1, source_target_pairs={{1,2},{2,1},{128,3},{3,128},{129,130},{130,129},{161,131},{131,161... | collective-permute-start | bytes 1572872 | tf_op jit(solution)/shard_map/ppermute | solution.py:546
  89.8 3.2 %collective-permute-done.9.refs_3_ = f32[8,128,128]{2,1,0:T(8,128)S(1)} collective-permute-done((f32[8,128,128]{2,1,0:T(8,128)S(1)}, f32[8,128,128]{2,1,0:T(8,128)S(1)}, u32[]{:S(2)}, u32[]{:S(2)}) %collective-permute-start.9) | collective-permute-done | bytes 524320 | tf_op jit(solution)/shard_map/ppermute | solution.py:546
  93.1 5.1 %time_filter.3 = (f32[8,128,128]{2,1,0:T(8,128)S(1)}, f32[8,128,128]{2,1,0:T(8,128)S(1)}, f32[8,128,128]{2,1,0:T(8,128)S(1)}, f32[8,128,128]{2,1,0:T(8,128)S(1)}) custom-call(s32[2]{0:T(128)S(1)} %pad_add_fusion.where_ref, f32[8,128,128]{2,1,0:T(8,128)S(1)} %get-tuple-element.25.refs_0_, f32[8,128,128]{2,1,0:T(8,128)S(1)} %collective-permute-done.7.refs_1_, ...), custom_call_target="tpu_custom_call" | custom-call | tf_op jit(solution)/shard_map/time_filter/pallas_call | solution.py:515
  98.2 1.3 collective-permute-start.10
  100.4 3.8 %collective-permute-start.12 = (f32[8,128,128]{2,1,0:T(8,128)S(1)}, f32[8,128,128]{2,1,0:T(8,128)S(1)}, u32[]{:S(2)}, u32[]{:S(2)}) collective-permute-start(f32[8,128,128]{2,1,0:T(8,128)S(1)} %get-tuple-element.30), channel_id=1, source_target_pairs={{2,1},{1,2},{3,128},{128,3},{130,129},{129,130},{131,161},{161,131... | collective-permute-start | bytes 1572872 | tf_op jit(solution)/shard_map/ppermute | solution.py:553
  104.2 1.8 collective-permute-done.2.refs_3_
  106.0 5.1 %time_filter.2 = (f32[8,128,128]{2,1,0:T(8,128)S(1)}, f32[8,128,128]{2,1,0:T(8,128)S(1)}, f32[8,128,128]{2,1,0:T(8,128)S(1)}, f32[8,128,128]{2,1,0:T(8,128)S(1)}) custom-call(s32[2]{0:T(128)S(1)} %pad_add_fusion.where_ref, f32[8,128,128]{2,1,0:T(8,128)S(1)} %get-tuple-element.19.refs_0_, f32[8,128,128]{2,1,0:T(8,128)S(1)} %collective-permute-done.refs_1_, ...), custom_call_target="tpu_custom_call" | custom-call | tf_op jit(solution)/shard_map/time_filter/pallas_call | solution.py:515
  111.1 1.3 collective-permute-start.4
  113.8 3.3 %collective-permute-start.6 = (f32[8,128,128]{2,1,0:T(8,128)S(1)}, f32[8,128,128]{2,1,0:T(8,128)S(1)}, u32[]{:S(2)}, u32[]{:S(2)}) collective-permute-start(f32[8,128,128]{2,1,0:T(8,128)S(1)} %get-tuple-element.24), channel_id=1, source_target_pairs={{2,1},{1,2},{3,128},{128,3},{130,129},{129,130},{131,161},{161,131... | collective-permute-start | bytes 1572872 | tf_op jit(solution)/shard_map/ppermute | solution.py:553
  118.2 5.4 %collective-permute-done.4.halo_ref = f32[8,128,128]{2,1,0:T(8,128)S(1)} collective-permute-done((f32[8,128,128]{2,1,0:T(8,128)S(1)}, f32[8,128,128]{2,1,0:T(8,128)S(1)}, u32[]{:S(2)}, u32[]{:S(2)}) %collective-permute-start.4) | collective-permute-done | bytes 524320 | tf_op jit(solution)/shard_map/ppermute | solution.py:552
  123.6 3.2 %collective-permute-done.6.cross_ref = f32[8,128,128]{2,1,0:T(8,128)S(1)} collective-permute-done((f32[8,128,128]{2,1,0:T(8,128)S(1)}, f32[8,128,128]{2,1,0:T(8,128)S(1)}, u32[]{:S(2)}, u32[]{:S(2)}) %collective-permute-start.6) | collective-permute-done | bytes 524320 | tf_op jit(solution)/shard_map/ppermute | solution.py:553
  126.8 2.1 %inverse_space.1 = f32[64,64,128]{2,1,0:T(8,128)S(1)} custom-call(s32[2]{0:T(128)S(1)} %pad_add_fusion.where_ref, f32[8,128,128]{2,1,0:T(8,128)S(1)} %get-tuple-element.21.own_ref, f32[8,128,128]{2,1,0:T(8,128)S(1)} %collective-permute-done.4.halo_ref, f32[8,128,128]{2,1,0:T(8,128)S(1)} %collective-permute-done.5.part_ref, ...), custom_call_target="tpu_custom_call" | custom-call | tf_op jit(solution)/shard_map/inverse_space/pallas_call | solution.py:382
  128.9 59.9 %all_to_all.10 = f32[256,16,128]{2,1,0:T(8,128)S(1)} all-to-all(f32[256,16,128]{2,1,0:T(8,128)S(1)} %bitcast.8), channel_id=1, replica_groups=mesh['chan'=128,'tile'=2] {'chan','tile'}, dimensions={0} | all-to-all | bytes 4194304 | tf_op jit(solution)/shard_map/all_to_all | solution.py:557
  188.8 1.5 unplane.1
  (27 shorter events, 4.8 us)
Async XLA Ops:
  5.1 16.8 %copy-start.5 = (f32[8]{0:T(128)S(1)}, f32[8]{0:T(128)}, u32[]{:S(2)}) copy-start(f32[8]{0:T(128)} %gain_ref.1) | copy-start | bytes 100
  5.1 67.6 %all-to-all-start = ((f32[256,16,128]{2,1,0:T(8,128)}), f32[256,16,128]{2,1,0:T(8,128)}, u32[]{:S(2)}, u32[]{:S(2)}) async-start(f32[256,16,128]{2,1,0:T(8,128)} %bitcast.9), calls=%async_computation | async-start | bytes 4194304 | tf_op jit(solution)/shard_map/all_to_all | solution.py:538
  21.8 51.0 %copy-start.1 = (bf16[32,128,384]{2,1,0:T(8,128)(2,1)S(1)}, bf16[32,128,384]{2,1,0:T(8,128)(2,1)}, u32[]{:S(2)}) copy-start(bf16[32,128,384]{2,1,0:T(8,128)(2,1)} %constant.29.clone.second_ref) | copy-start | bytes 9437188
  21.9 1.7 copy-start.4
  26.6 59.2 %collective-permute-start.3 = (f32[2,16,64,128]{3,2,1,0:T(8,128)}, f32[2,16,64,128]{3,2,1,0:T(8,128)}, u32[]{:S(2)}, u32[]{:S(2)}) collective-permute-start(f32[2,16,64,128]{3,2,1,0:T(8,128)} %gains.1.refs_4_), channel_id=1, source_target_pairs={{0,1},{1,0},{2,3},{3,2},{4,5},{5,4},{6,7},{7,6},{8,9},{9,8},{10,11... | collective-permute-start | bytes 3145736 | tf_op jit(solution)/shard_map/ppermute | solution.py:533
  75.9 13.8 %collective-permute-start.8 = (f32[8,128,128]{2,1,0:T(8,128)S(1)}, f32[8,128,128]{2,1,0:T(8,128)S(1)}, u32[]{:S(2)}, u32[]{:S(2)}) collective-permute-start(f32[8,128,128]{2,1,0:T(8,128)S(1)} %get-tuple-element.25.refs_0_), channel_id=1, source_target_pairs={{1,0},{2,3},{128,1},{3,130},{129,128},{130,131},{161,129},{131,163... | collective-permute-start | bytes 1572872 | tf_op jit(solution)/shard_map/ppermute | solution.py:545
  77.8 15.2 %collective-permute-start.9 = (f32[8,128,128]{2,1,0:T(8,128)S(1)}, f32[8,128,128]{2,1,0:T(8,128)S(1)}, u32[]{:S(2)}, u32[]{:S(2)}) collective-permute-start(f32[8,128,128]{2,1,0:T(8,128)S(1)} %get-tuple-element.26), channel_id=1, source_target_pairs={{1,2},{2,1},{128,3},{3,128},{129,130},{130,129},{161,131},{131,161... | collective-permute-start | bytes 1572872 | tf_op jit(solution)/shard_map/ppermute | solution.py:546
  82.5 10.5 %collective-permute-start.7 = (f32[8,128,128]{2,1,0:T(8,128)S(1)}, f32[8,128,128]{2,1,0:T(8,128)S(1)}, u32[]{:S(2)}, u32[]{:S(2)}) collective-permute-start(f32[8,128,128]{2,1,0:T(8,128)S(1)} %get-tuple-element.26), channel_id=1, source_target_pairs={{0,2},{2,0},{1,3},{3,1},{128,130},{130,128},{129,131},{131,129},{1... | collective-permute-start | bytes 1572872 | tf_op jit(solution)/shard_map/ppermute | solution.py:544
  82.6 10.4 %copy-start.2 = (bf16[2,512,512]{2,1,0:T(8,128)(2,1)S(1)}, bf16[2,512,512]{2,1,0:T(8,128)(2,1)}, u32[]{:S(2)}) copy-start(bf16[2,512,512]{2,1,0:T(8,128)(2,1)} %constant.32.clone.refs_7_) | copy-start | bytes 3145732
  82.6 10.4 %copy-start.3 = (bf16[2,512,512]{2,1,0:T(8,128)(2,1)S(1)}, bf16[2,512,512]{2,1,0:T(8,128)(2,1)}, u32[]{:S(2)}) copy-start(bf16[2,512,512]{2,1,0:T(8,128)(2,1)} %constant.31.clone.refs_6_) | copy-start | bytes 3145732
  83.8 16.7 %collective-permute-start.1 = (f32[8,128,128]{2,1,0:T(8,128)S(1)}, f32[8,128,128]{2,1,0:T(8,128)S(1)}, u32[]{:S(2)}, u32[]{:S(2)}) collective-permute-start(f32[8,128,128]{2,1,0:T(8,128)S(1)} %get-tuple-element.19.refs_0_), channel_id=1, source_target_pairs={{1,0},{2,3},{128,1},{3,130},{129,128},{130,131},{161,129},{131,163... | collective-permute-start | bytes 1572872 | tf_op jit(solution)/shard_map/ppermute | solution.py:545
  85.8 20.2 %collective-permute-start.2 = (f32[8,128,128]{2,1,0:T(8,128)S(1)}, f32[8,128,128]{2,1,0:T(8,128)S(1)}, u32[]{:S(2)}, u32[]{:S(2)}) collective-permute-start(f32[8,128,128]{2,1,0:T(8,128)S(1)} %get-tuple-element.20), channel_id=1, source_target_pairs={{1,2},{2,1},{128,3},{3,128},{129,130},{130,129},{161,131},{131,161... | collective-permute-start | bytes 1572872 | tf_op jit(solution)/shard_map/ppermute | solution.py:546
  89.7 16.3 %collective-permute-start = (f32[8,128,128]{2,1,0:T(8,128)S(1)}, f32[8,128,128]{2,1,0:T(8,128)S(1)}, u32[]{:S(2)}, u32[]{:S(2)}) collective-permute-start(f32[8,128,128]{2,1,0:T(8,128)S(1)} %get-tuple-element.20), channel_id=1, source_target_pairs={{0,2},{2,0},{1,3},{3,1},{128,130},{130,128},{129,131},{131,129},{1... | collective-permute-start | bytes 1572872 | tf_op jit(solution)/shard_map/ppermute | solution.py:544
  98.2 15.6 %collective-permute-start.10 = (f32[8,128,128]{2,1,0:T(8,128)S(1)}, f32[8,128,128]{2,1,0:T(8,128)S(1)}, u32[]{:S(2)}, u32[]{:S(2)}) collective-permute-start(f32[8,128,128]{2,1,0:T(8,128)S(1)} %get-tuple-element.28), channel_id=1, source_target_pairs={{0,1},{3,2},{1,128},{130,3},{128,129},{131,130},{129,161},{163,131... | collective-permute-start | bytes 1572872 | tf_op jit(solution)/shard_map/ppermute | solution.py:552
  99.5 17.6 %collective-permute-start.11 = (f32[8,128,128]{2,1,0:T(8,128)S(1)}, f32[8,128,128]{2,1,0:T(8,128)S(1)}, u32[]{:S(2)}, u32[]{:S(2)}) collective-permute-start(f32[8,128,128]{2,1,0:T(8,128)S(1)} %get-tuple-element.29), channel_id=1, source_target_pairs={{0,2},{2,0},{1,3},{3,1},{128,130},{130,128},{129,131},{131,129},{1... | collective-permute-start | bytes 1572872 | tf_op jit(solution)/shard_map/ppermute | solution.py:551
  100.4 16.7 %copy-start = (bf16[32,128,384]{2,1,0:T(8,128)(2,1)S(1)}, bf16[32,128,384]{2,1,0:T(8,128)(2,1)}, u32[]{:S(2)}) copy-start(bf16[32,128,384]{2,1,0:T(8,128)(2,1)} %constant.30.clone.inv_ref) | copy-start | bytes 9437188
  100.4 16.7 %collective-permute-start.12 = (f32[8,128,128]{2,1,0:T(8,128)S(1)}, f32[8,128,128]{2,1,0:T(8,128)S(1)}, u32[]{:S(2)}, u32[]{:S(2)}) collective-permute-start(f32[8,128,128]{2,1,0:T(8,128)S(1)} %get-tuple-element.30), channel_id=1, source_target_pairs={{2,1},{1,2},{3,128},{128,3},{130,129},{129,130},{131,161},{161,131... | collective-permute-start | bytes 1572872 | tf_op jit(solution)/shard_map/ppermute | solution.py:553
  111.1 12.4 %collective-permute-start.4 = (f32[8,128,128]{2,1,0:T(8,128)S(1)}, f32[8,128,128]{2,1,0:T(8,128)S(1)}, u32[]{:S(2)}, u32[]{:S(2)}) collective-permute-start(f32[8,128,128]{2,1,0:T(8,128)S(1)} %get-tuple-element.22), channel_id=1, source_target_pairs={{0,1},{3,2},{1,128},{130,3},{128,129},{131,130},{129,161},{163,131... | collective-permute-start | bytes 1572872 | tf_op jit(solution)/shard_map/ppermute | solution.py:552
  112.4 11.2 %collective-permute-start.5 = (f32[8,128,128]{2,1,0:T(8,128)S(1)}, f32[8,128,128]{2,1,0:T(8,128)S(1)}, u32[]{:S(2)}, u32[]{:S(2)}) collective-permute-start(f32[8,128,128]{2,1,0:T(8,128)S(1)} %get-tuple-element.23), channel_id=1, source_target_pairs={{0,2},{2,0},{1,3},{3,1},{128,130},{130,128},{129,131},{131,129},{1... | collective-permute-start | bytes 1572872 | tf_op jit(solution)/shard_map/ppermute | solution.py:551
  113.8 13.0 %collective-permute-start.6 = (f32[8,128,128]{2,1,0:T(8,128)S(1)}, f32[8,128,128]{2,1,0:T(8,128)S(1)}, u32[]{:S(2)}, u32[]{:S(2)}) collective-permute-start(f32[8,128,128]{2,1,0:T(8,128)S(1)} %get-tuple-element.24), channel_id=1, source_target_pairs={{2,1},{1,2},{3,128},{128,3},{130,129},{129,130},{131,161},{161,131... | collective-permute-start | bytes 1572872 | tf_op jit(solution)/shard_map/ppermute | solution.py:553

commit v5 on v4

--- a/solution.py
+++ b/solution.py
@@ -120,6 +120,10 @@
     return [(b, a) for a, b in pairs]
 
 
+def core_index():
+    return lax.rem(lax.axis_index("chan"), 2)
+
+
 def split(value):
     hi = value.astype(BF16)
     return hi, (value - hi.astype(F32)).astype(BF16)
@@ -141,15 +145,20 @@
     return x // 2, row, core, x % 2
 
 
-def decimate_kernel(taps_ref, raw_ref, out_ref, cur_ref, band_ref, stage_ref, in_sems, out_sems):
+def decimate_kernel(taps_hbm, raw_ref, out_ref, taps_ref, cur_ref, band_ref, stage_ref, in_sems, out_sems):
     planes = out_ref.shape[2]
     span = TAPS + DEC * BLK
     width = raw_ref.shape[1] // planes
+    pair = 2
     loads = []
-    for plane in range(planes):
-        part = pl.ds(plane * width, width)
-        loads.append(pltpu.make_async_copy(raw_ref.at[:, part], cur_ref.at[:, part], in_sems.at[plane]))
+    for n in range(planes // pair):
+        part = pl.ds(n * pair * width, pair * width)
+        loads.append(pltpu.make_async_copy(raw_ref.at[:, part], cur_ref.at[:, part], in_sems.at[n]))
         loads[-1].start()
+        if n == 0:
+            taps_load = pltpu.make_async_copy(taps_hbm, taps_ref, in_sems.at[planes])
+            taps_load.start()
+    taps_load.wait()
 
     i = lax.broadcasted_iota(jnp.int32, (TAPS, TAPS), 0)
     j = lax.broadcasted_iota(jnp.int32, (TAPS, TAPS), 1)
@@ -165,7 +174,8 @@
     band = band_ref[...]
     stores = []
     for plane in range(planes):
-        loads[plane].wait()
+        if plane % pair == 0:
+            loads[plane // pair].wait()
         for b0 in range(0, blocks, group):
             spans = []
             for b in range(b0, b0 + group):
@@ -191,14 +201,15 @@
     planes = 8
     return pl.pallas_call(
         decimate_kernel,
-        in_specs=[VMEM, ANY],
+        in_specs=[ANY, ANY],
         out_specs=ANY,
         out_shape=jax.ShapeDtypeStruct((2, 4, planes, 2, 2, channels, BLK), F32),
         scratch_shapes=[
+            pltpu.VMEM((1, TAPS), BF16),
             pltpu.VMEM(raw.shape, BF16),
             pltpu.VMEM((TAPS + DEC * BLK, BLK), BF16),
             pltpu.VMEM((planes, 2, 4, 2, 2, channels, BLK), F32),
-            pltpu.SemaphoreType.DMA((planes,)),
+            pltpu.SemaphoreType.DMA((planes + 1,)),
             pltpu.SemaphoreType.DMA((planes,)),
         ],
         compiler_params=params(60),
@@ -289,7 +300,14 @@
             other_ref[i - WIDTH] = wave
 
 
-def forward_kernel(where_ref, x_ref, second_ref, own_ref, other_ref, mid_ref):
+def forward_kernel(x_hbm, second_ref, own_ref, other_ref, mid_ref, x_ref, sems):
+    half = ROOT // 2
+    loads = []
+    for n in range(2):
+        part = pl.ds(n * half, half)
+        loads.append(pltpu.make_async_copy(x_hbm.at[:, part], x_ref.at[:, part], sems.at[n]))
+        loads[-1].start()
+
     def tile(t, carry):
         rows = pl.ds(pl.multiple_of(t * 8, 8), 8)
         rows_im = pl.ds(pl.multiple_of(ROOT + t * 8, 8), 8)
@@ -300,34 +318,37 @@
             mid_ref[s, rows, :], mid_ref[s, rows_im, :] = bins[s]
         return carry
 
-    lax.fori_loop(0, ROOT // 8, tile, 0)
-    second_stage(where_ref[0], 0, mid_ref, second_ref, own_ref, other_ref)
-
-
-def forward_space(where, x, second):
+    for n in range(2):
+        loads[n].wait()
+        lax.fori_loop(n * half // 8, (n + 1) * half // 8, tile, 0)
+    second_stage(core_index(), 0, mid_ref, second_ref, own_ref, other_ref)
+
+
+def forward_space(x, second):
     return pl.pallas_call(
         forward_kernel,
-        in_specs=[SMEM] + [VMEM] * 2,
+        in_specs=[ANY, VMEM],
         out_specs=[VMEM] * 3,
         out_shape=[WAVE, WAVE, jax.ShapeDtypeStruct((SLOTS, BLK, BLK), F32)],
+        scratch_shapes=[pltpu.VMEM((ROOT, ROOT, BLK), F32), pltpu.SemaphoreType.DMA((2,))],
         compiler_params=params(14),
         name="forward_space",
-    )(where, x.reshape(ROOT, ROOT, BLK), second)
-
-
-def forward_more_kernel(chunk, where_ref, mid_ref, second_ref, own_ref, other_ref):
-    second_stage(where_ref[0], chunk, mid_ref, second_ref, own_ref, other_ref)
-
-
-def forward_more(chunk, where, middle, second):
+    )(x.reshape(ROOT, ROOT, BLK), second)
+
+
+def forward_more_kernel(chunk, mid_ref, second_ref, own_ref, other_ref):
+    second_stage(core_index(), chunk, mid_ref, second_ref, own_ref, other_ref)
+
+
+def forward_more(chunk, middle, second):
     return pl.pallas_call(
         functools.partial(forward_more_kernel, chunk),
-        in_specs=[SMEM] + [VMEM] * 2,
+        in_specs=[VMEM] * 2,
         out_specs=[VMEM] * 2,
         out_shape=[WAVE, WAVE],
         compiler_params=params(12),
         name="forward_more",
-    )(where, middle, second)
+    )(middle, second)
 
 
 def inverse_stage(core, chunk, own_ref, halo_ref, part_ref, cross_ref, inv_ref, mid_ref):
@@ -339,24 +360,24 @@
         mid_ref[i] = dot(inv_ref[real_slot(core, chunk, i)], stacked(z))
 
 
-def inverse_more_kernel(chunk, where_ref, own_ref, halo_ref, part_ref, cross_ref, inv_ref, mid_ref):
-    inverse_stage(where_ref[0], chunk, own_ref, halo_ref, part_ref, cross_ref, inv_ref, mid_ref)
-
-
-def inverse_more(chunk, where, waves, inv):
+def inverse_more_kernel(chunk, own_ref, halo_ref, part_ref, cross_ref, inv_ref, mid_ref):
+    inverse_stage(core_index(), chunk, own_ref, halo_ref, part_ref, cross_ref, inv_ref, mid_ref)
+
+
+def inverse_more(chunk, waves, inv):
     return pl.pallas_call(
         functools.partial(inverse_more_kernel, chunk),
-        in_specs=[SMEM] + [VMEM] * 5,
+        in_specs=[VMEM] * 5,
         out_specs=VMEM,
         out_shape=MIDDLE,
         compiler_params=params(12),
         name="inverse_more",
-    )(where, *waves, inv)
-
-
-def inverse_kernel(where_ref, own_ref, halo_ref, part_ref, cross_ref, inv_ref, *rest):
+    )(*waves, inv)
+
+
+def inverse_kernel(own_ref, halo_ref, part_ref, cross_ref, inv_ref, *rest):
     earlier, out_ref, mid_ref = rest[:-2], rest[-2], rest[-1]
-    core = where_ref[0]
+    core = core_index()
     inverse_stage(core, CHUNKS - 1, own_ref, halo_ref, part_ref, cross_ref, inv_ref, mid_ref)
     refs = earlier + (mid_ref,)
 
@@ -378,20 +399,20 @@
     lax.fori_loop(0, ROOT // 8, tile, 0)
 
 
-def inverse_space(where, waves, earlier, inv):
+def inverse_space(waves, earlier, inv):
     return pl.pallas_call(
         inverse_kernel,
-        in_specs=[SMEM] + [VMEM] * (5 + len(earlier)),
+        in_specs=[VMEM] * (5 + len(earlier)),
         out_specs=VMEM,
         out_shape=jax.ShapeDtypeStruct((ROOT, ROOT, BLK), F32),
         scratch_shapes=[pltpu.VMEM(MIDDLE.shape, F32)],
         compiler_params=params(14),
         name="inverse_space",
-    )(where, *waves, inv, *earlier)
-
-
-def gains_kernel(where_ref, gain_ref, band_ref, out_ref):
-    core = where_ref[0]
+    )(*waves, inv, *earlier)
+
+
+def gains_kernel(gain_ref, band_ref, out_ref):
+    core = core_index()
     n = ROOT // 2
     i = lax.broadcasted_iota(jnp.int32, (ROOT, ROOT), 0)
     j = lax.broadcasted_iota(jnp.int32, (ROOT, ROOT), 1)
@@ -433,21 +454,21 @@
             put(0, rows(HALF, 0, ROOT), exact(mirror, rows(ROOT - HALF, 0, ROOT)))
 
 
-def gains(where, band_gain, fan_band):
+def gains(band_gain, fan_band):
     return pl.pallas_call(
         gains_kernel,
-        in_specs=[SMEM] * 2 + [VMEM],
+        in_specs=[SMEM, VMEM],
         out_specs=VMEM,
         out_shape=jax.ShapeDtypeStruct((2, HALF, ROOT, BLK), F32),
         compiler_params=params(8),
         name="gains",
-    )(where, band_gain, fan_band)
-
-
-def time_kernel(first_chunk, where_ref, *refs):
+    )(band_gain, fan_band)
+
+
+def time_kernel(first_chunk, *refs):
     own_ref, part_ref, same_ref, cross_ref, mine_ref, theirs_ref, fwd_ref, bwd_ref = refs[:8]
     out_refs = refs[8:]
-    core, xl = where_ref[0], where_ref[1]
+    core, xl = core_index(), lax.axis_index("tile")
     step = pl.program_id(0)
     slots = own_ref.shape[0]
     rows = slots * BLK
@@ -506,7 +527,7 @@
         out_ref[...] = value.reshape(slots, BLK, BLK)
 
 
-def time_filter(chunk, where, waves, mine, theirs, fwd, bwd):
+def time_filter(chunk, waves, mine, theirs, fwd, bwd):
     slots = 4
     steps = WIDTH // slots
     data = pl.BlockSpec((slots, BLK, BLK), lambda g: (g, 0, 0))
@@ -515,45 +536,44 @@
     return pl.pallas_call(
         functools.partial(time_kernel, chunk == 0),
         grid=(steps,),
-        in_specs=[SMEM] + [data] * 4 + [gain] * 2 + [table] * 2,
+        in_specs=[data] * 4 + [gain] * 2 + [table] * 2,
         out_specs=[data] * 4,
         out_shape=[jax.ShapeDtypeStruct((WIDTH, BLK, BLK), F32)] * 4,
         compiler_params=params(24),
         name="time_filter",
-    )(where, *waves, mine, theirs, fwd, bwd)
+    )(*waves, mine, theirs, fwd, bwd)
 
 
 def body(raw_strain, fir_taps, fan_band, band_gain):
-    where = jnp.stack([lax.axis_index("chan") % 2, lax.axis_index("tile")]).astype(jnp.int32)
     second, inverse = (jnp.asarray(t) for t in spatial_tables())
     fwd, bwd = (jnp.asarray(t) for t in temporal_tables())
     partner, same, cross = permutes(raw_strain.shape[1] // DEC // HOP)
 
-    mine = gains(where, band_gain, fan_band)
+    mine = gains(band_gain, fan_band)
     theirs = lax.ppermute(mine, "tile", [(0, 1), (1, 0)])
 
     blocks = decimate(raw_strain, fir_taps)
     shape = blocks.shape
     blocks = blocks.reshape((256,) + shape[5:])
     blocks = lax.all_to_all(blocks, AXES, 0, 0, tiled=True)
-    own, other, middle = forward_space(where, blocks, second)
+    own, other, middle = forward_space(blocks, second)
     received = []
     for g in range(CHUNKS):
         if g:
-            own, other = forward_more(g, where, middle, second)
+            own, other = forward_more(g, middle, second)
         from_partner = lax.ppermute(other, AXES, partner)
         from_same = lax.ppermute(own, AXES, same)
         from_cross = lax.ppermute(other, AXES, cross)
         received.append((own, from_partner, from_same, from_cross))
     returned = []
     for g in range(CHUNKS):
-        own, part, halo, far = time_filter(g, where, received[g], mine, theirs, fwd, bwd)
+        own, part, halo, far = time_filter(g, received[g], mine, theirs, fwd, bwd)
         back_partner = lax.ppermute(part, AXES, partner)
         back_same = lax.ppermute(halo, AXES, flipped(same))
         back_cross = lax.ppermute(far, AXES, flipped(cross))
         returned.append((own, back_same, back_partner, back_cross))
-    earlier = [inverse_more(g, where, returned[g], inverse) for g in range(CHUNKS - 1)]
-    filtered = inverse_space(where, returned[-1], earlier, inverse)
+    earlier = [inverse_more(g, returned[g], inverse) for g in range(CHUNKS - 1)]
+    filtered = inverse_space(returned[-1], earlier, inverse)
     filtered = lax.all_to_all(filtered.reshape(256, 16, BLK), AXES, 0, 0, tiled=True)
     return unplane(filtered.reshape(shape))
 

time: 191 us -> 189 us (0.990)
  Pallas kernels: 27.2 us -> 24 us
    pallas_call x6, Pallas kernels: 15.5 us -> 12.6 us  [the longest x1 4.16 us: decimate(): pl.pallas_call(decimate_kernel, in_specs=[ANY, ANY], out_specs=ANY, out_s...]
  transfers between devices with their start and end apart: 14 -> 14, of which waited for: 6 -> 6; matrix products, arithmetic and copies ran while one was open for 0% -> 0% of each run, Pallas kernels for 10% -> 9%
where the time goes in v5:
time: 189 us; the launch traced here: 188 us
  waiting for transfers between devices  60 us (32%)
  blocking collectives  59.6 us (32%)
  starting transfers between devices  42.7 us (23%)
  Pallas kernels  24 us (13%)
    all_to_all x1, blocking collectives, body(): lax.all_to_all(filtered.reshape(256, 16, BLK), AXES, 0, 0, tiled=True)  59.6 us
    all_to_all x1, waiting for transfers between devices, body(): blocks = lax.all_to_all(blocks, AXES, 0, 0, tiled=True)  45 us
    all_to_all x1, starting transfers between devices, body(): blocks = lax.all_to_all(blocks, AXES, 0, 0, tiled=True)  16.7 us
    pallas_call x2, Pallas kernels, time_filter(): pl.pallas_call(functools.partial(time_kernel, chunk == 0), grid=(steps,),...  9.9 us
    ppermute x2, starting transfers between devices, body(): from_cross = lax.ppermute(other, AXES, cross)  8.58 us
    ppermute x2, starting transfers between devices, body(): back_cross = lax.ppermute(far, AXES, flipped(cross))  7.18 us
    ppermute x2, waiting for transfers between devices, body(): back_same = lax.ppermute(halo, AXES, flipped(same))  6.11 us
    ppermute x2, waiting for transfers between devices, body(): from_cross = lax.ppermute(other, AXES, cross)  5.75 us
  transfers between devices with their start and end apart: 14, of which 6 were waited for; matrix products, arithmetic and copies ran while one was open for 0% of the time, Pallas kernels for 9%

profile of v5, /device:TPU:1, one launch (start us, length us, event | category | flops | bytes accessed | tf_op | source)
XLA Modules:
  0.0 188.2 jit_solution(5003916454735001670)
XLA Ops:
  0.0 4.2 %decimate.1 = f32[2,4,8,2,2,16,128]{6,5,4,3,2,1,0:T(8,128)} custom-call(bf16[1,128]{1,0:T(2,128)(2,1)} %bitcast.8, bf16[16,131072]{1,0:T(8,128)(2,1)} %raw_ref.1), custom_call_target="tpu_custom_call" | custom-call | tf_op jit(solution)/shard_map/decimate/pallas_call | solution.py:202
  4.2 16.7 %all-to-all-start = ((f32[256,16,128]{2,1,0:T(8,128)}), f32[256,16,128]{2,1,0:T(8,128)}, u32[]{:S(2)}, u32[]{:S(2)}) async-start(f32[256,16,128]{2,1,0:T(8,128)} %bitcast.7), calls=%async_computation | async-start | bytes 4194304 | tf_op jit(solution)/shard_map/all_to_all | solution.py:558
  20.9 1.6 copy-done.4
  22.5 2.9 %gains.1.refs_4_ = f32[2,16,64,128]{3,2,1,0:T(8,128)} custom-call(f32[8]{0:T(128)S(1)} %copy-done.5, s32[4096,128]{1,0:T(8,128)S(1)} %copy-done.4), custom_call_target="tpu_custom_call" | custom-call | tf_op jit(solution)/shard_map/gains/pallas_call | solution.py:458
  25.4 1.4 collective-permute-start.3
  26.8 45.0 %all-to-all-done = f32[256,16,128]{2,1,0:T(8,128)} async-done(((f32[256,16,128]{2,1,0:T(8,128)}), f32[256,16,128]{2,1,0:T(8,128)}, u32[]{:S(2)}, u32[]{:S(2)}) %all-to-all-start) | async-done | bytes 2097184 | tf_op jit(solution)/shard_map/all_to_all | solution.py:558
  71.8 2.8 %forward_space.1 = (f32[8,128,128]{2,1,0:T(8,128)S(1)}, f32[8,128,128]{2,1,0:T(8,128)S(1)}, f32[32,128,128]{2,1,0:T(8,128)S(1)}) custom-call(f32[64,64,128]{2,1,0:T(8,128)} %bitcast.2.x_hbm, bf16[32,128,384]{2,1,0:T(8,128)(2,1)S(1)} %copy-done), custom_call_target="tpu_custom_call" | custom-call | tf_op jit(solution)/shard_map/forward_space/pallas_call | solution.py:328
  74.6 1.9 %collective-permute-start.8 = (f32[8,128,128]{2,1,0:T(8,128)S(1)}, f32[8,128,128]{2,1,0:T(8,128)S(1)}, u32[]{:S(2)}, u32[]{:S(2)}) collective-permute-start(f32[8,128,128]{2,1,0:T(8,128)S(1)} %get-tuple-element.25.refs_0_), channel_id=1, source_target_pairs={{1,0},{2,3},{128,1},{3,130},{129,128},{130,131},{161,129},{131,163... | collective-permute-start | bytes 1572872 | tf_op jit(solution)/shard_map/ppermute | solution.py:565
  76.5 4.7 %collective-permute-start.9 = (f32[8,128,128]{2,1,0:T(8,128)S(1)}, f32[8,128,128]{2,1,0:T(8,128)S(1)}, u32[]{:S(2)}, u32[]{:S(2)}) collective-permute-start(f32[8,128,128]{2,1,0:T(8,128)S(1)} %get-tuple-element.26), channel_id=1, source_target_pairs={{1,2},{2,1},{128,3},{3,128},{129,130},{130,129},{161,131},{131,161... | collective-permute-start | bytes 1572872 | tf_op jit(solution)/shard_map/ppermute | solution.py:566
  81.9 2.1 %collective-permute-start.1 = (f32[8,128,128]{2,1,0:T(8,128)S(1)}, f32[8,128,128]{2,1,0:T(8,128)S(1)}, u32[]{:S(2)}, u32[]{:S(2)}) collective-permute-start(f32[8,128,128]{2,1,0:T(8,128)S(1)} %get-tuple-element.19.refs_0_), channel_id=1, source_target_pairs={{1,0},{2,3},{128,1},{3,130},{129,128},{130,131},{161,129},{131,163... | collective-permute-start | bytes 1572872 | tf_op jit(solution)/shard_map/ppermute | solution.py:565
  84.1 3.9 %collective-permute-start.2 = (f32[8,128,128]{2,1,0:T(8,128)S(1)}, f32[8,128,128]{2,1,0:T(8,128)S(1)}, u32[]{:S(2)}, u32[]{:S(2)}) collective-permute-start(f32[8,128,128]{2,1,0:T(8,128)S(1)} %get-tuple-element.20), channel_id=1, source_target_pairs={{1,2},{2,1},{128,3},{3,128},{129,130},{130,129},{161,131},{131,161... | collective-permute-start | bytes 1572872 | tf_op jit(solution)/shard_map/ppermute | solution.py:566
  88.1 3.7 %collective-permute-done.9.refs_3_ = f32[8,128,128]{2,1,0:T(8,128)S(1)} collective-permute-done((f32[8,128,128]{2,1,0:T(8,128)S(1)}, f32[8,128,128]{2,1,0:T(8,128)S(1)}, u32[]{:S(2)}, u32[]{:S(2)}) %collective-permute-start.9) | collective-permute-done | bytes 524320 | tf_op jit(solution)/shard_map/ppermute | solution.py:566
  91.8 5.0 %time_filter.3 = (f32[8,128,128]{2,1,0:T(8,128)S(1)}, f32[8,128,128]{2,1,0:T(8,128)S(1)}, f32[8,128,128]{2,1,0:T(8,128)S(1)}, f32[8,128,128]{2,1,0:T(8,128)S(1)}) custom-call(f32[8,128,128]{2,1,0:T(8,128)S(1)} %get-tuple-element.25.refs_0_, f32[8,128,128]{2,1,0:T(8,128)S(1)} %collective-permute-done.7.refs_1_, ...), custom_call_target="tpu_custom_call" | custom-call | tf_op jit(solution)/shard_map/time_filter/pallas_call | solution.py:536
  96.7 1.3 collective-permute-start.10
  99.0 3.8 %collective-permute-start.12 = (f32[8,128,128]{2,1,0:T(8,128)S(1)}, f32[8,128,128]{2,1,0:T(8,128)S(1)}, u32[]{:S(2)}, u32[]{:S(2)}) collective-permute-start(f32[8,128,128]{2,1,0:T(8,128)S(1)} %get-tuple-element.30), channel_id=1, source_target_pairs={{2,1},{1,2},{3,128},{128,3},{130,129},{129,130},{131,161},{161,131... | collective-permute-start | bytes 1572872 | tf_op jit(solution)/shard_map/ppermute | solution.py:573
  102.8 2.1 %collective-permute-done.2.refs_3_ = f32[8,128,128]{2,1,0:T(8,128)S(1)} collective-permute-done((f32[8,128,128]{2,1,0:T(8,128)S(1)}, f32[8,128,128]{2,1,0:T(8,128)S(1)}, u32[]{:S(2)}, u32[]{:S(2)}) %collective-permute-start.2) | collective-permute-done | bytes 524320 | tf_op jit(solution)/shard_map/ppermute | solution.py:566
  104.9 4.9 %time_filter.2 = (f32[8,128,128]{2,1,0:T(8,128)S(1)}, f32[8,128,128]{2,1,0:T(8,128)S(1)}, f32[8,128,128]{2,1,0:T(8,128)S(1)}, f32[8,128,128]{2,1,0:T(8,128)S(1)}) custom-call(f32[8,128,128]{2,1,0:T(8,128)S(1)} %get-tuple-element.19.refs_0_, f32[8,128,128]{2,1,0:T(8,128)S(1)} %collective-permute-done.refs_1_, ...), custom_call_target="tpu_custom_call" | custom-call | tf_op jit(solution)/shard_map/time_filter/pallas_call | solution.py:536
  109.8 1.3 collective-permute-start.4
  112.3 3.4 %collective-permute-start.6 = (f32[8,128,128]{2,1,0:T(8,128)S(1)}, f32[8,128,128]{2,1,0:T(8,128)S(1)}, u32[]{:S(2)}, u32[]{:S(2)}) collective-permute-start(f32[8,128,128]{2,1,0:T(8,128)S(1)} %get-tuple-element.24), channel_id=1, source_target_pairs={{2,1},{1,2},{3,128},{128,3},{130,129},{129,130},{131,161},{161,131... | collective-permute-start | bytes 1572872 | tf_op jit(solution)/shard_map/ppermute | solution.py:573
  116.4 6.0 %collective-permute-done.4.halo_ref = f32[8,128,128]{2,1,0:T(8,128)S(1)} collective-permute-done((f32[8,128,128]{2,1,0:T(8,128)S(1)}, f32[8,128,128]{2,1,0:T(8,128)S(1)}, u32[]{:S(2)}, u32[]{:S(2)}) %collective-permute-start.4) | collective-permute-done | bytes 524320 | tf_op jit(solution)/shard_map/ppermute | solution.py:572
  122.4 3.1 %collective-permute-done.6.cross_ref = f32[8,128,128]{2,1,0:T(8,128)S(1)} collective-permute-done((f32[8,128,128]{2,1,0:T(8,128)S(1)}, f32[8,128,128]{2,1,0:T(8,128)S(1)}, u32[]{:S(2)}, u32[]{:S(2)}) %collective-permute-start.6) | collective-permute-done | bytes 524320 | tf_op jit(solution)/shard_map/ppermute | solution.py:573
  125.5 1.6 inverse_space.1
  127.1 59.6 %all_to_all.10 = f32[256,16,128]{2,1,0:T(8,128)S(1)} all-to-all(f32[256,16,128]{2,1,0:T(8,128)S(1)} %bitcast.6), channel_id=1, replica_groups=mesh['chan'=128,'tile'=2] {'chan','tile'}, dimensions={0} | all-to-all | bytes 4194304 | tf_op jit(solution)/shard_map/all_to_all | solution.py:577
  186.7 1.5 unplane.1
  (26 shorter events, 3.6 us)
Async XLA Ops:
  4.2 16.7 %copy-start.5 = (f32[8]{0:T(128)S(1)}, f32[8]{0:T(128)}, u32[]{:S(2)}) copy-start(f32[8]{0:T(128)} %gain_ref.1) | copy-start | bytes 100
  4.2 67.6 %all-to-all-start = ((f32[256,16,128]{2,1,0:T(8,128)}), f32[256,16,128]{2,1,0:T(8,128)}, u32[]{:S(2)}, u32[]{:S(2)}) async-start(f32[256,16,128]{2,1,0:T(8,128)} %bitcast.7), calls=%async_computation | async-start | bytes 4194304 | tf_op jit(solution)/shard_map/all_to_all | solution.py:558
  20.9 1.6 copy-start.4
  22.4 49.4 %copy-start = (bf16[32,128,384]{2,1,0:T(8,128)(2,1)S(1)}, bf16[32,128,384]{2,1,0:T(8,128)(2,1)}, u32[]{:S(2)}) copy-start(bf16[32,128,384]{2,1,0:T(8,128)(2,1)} %constant.8.clone.second_ref) | copy-start | bytes 9437188
  25.4 58.7 %collective-permute-start.3 = (f32[2,16,64,128]{3,2,1,0:T(8,128)}, f32[2,16,64,128]{3,2,1,0:T(8,128)}, u32[]{:S(2)}, u32[]{:S(2)}) collective-permute-start(f32[2,16,64,128]{3,2,1,0:T(8,128)} %gains.1.refs_4_), channel_id=1, source_target_pairs={{0,1},{1,0},{2,3},{3,2},{4,5},{5,4},{6,7},{7,6},{8,9},{9,8},{10,11... | collective-permute-start | bytes 3145736 | tf_op jit(solution)/shard_map/ppermute | solution.py:553
  74.6 13.4 %collective-permute-start.8 = (f32[8,128,128]{2,1,0:T(8,128)S(1)}, f32[8,128,128]{2,1,0:T(8,128)S(1)}, u32[]{:S(2)}, u32[]{:S(2)}) collective-permute-start(f32[8,128,128]{2,1,0:T(8,128)S(1)} %get-tuple-element.25.refs_0_), channel_id=1, source_target_pairs={{1,0},{2,3},{128,1},{3,130},{129,128},{130,131},{161,129},{131,163... | collective-permute-start | bytes 1572872 | tf_op jit(solution)/shard_map/ppermute | solution.py:565
  76.5 15.2 %collective-permute-start.9 = (f32[8,128,128]{2,1,0:T(8,128)S(1)}, f32[8,128,128]{2,1,0:T(8,128)S(1)}, u32[]{:S(2)}, u32[]{:S(2)}) collective-permute-start(f32[8,128,128]{2,1,0:T(8,128)S(1)} %get-tuple-element.26), channel_id=1, source_target_pairs={{1,2},{2,1},{128,3},{3,128},{129,130},{130,129},{161,131},{131,161... | collective-permute-start | bytes 1572872 | tf_op jit(solution)/shard_map/ppermute | solution.py:566
  81.2 10.5 %collective-permute-start.7 = (f32[8,128,128]{2,1,0:T(8,128)S(1)}, f32[8,128,128]{2,1,0:T(8,128)S(1)}, u32[]{:S(2)}, u32[]{:S(2)}) collective-permute-start(f32[8,128,128]{2,1,0:T(8,128)S(1)} %get-tuple-element.26), channel_id=1, source_target_pairs={{0,2},{2,0},{1,3},{3,1},{128,130},{130,128},{129,131},{131,129},{1... | collective-permute-start | bytes 1572872 | tf_op jit(solution)/shard_map/ppermute | solution.py:564
  81.3 10.4 %copy-start.2 = (bf16[2,512,512]{2,1,0:T(8,128)(2,1)S(1)}, bf16[2,512,512]{2,1,0:T(8,128)(2,1)}, u32[]{:S(2)}) copy-start(bf16[2,512,512]{2,1,0:T(8,128)(2,1)} %constant.11.clone.refs_7_) | copy-start | bytes 3145732
  81.3 10.4 %copy-start.3 = (bf16[2,512,512]{2,1,0:T(8,128)(2,1)S(1)}, bf16[2,512,512]{2,1,0:T(8,128)(2,1)}, u32[]{:S(2)}) copy-start(bf16[2,512,512]{2,1,0:T(8,128)(2,1)} %constant.10.clone.refs_6_) | copy-start | bytes 3145732
  81.9 17.1 %collective-permute-start.1 = (f32[8,128,128]{2,1,0:T(8,128)S(1)}, f32[8,128,128]{2,1,0:T(8,128)S(1)}, u32[]{:S(2)}, u32[]{:S(2)}) collective-permute-start(f32[8,128,128]{2,1,0:T(8,128)S(1)} %get-tuple-element.19.refs_0_), channel_id=1, source_target_pairs={{1,0},{2,3},{128,1},{3,130},{129,128},{130,131},{161,129},{131,163... | collective-permute-start | bytes 1572872 | tf_op jit(solution)/shard_map/ppermute | solution.py:565
  84.1 20.8 %collective-permute-start.2 = (f32[8,128,128]{2,1,0:T(8,128)S(1)}, f32[8,128,128]{2,1,0:T(8,128)S(1)}, u32[]{:S(2)}, u32[]{:S(2)}) collective-permute-start(f32[8,128,128]{2,1,0:T(8,128)S(1)} %get-tuple-element.20), channel_id=1, source_target_pairs={{1,2},{2,1},{128,3},{3,128},{129,130},{130,129},{161,131},{131,161... | collective-permute-start | bytes 1572872 | tf_op jit(solution)/shard_map/ppermute | solution.py:566
  88.0 16.9 %collective-permute-start = (f32[8,128,128]{2,1,0:T(8,128)S(1)}, f32[8,128,128]{2,1,0:T(8,128)S(1)}, u32[]{:S(2)}, u32[]{:S(2)}) collective-permute-start(f32[8,128,128]{2,1,0:T(8,128)S(1)} %get-tuple-element.20), channel_id=1, source_target_pairs={{0,2},{2,0},{1,3},{3,1},{128,130},{130,128},{129,131},{131,129},{1... | collective-permute-start | bytes 1572872 | tf_op jit(solution)/shard_map/ppermute | solution.py:564
  96.7 15.6 %collective-permute-start.10 = (f32[8,128,128]{2,1,0:T(8,128)S(1)}, f32[8,128,128]{2,1,0:T(8,128)S(1)}, u32[]{:S(2)}, u32[]{:S(2)}) collective-permute-start(f32[8,128,128]{2,1,0:T(8,128)S(1)} %get-tuple-element.28), channel_id=1, source_target_pairs={{0,1},{3,2},{1,128},{130,3},{128,129},{131,130},{129,161},{163,131... | collective-permute-start | bytes 1572872 | tf_op jit(solution)/shard_map/ppermute | solution.py:572
  98.0 17.7 %collective-permute-start.11 = (f32[8,128,128]{2,1,0:T(8,128)S(1)}, f32[8,128,128]{2,1,0:T(8,128)S(1)}, u32[]{:S(2)}, u32[]{:S(2)}) collective-permute-start(f32[8,128,128]{2,1,0:T(8,128)S(1)} %get-tuple-element.29), channel_id=1, source_target_pairs={{0,2},{2,0},{1,3},{3,1},{128,130},{130,128},{129,131},{131,129},{1... | collective-permute-start | bytes 1572872 | tf_op jit(solution)/shard_map/ppermute | solution.py:571
  99.0 16.8 %copy-start.1 = (bf16[32,128,384]{2,1,0:T(8,128)(2,1)S(1)}, bf16[32,128,384]{2,1,0:T(8,128)(2,1)}, u32[]{:S(2)}) copy-start(bf16[32,128,384]{2,1,0:T(8,128)(2,1)} %constant.9.clone.inv_ref) | copy-start | bytes 9437188
  99.0 16.8 %collective-permute-start.12 = (f32[8,128,128]{2,1,0:T(8,128)S(1)}, f32[8,128,128]{2,1,0:T(8,128)S(1)}, u32[]{:S(2)}, u32[]{:S(2)}) collective-permute-start(f32[8,128,128]{2,1,0:T(8,128)S(1)} %get-tuple-element.30), channel_id=1, source_target_pairs={{2,1},{1,2},{3,128},{128,3},{130,129},{129,130},{131,161},{161,131... | collective-permute-start | bytes 1572872 | tf_op jit(solution)/shard_map/ppermute | solution.py:573
  109.8 12.6 %collective-permute-start.4 = (f32[8,128,128]{2,1,0:T(8,128)S(1)}, f32[8,128,128]{2,1,0:T(8,128)S(1)}, u32[]{:S(2)}, u32[]{:S(2)}) collective-permute-start(f32[8,128,128]{2,1,0:T(8,128)S(1)} %get-tuple-element.22), channel_id=1, source_target_pairs={{0,1},{3,2},{1,128},{130,3},{128,129},{131,130},{129,161},{163,131... | collective-permute-start | bytes 1572872 | tf_op jit(solution)/shard_map/ppermute | solution.py:572
  111.1 11.3 %collective-permute-start.5 = (f32[8,128,128]{2,1,0:T(8,128)S(1)}, f32[8,128,128]{2,1,0:T(8,128)S(1)}, u32[]{:S(2)}, u32[]{:S(2)}) collective-permute-start(f32[8,128,128]{2,1,0:T(8,128)S(1)} %get-tuple-element.23), channel_id=1, source_target_pairs={{0,2},{2,0},{1,3},{3,1},{128,130},{130,128},{129,131},{131,129},{1... | collective-permute-start | bytes 1572872 | tf_op jit(solution)/shard_map/ppermute | solution.py:571
  112.3 13.1 %collective-permute-start.6 = (f32[8,128,128]{2,1,0:T(8,128)S(1)}, f32[8,128,128]{2,1,0:T(8,128)S(1)}, u32[]{:S(2)}, u32[]{:S(2)}) collective-permute-start(f32[8,128,128]{2,1,0:T(8,128)S(1)} %get-tuple-element.24), channel_id=1, source_target_pairs={{2,1},{1,2},{3,128},{128,3},{130,129},{129,130},{131,161},{161,131... | collective-permute-start | bytes 1572872 | tf_op jit(solution)/shard_map/ppermute | solution.py:573

commit v6 on v5

--- a/solution.py
+++ b/solution.py
@@ -528,7 +528,7 @@
 
 
 def time_filter(chunk, waves, mine, theirs, fwd, bwd):
-    slots = 4
+    slots = 8
     steps = WIDTH // slots
     data = pl.BlockSpec((slots, BLK, BLK), lambda g: (g, 0, 0))
     gain = pl.BlockSpec((2, slots, ROOT, BLK), lambda g: (0, chunk * steps + g, 0, 0))

time: 189 us -> 188 us (level)
  transfers between devices with their start and end apart: 14 -> 14, of which waited for: 6 -> 5; matrix products, arithmetic and copies ran while one was open for 0% -> 0% of each run, Pallas kernels for 9% -> 9%
where the time goes in v6:
time: 188 us
  waiting for transfers between devices  60.5 us (32%)
  blocking collectives  59.2 us (31%)
  starting transfers between devices  42.8 us (23%)
  Pallas kernels  23.4 us (12%)
    all_to_all x1, blocking collectives, body(): lax.all_to_all(filtered.reshape(256, 16, BLK), AXES, 0, 0, tiled=True)  59.2 us
    all_to_all x1, waiting for transfers between devices, body(): blocks = lax.all_to_all(blocks, AXES, 0, 0, tiled=True)  45 us
    all_to_all x1, starting transfers between devices, body(): blocks = lax.all_to_all(blocks, AXES, 0, 0, tiled=True)  16.7 us
    pallas_call x2, Pallas kernels, time_filter(): pl.pallas_call(functools.partial(time_kernel, chunk == 0), grid=(steps,),...  9.32 us
    ppermute x2, starting transfers between devices, body(): from_cross = lax.ppermute(other, AXES, cross)  8.58 us
    ppermute x2, starting transfers between devices, body(): back_cross = lax.ppermute(far, AXES, flipped(cross))  7.45 us
    ppermute x2, waiting for transfers between devices, body(): back_same = lax.ppermute(halo, AXES, flipped(same))  6.46 us
    ppermute x2, waiting for transfers between devices, body(): from_cross = lax.ppermute(other, AXES, cross)  6.16 us
  transfers between devices with their start and end apart: 14, of which 5 were waited for; matrix products, arithmetic and copies ran while one was open for 0% of the time, Pallas kernels for 9%

profile of v6, /device:TPU:1, one launch (start us, length us, event | category | flops | bytes accessed | tf_op | source)
XLA Modules:
  0.0 187.7 jit_solution(15457466197984382150)
XLA Ops:
  0.0 4.2 %decimate.1 = f32[2,4,8,2,2,16,128]{6,5,4,3,2,1,0:T(8,128)} custom-call(bf16[1,128]{1,0:T(2,128)(2,1)} %bitcast.8, bf16[16,131072]{1,0:T(8,128)(2,1)} %raw_ref.1), custom_call_target="tpu_custom_call" | custom-call | tf_op jit(solution)/shard_map/decimate/pallas_call | solution.py:202
  4.2 16.7 %all-to-all-start = ((f32[256,16,128]{2,1,0:T(8,128)}), f32[256,16,128]{2,1,0:T(8,128)}, u32[]{:S(2)}, u32[]{:S(2)}) async-start(f32[256,16,128]{2,1,0:T(8,128)} %bitcast.7), calls=%async_computation | async-start | bytes 4194304 | tf_op jit(solution)/shard_map/all_to_all | solution.py:558
  20.9 1.6 copy-done.4
  22.5 2.9 %gains.1.refs_4_ = f32[2,16,64,128]{3,2,1,0:T(8,128)} custom-call(f32[8]{0:T(128)S(1)} %copy-done.5, s32[4096,128]{1,0:T(8,128)S(1)} %copy-done.4), custom_call_target="tpu_custom_call" | custom-call | tf_op jit(solution)/shard_map/gains/pallas_call | solution.py:458
  25.4 1.4 collective-permute-start.3
  26.8 45.0 %all-to-all-done = f32[256,16,128]{2,1,0:T(8,128)} async-done(((f32[256,16,128]{2,1,0:T(8,128)}), f32[256,16,128]{2,1,0:T(8,128)}, u32[]{:S(2)}, u32[]{:S(2)}) %all-to-all-start) | async-done | bytes 2097184 | tf_op jit(solution)/shard_map/all_to_all | solution.py:558
  71.8 2.8 %forward_space.1 = (f32[8,128,128]{2,1,0:T(8,128)S(1)}, f32[8,128,128]{2,1,0:T(8,128)S(1)}, f32[32,128,128]{2,1,0:T(8,128)S(1)}) custom-call(f32[64,64,128]{2,1,0:T(8,128)} %bitcast.2.x_hbm, bf16[32,128,384]{2,1,0:T(8,128)(2,1)S(1)} %copy-done), custom_call_target="tpu_custom_call" | custom-call | tf_op jit(solution)/shard_map/forward_space/pallas_call | solution.py:328
  74.6 1.9 %collective-permute-start.8 = (f32[8,128,128]{2,1,0:T(8,128)S(1)}, f32[8,128,128]{2,1,0:T(8,128)S(1)}, u32[]{:S(2)}, u32[]{:S(2)}) collective-permute-start(f32[8,128,128]{2,1,0:T(8,128)S(1)} %get-tuple-element.25.refs_0_), channel_id=1, source_target_pairs={{1,0},{2,3},{128,1},{3,130},{129,128},{130,131},{161,129},{131,163... | collective-permute-start | bytes 1572872 | tf_op jit(solution)/shard_map/ppermute | solution.py:565
  76.5 4.7 %collective-permute-start.9 = (f32[8,128,128]{2,1,0:T(8,128)S(1)}, f32[8,128,128]{2,1,0:T(8,128)S(1)}, u32[]{:S(2)}, u32[]{:S(2)}) collective-permute-start(f32[8,128,128]{2,1,0:T(8,128)S(1)} %get-tuple-element.26), channel_id=1, source_target_pairs={{1,2},{2,1},{128,3},{3,128},{129,130},{130,129},{161,131},{131,161... | collective-permute-start | bytes 1572872 | tf_op jit(solution)/shard_map/ppermute | solution.py:566
  81.9 2.1 %collective-permute-start.1 = (f32[8,128,128]{2,1,0:T(8,128)S(1)}, f32[8,128,128]{2,1,0:T(8,128)S(1)}, u32[]{:S(2)}, u32[]{:S(2)}) collective-permute-start(f32[8,128,128]{2,1,0:T(8,128)S(1)} %get-tuple-element.19.refs_0_), channel_id=1, source_target_pairs={{1,0},{2,3},{128,1},{3,130},{129,128},{130,131},{161,129},{131,163... | collective-permute-start | bytes 1572872 | tf_op jit(solution)/shard_map/ppermute | solution.py:565
  84.1 3.9 %collective-permute-start.2 = (f32[8,128,128]{2,1,0:T(8,128)S(1)}, f32[8,128,128]{2,1,0:T(8,128)S(1)}, u32[]{:S(2)}, u32[]{:S(2)}) collective-permute-start(f32[8,128,128]{2,1,0:T(8,128)S(1)} %get-tuple-element.20), channel_id=1, source_target_pairs={{1,2},{2,1},{128,3},{3,128},{129,130},{130,129},{161,131},{131,161... | collective-permute-start | bytes 1572872 | tf_op jit(solution)/shard_map/ppermute | solution.py:566
  88.1 3.7 %collective-permute-done.9.refs_3_ = f32[8,128,128]{2,1,0:T(8,128)S(1)} collective-permute-done((f32[8,128,128]{2,1,0:T(8,128)S(1)}, f32[8,128,128]{2,1,0:T(8,128)S(1)}, u32[]{:S(2)}, u32[]{:S(2)}) %collective-permute-start.9) | collective-permute-done | bytes 524320 | tf_op jit(solution)/shard_map/ppermute | solution.py:566
  91.8 4.7 %time_filter.3 = (f32[8,128,128]{2,1,0:T(8,128)S(1)}, f32[8,128,128]{2,1,0:T(8,128)S(1)}, f32[8,128,128]{2,1,0:T(8,128)S(1)}, f32[8,128,128]{2,1,0:T(8,128)S(1)}) custom-call(f32[8,128,128]{2,1,0:T(8,128)S(1)} %get-tuple-element.25.refs_0_, f32[8,128,128]{2,1,0:T(8,128)S(1)} %collective-permute-done.7.refs_1_, ...), custom_call_target="tpu_custom_call" | custom-call | tf_op jit(solution)/shard_map/time_filter/pallas_call | solution.py:536
  96.4 1.3 collective-permute-start.10
  98.7 3.9 %collective-permute-start.12 = (f32[8,128,128]{2,1,0:T(8,128)S(1)}, f32[8,128,128]{2,1,0:T(8,128)S(1)}, u32[]{:S(2)}, u32[]{:S(2)}) collective-permute-start(f32[8,128,128]{2,1,0:T(8,128)S(1)} %get-tuple-element.30), channel_id=1, source_target_pairs={{2,1},{1,2},{3,128},{128,3},{130,129},{129,130},{131,161},{161,131... | collective-permute-start | bytes 1572872 | tf_op jit(solution)/shard_map/ppermute | solution.py:573
  102.7 2.5 %collective-permute-done.2.refs_3_ = f32[8,128,128]{2,1,0:T(8,128)S(1)} collective-permute-done((f32[8,128,128]{2,1,0:T(8,128)S(1)}, f32[8,128,128]{2,1,0:T(8,128)S(1)}, u32[]{:S(2)}, u32[]{:S(2)}) %collective-permute-start.2) | collective-permute-done | bytes 524320 | tf_op jit(solution)/shard_map/ppermute | solution.py:566
  105.2 4.7 %time_filter.2 = (f32[8,128,128]{2,1,0:T(8,128)S(1)}, f32[8,128,128]{2,1,0:T(8,128)S(1)}, f32[8,128,128]{2,1,0:T(8,128)S(1)}, f32[8,128,128]{2,1,0:T(8,128)S(1)}) custom-call(f32[8,128,128]{2,1,0:T(8,128)S(1)} %get-tuple-element.19.refs_0_, f32[8,128,128]{2,1,0:T(8,128)S(1)} %collective-permute-done.refs_1_, ...), custom_call_target="tpu_custom_call" | custom-call | tf_op jit(solution)/shard_map/time_filter/pallas_call | solution.py:536
  109.8 1.3 collective-permute-start.4
  112.1 3.5 %collective-permute-start.6 = (f32[8,128,128]{2,1,0:T(8,128)S(1)}, f32[8,128,128]{2,1,0:T(8,128)S(1)}, u32[]{:S(2)}, u32[]{:S(2)}) collective-permute-start(f32[8,128,128]{2,1,0:T(8,128)S(1)} %get-tuple-element.24), channel_id=1, source_target_pairs={{2,1},{1,2},{3,128},{128,3},{130,129},{129,130},{131,161},{161,131... | collective-permute-start | bytes 1572872 | tf_op jit(solution)/shard_map/ppermute | solution.py:573
  116.2 6.5 %collective-permute-done.4.halo_ref = f32[8,128,128]{2,1,0:T(8,128)S(1)} collective-permute-done((f32[8,128,128]{2,1,0:T(8,128)S(1)}, f32[8,128,128]{2,1,0:T(8,128)S(1)}, u32[]{:S(2)}, u32[]{:S(2)}) %collective-permute-start.4) | collective-permute-done | bytes 524320 | tf_op jit(solution)/shard_map/ppermute | solution.py:572
  122.7 2.8 %collective-permute-done.6.cross_ref = f32[8,128,128]{2,1,0:T(8,128)S(1)} collective-permute-done((f32[8,128,128]{2,1,0:T(8,128)S(1)}, f32[8,128,128]{2,1,0:T(8,128)S(1)}, u32[]{:S(2)}, u32[]{:S(2)}) %collective-permute-start.6) | collective-permute-done | bytes 524320 | tf_op jit(solution)/shard_map/ppermute | solution.py:573
  125.5 1.6 inverse_space.1
  127.1 59.2 %all_to_all.10 = f32[256,16,128]{2,1,0:T(8,128)S(1)} all-to-all(f32[256,16,128]{2,1,0:T(8,128)S(1)} %bitcast.6), channel_id=1, replica_groups=mesh['chan'=128,'tile'=2] {'chan','tile'}, dimensions={0} | all-to-all | bytes 4194304 | tf_op jit(solution)/shard_map/all_to_all | solution.py:577
  186.3 1.5 unplane.1
  (26 shorter events, 3.3 us)
Async XLA Ops:
  4.2 16.7 %copy-start.5 = (f32[8]{0:T(128)S(1)}, f32[8]{0:T(128)}, u32[]{:S(2)}) copy-start(f32[8]{0:T(128)} %gain_ref.1) | copy-start | bytes 100
  4.2 67.6 %all-to-all-start = ((f32[256,16,128]{2,1,0:T(8,128)}), f32[256,16,128]{2,1,0:T(8,128)}, u32[]{:S(2)}, u32[]{:S(2)}) async-start(f32[256,16,128]{2,1,0:T(8,128)} %bitcast.7), calls=%async_computation | async-start | bytes 4194304 | tf_op jit(solution)/shard_map/all_to_all | solution.py:558
  20.9 1.6 copy-start.4
  22.4 49.4 %copy-start = (bf16[32,128,384]{2,1,0:T(8,128)(2,1)S(1)}, bf16[32,128,384]{2,1,0:T(8,128)(2,1)}, u32[]{:S(2)}) copy-start(bf16[32,128,384]{2,1,0:T(8,128)(2,1)} %constant.8.clone.second_ref) | copy-start | bytes 9437188
  25.4 58.7 %collective-permute-start.3 = (f32[2,16,64,128]{3,2,1,0:T(8,128)}, f32[2,16,64,128]{3,2,1,0:T(8,128)}, u32[]{:S(2)}, u32[]{:S(2)}) collective-permute-start(f32[2,16,64,128]{3,2,1,0:T(8,128)} %gains.1.refs_4_), channel_id=1, source_target_pairs={{0,1},{1,0},{2,3},{3,2},{4,5},{5,4},{6,7},{7,6},{8,9},{9,8},{10,11... | collective-permute-start | bytes 3145736 | tf_op jit(solution)/shard_map/ppermute | solution.py:553
  74.6 13.4 %collective-permute-start.8 = (f32[8,128,128]{2,1,0:T(8,128)S(1)}, f32[8,128,128]{2,1,0:T(8,128)S(1)}, u32[]{:S(2)}, u32[]{:S(2)}) collective-permute-start(f32[8,128,128]{2,1,0:T(8,128)S(1)} %get-tuple-element.25.refs_0_), channel_id=1, source_target_pairs={{1,0},{2,3},{128,1},{3,130},{129,128},{130,131},{161,129},{131,163... | collective-permute-start | bytes 1572872 | tf_op jit(solution)/shard_map/ppermute | solution.py:565
  76.5 15.2 %collective-permute-start.9 = (f32[8,128,128]{2,1,0:T(8,128)S(1)}, f32[8,128,128]{2,1,0:T(8,128)S(1)}, u32[]{:S(2)}, u32[]{:S(2)}) collective-permute-start(f32[8,128,128]{2,1,0:T(8,128)S(1)} %get-tuple-element.26), channel_id=1, source_target_pairs={{1,2},{2,1},{128,3},{3,128},{129,130},{130,129},{161,131},{131,161... | collective-permute-start | bytes 1572872 | tf_op jit(solution)/shard_map/ppermute | solution.py:566
  81.2 10.5 %collective-permute-start.7 = (f32[8,128,128]{2,1,0:T(8,128)S(1)}, f32[8,128,128]{2,1,0:T(8,128)S(1)}, u32[]{:S(2)}, u32[]{:S(2)}) collective-permute-start(f32[8,128,128]{2,1,0:T(8,128)S(1)} %get-tuple-element.26), channel_id=1, source_target_pairs={{0,2},{2,0},{1,3},{3,1},{128,130},{130,128},{129,131},{131,129},{1... | collective-permute-start | bytes 1572872 | tf_op jit(solution)/shard_map/ppermute | solution.py:564
  81.3 10.4 %copy-start.2 = (bf16[2,512,512]{2,1,0:T(8,128)(2,1)S(1)}, bf16[2,512,512]{2,1,0:T(8,128)(2,1)}, u32[]{:S(2)}) copy-start(bf16[2,512,512]{2,1,0:T(8,128)(2,1)} %constant.11.clone.refs_7_) | copy-start | bytes 3145732
  81.3 10.4 %copy-start.3 = (bf16[2,512,512]{2,1,0:T(8,128)(2,1)S(1)}, bf16[2,512,512]{2,1,0:T(8,128)(2,1)}, u32[]{:S(2)}) copy-start(bf16[2,512,512]{2,1,0:T(8,128)(2,1)} %constant.10.clone.refs_6_) | copy-start | bytes 3145732
  81.9 16.8 %collective-permute-start.1 = (f32[8,128,128]{2,1,0:T(8,128)S(1)}, f32[8,128,128]{2,1,0:T(8,128)S(1)}, u32[]{:S(2)}, u32[]{:S(2)}) collective-permute-start(f32[8,128,128]{2,1,0:T(8,128)S(1)} %get-tuple-element.19.refs_0_), channel_id=1, source_target_pairs={{1,0},{2,3},{128,1},{3,130},{129,128},{130,131},{161,129},{131,163... | collective-permute-start | bytes 1572872 | tf_op jit(solution)/shard_map/ppermute | solution.py:565
  84.1 21.1 %collective-permute-start.2 = (f32[8,128,128]{2,1,0:T(8,128)S(1)}, f32[8,128,128]{2,1,0:T(8,128)S(1)}, u32[]{:S(2)}, u32[]{:S(2)}) collective-permute-start(f32[8,128,128]{2,1,0:T(8,128)S(1)} %get-tuple-element.20), channel_id=1, source_target_pairs={{1,2},{2,1},{128,3},{3,128},{129,130},{130,129},{161,131},{131,161... | collective-permute-start | bytes 1572872 | tf_op jit(solution)/shard_map/ppermute | solution.py:566
  88.0 17.2 %collective-permute-start = (f32[8,128,128]{2,1,0:T(8,128)S(1)}, f32[8,128,128]{2,1,0:T(8,128)S(1)}, u32[]{:S(2)}, u32[]{:S(2)}) collective-permute-start(f32[8,128,128]{2,1,0:T(8,128)S(1)} %get-tuple-element.20), channel_id=1, source_target_pairs={{0,2},{2,0},{1,3},{3,1},{128,130},{130,128},{129,131},{131,129},{1... | collective-permute-start | bytes 1572872 | tf_op jit(solution)/shard_map/ppermute | solution.py:564
  96.4 15.7 %collective-permute-start.10 = (f32[8,128,128]{2,1,0:T(8,128)S(1)}, f32[8,128,128]{2,1,0:T(8,128)S(1)}, u32[]{:S(2)}, u32[]{:S(2)}) collective-permute-start(f32[8,128,128]{2,1,0:T(8,128)S(1)} %get-tuple-element.28), channel_id=1, source_target_pairs={{0,1},{3,2},{1,128},{130,3},{128,129},{131,130},{129,161},{163,131... | collective-permute-start | bytes 1572872 | tf_op jit(solution)/shard_map/ppermute | solution.py:572
  97.7 17.9 %collective-permute-start.11 = (f32[8,128,128]{2,1,0:T(8,128)S(1)}, f32[8,128,128]{2,1,0:T(8,128)S(1)}, u32[]{:S(2)}, u32[]{:S(2)}) collective-permute-start(f32[8,128,128]{2,1,0:T(8,128)S(1)} %get-tuple-element.29), channel_id=1, source_target_pairs={{0,2},{2,0},{1,3},{3,1},{128,130},{130,128},{129,131},{131,129},{1... | collective-permute-start | bytes 1572872 | tf_op jit(solution)/shard_map/ppermute | solution.py:571
  98.7 16.9 %copy-start.1 = (bf16[32,128,384]{2,1,0:T(8,128)(2,1)S(1)}, bf16[32,128,384]{2,1,0:T(8,128)(2,1)}, u32[]{:S(2)}) copy-start(bf16[32,128,384]{2,1,0:T(8,128)(2,1)} %constant.9.clone.inv_ref) | copy-start | bytes 9437188
  98.7 16.9 %collective-permute-start.12 = (f32[8,128,128]{2,1,0:T(8,128)S(1)}, f32[8,128,128]{2,1,0:T(8,128)S(1)}, u32[]{:S(2)}, u32[]{:S(2)}) collective-permute-start(f32[8,128,128]{2,1,0:T(8,128)S(1)} %get-tuple-element.30), channel_id=1, source_target_pairs={{2,1},{1,2},{3,128},{128,3},{130,129},{129,130},{131,161},{161,131... | collective-permute-start | bytes 1572872 | tf_op jit(solution)/shard_map/ppermute | solution.py:573
  109.8 12.8 %collective-permute-start.4 = (f32[8,128,128]{2,1,0:T(8,128)S(1)}, f32[8,128,128]{2,1,0:T(8,128)S(1)}, u32[]{:S(2)}, u32[]{:S(2)}) collective-permute-start(f32[8,128,128]{2,1,0:T(8,128)S(1)} %get-tuple-element.22), channel_id=1, source_target_pairs={{0,1},{3,2},{1,128},{130,3},{128,129},{131,130},{129,161},{163,131... | collective-permute-start | bytes 1572872 | tf_op jit(solution)/shard_map/ppermute | solution.py:572
  111.1 11.5 %collective-permute-start.5 = (f32[8,128,128]{2,1,0:T(8,128)S(1)}, f32[8,128,128]{2,1,0:T(8,128)S(1)}, u32[]{:S(2)}, u32[]{:S(2)}) collective-permute-start(f32[8,128,128]{2,1,0:T(8,128)S(1)} %get-tuple-element.23), channel_id=1, source_target_pairs={{0,2},{2,0},{1,3},{3,1},{128,130},{130,128},{129,131},{131,129},{1... | collective-permute-start | bytes 1572872 | tf_op jit(solution)/shard_map/ppermute | solution.py:571
  112.1 13.4 %collective-permute-start.6 = (f32[8,128,128]{2,1,0:T(8,128)S(1)}, f32[8,128,128]{2,1,0:T(8,128)S(1)}, u32[]{:S(2)}, u32[]{:S(2)}) collective-permute-start(f32[8,128,128]{2,1,0:T(8,128)S(1)} %get-tuple-element.24), channel_id=1, source_target_pairs={{2,1},{1,2},{3,128},{128,3},{130,129},{129,130},{131,161},{161,131... | collective-permute-start | bytes 1572872 | tf_op jit(solution)/shard_map/ppermute | solution.py:573

commit v7 on v6

--- a/solution.py
+++ b/solution.py
@@ -217,14 +217,23 @@
     )(taps.reshape(1, TAPS), raw)
 
 
-def unplane_kernel(in_ref, out_ref):
+def unplane_kernel(in_ref, out_ref, stage_ref, sems):
     planes = in_ref.shape[2]
+    pair = 2
+    stores = []
     for plane in range(planes):
         for b in range(32):
             xh, row, core, xl = plane_slot(b)
             y = row if plane % 2 == 0 else 3 - row
             start = (plane * 32 + b) * BLK
-            out_ref[:, start : start + BLK] = in_ref[xh, y, plane, core, xl]
+            stage_ref[:, start : start + BLK] = in_ref[xh, y, plane, core, xl]
+        if plane % pair == pair - 1:
+            part = pl.ds((plane + 1 - pair) * 32 * BLK, pair * 32 * BLK)
+            store = pltpu.make_async_copy(stage_ref.at[:, part], out_ref.at[:, part], sems.at[plane // pair])
+            store.start()
+            stores.append(store)
+    for store in stores:
+        store.wait()
 
 
 def unplane(blocks):
@@ -233,8 +242,12 @@
     return pl.pallas_call(
         unplane_kernel,
         in_specs=[VMEM],
-        out_specs=VMEM,
+        out_specs=ANY,
         out_shape=jax.ShapeDtypeStruct((channels, planes * 32 * BLK), F32),
+        scratch_shapes=[
+            pltpu.VMEM((channels, planes * 32 * BLK), F32),
+            pltpu.SemaphoreType.DMA((planes // 2,)),
+        ],
         compiler_params=params(8),
         name="unplane",
     )(blocks)
@@ -465,11 +478,10 @@
     )(band_gain, fan_band)
 
 
-def time_kernel(first_chunk, *refs):
+def time_kernel(chunk, *refs):
     own_ref, part_ref, same_ref, cross_ref, mine_ref, theirs_ref, fwd_ref, bwd_ref = refs[:8]
     out_refs = refs[8:]
     core, xl = core_index(), lax.axis_index("tile")
-    step = pl.program_id(0)
     slots = own_ref.shape[0]
     rows = slots * BLK
     even = core == 0
@@ -498,16 +510,17 @@
         c, b = q[:, :BINS], q[:, BINS:]
 
         def wide(kind):
-            mine, theirs = mine_ref[kind, s], theirs_ref[kind, s]
+            place = chunk * WIDTH + s
+            mine, theirs = mine_ref[kind, place], theirs_ref[kind, place]
             low = jnp.where(xl == 0, mine, theirs)
             high = jnp.where(xl == 0, theirs, mine)
             return jnp.concatenate([low, high], axis=1)
 
         gs, gd = wide(0), wide(1)
         gr = gi = gs
-        if s == 0 and first_chunk:
+        if s == 0 and chunk == 0:
             row = lax.broadcasted_iota(jnp.int32, (ROOT, BINS), 0)
-            pair = (row == 0) & (step == 0) & even
+            pair = (row == 0) & even
             gr = jnp.where(pair, gs + gd, gs)
             gi = jnp.where(pair, gs - gd, gs)
             gd = jnp.where(pair, 0.0, gd)
@@ -528,18 +541,12 @@
 
 
 def time_filter(chunk, waves, mine, theirs, fwd, bwd):
-    slots = 8
-    steps = WIDTH // slots
-    data = pl.BlockSpec((slots, BLK, BLK), lambda g: (g, 0, 0))
-    gain = pl.BlockSpec((2, slots, ROOT, BLK), lambda g: (0, chunk * steps + g, 0, 0))
-    table = pl.BlockSpec((2, WIN, WIN), lambda g: (0, 0, 0))
-    return pl.pallas_call(
-        functools.partial(time_kernel, chunk == 0),
-        grid=(steps,),
-        in_specs=[data] * 4 + [gain] * 2 + [table] * 2,
-        out_specs=[data] * 4,
-        out_shape=[jax.ShapeDtypeStruct((WIDTH, BLK, BLK), F32)] * 4,
-        compiler_params=params(24),
+    return pl.pallas_call(
+        functools.partial(time_kernel, chunk),
+        in_specs=[VMEM] * 8,
+        out_specs=[VMEM] * 4,
+        out_shape=[WAVE] * 4,
+        compiler_params=params(28),
         name="time_filter",
     )(*waves, mine, theirs, fwd, bwd)
 

time: 188 us -> 189 us (level)
  transfers between devices with their start and end apart: 14 -> 14, of which waited for: 5 -> 6; matrix products, arithmetic and copies ran while one was open for 0% -> 0% of each run, Pallas kernels for 9% -> 9%
where the time goes in v7:
time: 189 us; the launch traced here: 188 us
  waiting for transfers between devices  60.1 us (32%)
  blocking collectives  59.9 us (32%)
  starting transfers between devices  42.5 us (22%)
  Pallas kernels  24 us (13%)
    all_to_all x1, blocking collectives, body(): lax.all_to_all(filtered.reshape(256, 16, BLK), AXES, 0, 0, tiled=True)  59.9 us
    all_to_all x1, waiting for transfers between devices, body(): blocks = lax.all_to_all(blocks, AXES, 0, 0, tiled=True)  45 us
    all_to_all x1, starting transfers between devices, body(): blocks = lax.all_to_all(blocks, AXES, 0, 0, tiled=True)  16.7 us
    pallas_call x2, Pallas kernels, time_filter(): pl.pallas_call(functools.partial(time_kernel, chunk), in_specs=[VMEM] * 8...  9.99 us
    ppermute x2, starting transfers between devices, body(): from_cross = lax.ppermute(other, AXES, cross)  8.58 us
    ppermute x2, starting transfers between devices, body(): back_cross = lax.ppermute(far, AXES, flipped(cross))  7.17 us
    ppermute x2, waiting for transfers between devices, body(): back_same = lax.ppermute(halo, AXES, flipped(same))  6.44 us
    ppermute x2, waiting for transfers between devices, body(): from_cross = lax.ppermute(other, AXES, cross)  5.5 us
  transfers between devices with their start and end apart: 14, of which 6 were waited for; matrix products, arithmetic and copies ran while one was open for 0% of the time, Pallas kernels for 9%

profile of v7, /device:TPU:1, one launch (start us, length us, event | category | flops | bytes accessed | tf_op | source)
XLA Modules:
  0.0 188.5 jit_solution(929754459417820939)
XLA Ops:
  0.0 4.2 %decimate.1 = f32[2,4,8,2,2,16,128]{6,5,4,3,2,1,0:T(8,128)} custom-call(bf16[1,128]{1,0:T(2,128)(2,1)} %bitcast.8, bf16[16,131072]{1,0:T(8,128)(2,1)} %raw_ref.1), custom_call_target="tpu_custom_call" | custom-call | tf_op jit(solution)/shard_map/decimate/pallas_call | solution.py:202
  4.2 16.7 %all-to-all-start = ((f32[256,16,128]{2,1,0:T(8,128)}), f32[256,16,128]{2,1,0:T(8,128)}, u32[]{:S(2)}, u32[]{:S(2)}) async-start(f32[256,16,128]{2,1,0:T(8,128)} %bitcast.7), calls=%async_computation | async-start | bytes 4194304 | tf_op jit(solution)/shard_map/all_to_all | solution.py:565
  20.9 1.6 copy-done.4
  22.5 2.9 %gains.1.refs_4_ = f32[2,16,64,128]{3,2,1,0:T(8,128)} custom-call(f32[8]{0:T(128)S(1)} %copy-done.5, s32[4096,128]{1,0:T(8,128)S(1)} %copy-done.4), custom_call_target="tpu_custom_call" | custom-call | tf_op jit(solution)/shard_map/gains/pallas_call | solution.py:471
  25.4 1.4 collective-permute-start.3
  26.8 45.0 %all-to-all-done = f32[256,16,128]{2,1,0:T(8,128)} async-done(((f32[256,16,128]{2,1,0:T(8,128)}), f32[256,16,128]{2,1,0:T(8,128)}, u32[]{:S(2)}, u32[]{:S(2)}) %all-to-all-start) | async-done | bytes 2097184 | tf_op jit(solution)/shard_map/all_to_all | solution.py:565
  71.8 2.8 %forward_space.1 = (f32[8,128,128]{2,1,0:T(8,128)S(1)}, f32[8,128,128]{2,1,0:T(8,128)S(1)}, f32[32,128,128]{2,1,0:T(8,128)S(1)}) custom-call(f32[64,64,128]{2,1,0:T(8,128)} %bitcast.2.x_hbm, bf16[32,128,384]{2,1,0:T(8,128)(2,1)S(1)} %copy-done), custom_call_target="tpu_custom_call" | custom-call | tf_op jit(solution)/shard_map/forward_space/pallas_call | solution.py:341
  74.6 1.9 %collective-permute-start.8 = (f32[8,128,128]{2,1,0:T(8,128)S(1)}, f32[8,128,128]{2,1,0:T(8,128)S(1)}, u32[]{:S(2)}, u32[]{:S(2)}) collective-permute-start(f32[8,128,128]{2,1,0:T(8,128)S(1)} %get-tuple-element.25.refs_0_), channel_id=1, source_target_pairs={{1,0},{2,3},{128,1},{3,130},{129,128},{130,131},{161,129},{131,163... | collective-permute-start | bytes 1572872 | tf_op jit(solution)/shard_map/ppermute | solution.py:572
  76.5 4.7 %collective-permute-start.9 = (f32[8,128,128]{2,1,0:T(8,128)S(1)}, f32[8,128,128]{2,1,0:T(8,128)S(1)}, u32[]{:S(2)}, u32[]{:S(2)}) collective-permute-start(f32[8,128,128]{2,1,0:T(8,128)S(1)} %get-tuple-element.26), channel_id=1, source_target_pairs={{1,2},{2,1},{128,3},{3,128},{129,130},{130,129},{161,131},{131,161... | collective-permute-start | bytes 1572872 | tf_op jit(solution)/shard_map/ppermute | solution.py:573
  81.9 2.1 %collective-permute-start.1 = (f32[8,128,128]{2,1,0:T(8,128)S(1)}, f32[8,128,128]{2,1,0:T(8,128)S(1)}, u32[]{:S(2)}, u32[]{:S(2)}) collective-permute-start(f32[8,128,128]{2,1,0:T(8,128)S(1)} %get-tuple-element.19.refs_0_), channel_id=1, source_target_pairs={{1,0},{2,3},{128,1},{3,130},{129,128},{130,131},{161,129},{131,163... | collective-permute-start | bytes 1572872 | tf_op jit(solution)/shard_map/ppermute | solution.py:572
  84.1 3.9 %collective-permute-start.2 = (f32[8,128,128]{2,1,0:T(8,128)S(1)}, f32[8,128,128]{2,1,0:T(8,128)S(1)}, u32[]{:S(2)}, u32[]{:S(2)}) collective-permute-start(f32[8,128,128]{2,1,0:T(8,128)S(1)} %get-tuple-element.20), channel_id=1, source_target_pairs={{1,2},{2,1},{128,3},{3,128},{129,130},{130,129},{161,131},{131,161... | collective-permute-start | bytes 1572872 | tf_op jit(solution)/shard_map/ppermute | solution.py:573
  88.1 3.7 %collective-permute-done.9.refs_3_ = f32[8,128,128]{2,1,0:T(8,128)S(1)} collective-permute-done((f32[8,128,128]{2,1,0:T(8,128)S(1)}, f32[8,128,128]{2,1,0:T(8,128)S(1)}, u32[]{:S(2)}, u32[]{:S(2)}) %collective-permute-start.9) | collective-permute-done | bytes 524320 | tf_op jit(solution)/shard_map/ppermute | solution.py:573
  91.8 5.0 %time_filter.3 = (f32[8,128,128]{2,1,0:T(8,128)S(1)}, f32[8,128,128]{2,1,0:T(8,128)S(1)}, f32[8,128,128]{2,1,0:T(8,128)S(1)}, f32[8,128,128]{2,1,0:T(8,128)S(1)}) custom-call(f32[8,128,128]{2,1,0:T(8,128)S(1)} %get-tuple-element.25.refs_0_, f32[8,128,128]{2,1,0:T(8,128)S(1)} %collective-permute-done.7.refs_1_, ...), custom_call_target="tpu_custom_call" | custom-call | tf_op jit(solution)/shard_map/time_filter/pallas_call | solution.py:544
  96.8 1.3 collective-permute-start.10
  99.0 3.9 %collective-permute-start.12 = (f32[8,128,128]{2,1,0:T(8,128)S(1)}, f32[8,128,128]{2,1,0:T(8,128)S(1)}, u32[]{:S(2)}, u32[]{:S(2)}) collective-permute-start(f32[8,128,128]{2,1,0:T(8,128)S(1)} %get-tuple-element.30), channel_id=1, source_target_pairs={{2,1},{1,2},{3,128},{128,3},{130,129},{129,130},{131,161},{161,131... | collective-permute-start | bytes 1572872 | tf_op jit(solution)/shard_map/ppermute | solution.py:580
  103.0 1.8 collective-permute-done.2.refs_3_
  104.8 5.0 %time_filter.2 = (f32[8,128,128]{2,1,0:T(8,128)S(1)}, f32[8,128,128]{2,1,0:T(8,128)S(1)}, f32[8,128,128]{2,1,0:T(8,128)S(1)}, f32[8,128,128]{2,1,0:T(8,128)S(1)}) custom-call(f32[8,128,128]{2,1,0:T(8,128)S(1)} %get-tuple-element.19.refs_0_, f32[8,128,128]{2,1,0:T(8,128)S(1)} %collective-permute-done.refs_1_, ...), custom_call_target="tpu_custom_call" | custom-call | tf_op jit(solution)/shard_map/time_filter/pallas_call | solution.py:544
  109.8 1.3 collective-permute-start.4
  112.4 3.2 %collective-permute-start.6 = (f32[8,128,128]{2,1,0:T(8,128)S(1)}, f32[8,128,128]{2,1,0:T(8,128)S(1)}, u32[]{:S(2)}, u32[]{:S(2)}) collective-permute-start(f32[8,128,128]{2,1,0:T(8,128)S(1)} %get-tuple-element.24), channel_id=1, source_target_pairs={{2,1},{1,2},{3,128},{128,3},{130,129},{129,130},{131,161},{161,131... | collective-permute-start | bytes 1572872 | tf_op jit(solution)/shard_map/ppermute | solution.py:580
  116.2 6.2 %collective-permute-done.4.halo_ref = f32[8,128,128]{2,1,0:T(8,128)S(1)} collective-permute-done((f32[8,128,128]{2,1,0:T(8,128)S(1)}, f32[8,128,128]{2,1,0:T(8,128)S(1)}, u32[]{:S(2)}, u32[]{:S(2)}) %collective-permute-start.4) | collective-permute-done | bytes 524320 | tf_op jit(solution)/shard_map/ppermute | solution.py:579
  122.4 3.1 %collective-permute-done.6.cross_ref = f32[8,128,128]{2,1,0:T(8,128)S(1)} collective-permute-done((f32[8,128,128]{2,1,0:T(8,128)S(1)}, f32[8,128,128]{2,1,0:T(8,128)S(1)}, u32[]{:S(2)}, u32[]{:S(2)}) %collective-permute-start.6) | collective-permute-done | bytes 524320 | tf_op jit(solution)/shard_map/ppermute | solution.py:580
  125.5 1.6 inverse_space.1
  127.1 59.9 %all_to_all.10 = f32[256,16,128]{2,1,0:T(8,128)S(1)} all-to-all(f32[256,16,128]{2,1,0:T(8,128)S(1)} %bitcast.6), channel_id=1, replica_groups=mesh['chan'=128,'tile'=2] {'chan','tile'}, dimensions={0} | all-to-all | bytes 4194304 | tf_op jit(solution)/shard_map/all_to_all | solution.py:584
  187.0 1.4 unplane.1
  (26 shorter events, 3.6 us)
Async XLA Ops:
  4.2 16.7 %copy-start.5 = (f32[8]{0:T(128)S(1)}, f32[8]{0:T(128)}, u32[]{:S(2)}) copy-start(f32[8]{0:T(128)} %gain_ref.1) | copy-start | bytes 100
  4.2 67.6 %all-to-all-start = ((f32[256,16,128]{2,1,0:T(8,128)}), f32[256,16,128]{2,1,0:T(8,128)}, u32[]{:S(2)}, u32[]{:S(2)}) async-start(f32[256,16,128]{2,1,0:T(8,128)} %bitcast.7), calls=%async_computation | async-start | bytes 4194304 | tf_op jit(solution)/shard_map/all_to_all | solution.py:565
  20.9 1.6 copy-start.4
  22.4 49.4 %copy-start = (bf16[32,128,384]{2,1,0:T(8,128)(2,1)S(1)}, bf16[32,128,384]{2,1,0:T(8,128)(2,1)}, u32[]{:S(2)}) copy-start(bf16[32,128,384]{2,1,0:T(8,128)(2,1)} %constant.8.clone.second_ref) | copy-start | bytes 9437188
  25.4 58.7 %collective-permute-start.3 = (f32[2,16,64,128]{3,2,1,0:T(8,128)}, f32[2,16,64,128]{3,2,1,0:T(8,128)}, u32[]{:S(2)}, u32[]{:S(2)}) collective-permute-start(f32[2,16,64,128]{3,2,1,0:T(8,128)} %gains.1.refs_4_), channel_id=1, source_target_pairs={{0,1},{1,0},{2,3},{3,2},{4,5},{5,4},{6,7},{7,6},{8,9},{9,8},{10,11... | collective-permute-start | bytes 3145736 | tf_op jit(solution)/shard_map/ppermute | solution.py:560
  74.6 13.4 %collective-permute-start.8 = (f32[8,128,128]{2,1,0:T(8,128)S(1)}, f32[8,128,128]{2,1,0:T(8,128)S(1)}, u32[]{:S(2)}, u32[]{:S(2)}) collective-permute-start(f32[8,128,128]{2,1,0:T(8,128)S(1)} %get-tuple-element.25.refs_0_), channel_id=1, source_target_pairs={{1,0},{2,3},{128,1},{3,130},{129,128},{130,131},{161,129},{131,163... | collective-permute-start | bytes 1572872 | tf_op jit(solution)/shard_map/ppermute | solution.py:572
  76.5 15.2 %collective-permute-start.9 = (f32[8,128,128]{2,1,0:T(8,128)S(1)}, f32[8,128,128]{2,1,0:T(8,128)S(1)}, u32[]{:S(2)}, u32[]{:S(2)}) collective-permute-start(f32[8,128,128]{2,1,0:T(8,128)S(1)} %get-tuple-element.26), channel_id=1, source_target_pairs={{1,2},{2,1},{128,3},{3,128},{129,130},{130,129},{161,131},{131,161... | collective-permute-start | bytes 1572872 | tf_op jit(solution)/shard_map/ppermute | solution.py:573
  81.2 10.5 %collective-permute-start.7 = (f32[8,128,128]{2,1,0:T(8,128)S(1)}, f32[8,128,128]{2,1,0:T(8,128)S(1)}, u32[]{:S(2)}, u32[]{:S(2)}) collective-permute-start(f32[8,128,128]{2,1,0:T(8,128)S(1)} %get-tuple-element.26), channel_id=1, source_target_pairs={{0,2},{2,0},{1,3},{3,1},{128,130},{130,128},{129,131},{131,129},{1... | collective-permute-start | bytes 1572872 | tf_op jit(solution)/shard_map/ppermute | solution.py:571
  81.3 10.4 %copy-start.2 = (bf16[2,512,512]{2,1,0:T(8,128)(2,1)S(1)}, bf16[2,512,512]{2,1,0:T(8,128)(2,1)}, u32[]{:S(2)}) copy-start(bf16[2,512,512]{2,1,0:T(8,128)(2,1)} %constant.11.clone.refs_7_) | copy-start | bytes 3145732
  81.3 10.4 %copy-start.3 = (bf16[2,512,512]{2,1,0:T(8,128)(2,1)S(1)}, bf16[2,512,512]{2,1,0:T(8,128)(2,1)}, u32[]{:S(2)}) copy-start(bf16[2,512,512]{2,1,0:T(8,128)(2,1)} %constant.10.clone.refs_6_) | copy-start | bytes 3145732
  81.9 17.1 %collective-permute-start.1 = (f32[8,128,128]{2,1,0:T(8,128)S(1)}, f32[8,128,128]{2,1,0:T(8,128)S(1)}, u32[]{:S(2)}, u32[]{:S(2)}) collective-permute-start(f32[8,128,128]{2,1,0:T(8,128)S(1)} %get-tuple-element.19.refs_0_), channel_id=1, source_target_pairs={{1,0},{2,3},{128,1},{3,130},{129,128},{130,131},{161,129},{131,163... | collective-permute-start | bytes 1572872 | tf_op jit(solution)/shard_map/ppermute | solution.py:572
  84.1 20.7 %collective-permute-start.2 = (f32[8,128,128]{2,1,0:T(8,128)S(1)}, f32[8,128,128]{2,1,0:T(8,128)S(1)}, u32[]{:S(2)}, u32[]{:S(2)}) collective-permute-start(f32[8,128,128]{2,1,0:T(8,128)S(1)} %get-tuple-element.20), channel_id=1, source_target_pairs={{1,2},{2,1},{128,3},{3,128},{129,130},{130,129},{161,131},{131,161... | collective-permute-start | bytes 1572872 | tf_op jit(solution)/shard_map/ppermute | solution.py:573
  88.0 16.8 %collective-permute-start = (f32[8,128,128]{2,1,0:T(8,128)S(1)}, f32[8,128,128]{2,1,0:T(8,128)S(1)}, u32[]{:S(2)}, u32[]{:S(2)}) collective-permute-start(f32[8,128,128]{2,1,0:T(8,128)S(1)} %get-tuple-element.20), channel_id=1, source_target_pairs={{0,2},{2,0},{1,3},{3,1},{128,130},{130,128},{129,131},{131,129},{1... | collective-permute-start | bytes 1572872 | tf_op jit(solution)/shard_map/ppermute | solution.py:571
  96.8 15.6 %collective-permute-start.10 = (f32[8,128,128]{2,1,0:T(8,128)S(1)}, f32[8,128,128]{2,1,0:T(8,128)S(1)}, u32[]{:S(2)}, u32[]{:S(2)}) collective-permute-start(f32[8,128,128]{2,1,0:T(8,128)S(1)} %get-tuple-element.28), channel_id=1, source_target_pairs={{0,1},{3,2},{1,128},{130,3},{128,129},{131,130},{129,161},{163,131... | collective-permute-start | bytes 1572872 | tf_op jit(solution)/shard_map/ppermute | solution.py:579
  98.1 17.5 %collective-permute-start.11 = (f32[8,128,128]{2,1,0:T(8,128)S(1)}, f32[8,128,128]{2,1,0:T(8,128)S(1)}, u32[]{:S(2)}, u32[]{:S(2)}) collective-permute-start(f32[8,128,128]{2,1,0:T(8,128)S(1)} %get-tuple-element.29), channel_id=1, source_target_pairs={{0,2},{2,0},{1,3},{3,1},{128,130},{130,128},{129,131},{131,129},{1... | collective-permute-start | bytes 1572872 | tf_op jit(solution)/shard_map/ppermute | solution.py:578
  99.0 16.6 %copy-start.1 = (bf16[32,128,384]{2,1,0:T(8,128)(2,1)S(1)}, bf16[32,128,384]{2,1,0:T(8,128)(2,1)}, u32[]{:S(2)}) copy-start(bf16[32,128,384]{2,1,0:T(8,128)(2,1)} %constant.9.clone.inv_ref) | copy-start | bytes 9437188
  99.0 16.6 %collective-permute-start.12 = (f32[8,128,128]{2,1,0:T(8,128)S(1)}, f32[8,128,128]{2,1,0:T(8,128)S(1)}, u32[]{:S(2)}, u32[]{:S(2)}) collective-permute-start(f32[8,128,128]{2,1,0:T(8,128)S(1)} %get-tuple-element.30), channel_id=1, source_target_pairs={{2,1},{1,2},{3,128},{128,3},{130,129},{129,130},{131,161},{161,131... | collective-permute-start | bytes 1572872 | tf_op jit(solution)/shard_map/ppermute | solution.py:580
  109.8 12.5 %collective-permute-start.4 = (f32[8,128,128]{2,1,0:T(8,128)S(1)}, f32[8,128,128]{2,1,0:T(8,128)S(1)}, u32[]{:S(2)}, u32[]{:S(2)}) collective-permute-start(f32[8,128,128]{2,1,0:T(8,128)S(1)} %get-tuple-element.22), channel_id=1, source_target_pairs={{0,1},{3,2},{1,128},{130,3},{128,129},{131,130},{129,161},{163,131... | collective-permute-start | bytes 1572872 | tf_op jit(solution)/shard_map/ppermute | solution.py:579
  111.1 11.2 %collective-permute-start.5 = (f32[8,128,128]{2,1,0:T(8,128)S(1)}, f32[8,128,128]{2,1,0:T(8,128)S(1)}, u32[]{:S(2)}, u32[]{:S(2)}) collective-permute-start(f32[8,128,128]{2,1,0:T(8,128)S(1)} %get-tuple-element.23), channel_id=1, source_target_pairs={{0,2},{2,0},{1,3},{3,1},{128,130},{130,128},{129,131},{131,129},{1... | collective-permute-start | bytes 1572872 | tf_op jit(solution)/shard_map/ppermute | solution.py:578
  112.4 13.1 %collective-permute-start.6 = (f32[8,128,128]{2,1,0:T(8,128)S(1)}, f32[8,128,128]{2,1,0:T(8,128)S(1)}, u32[]{:S(2)}, u32[]{:S(2)}) collective-permute-start(f32[8,128,128]{2,1,0:T(8,128)S(1)} %get-tuple-element.24), channel_id=1, source_target_pairs={{2,1},{1,2},{3,128},{128,3},{130,129},{129,130},{131,161},{161,131... | collective-permute-start | bytes 1572872 | tf_op jit(solution)/shard_map/ppermute | solution.py:580

commit v8 on v6

--- a/solution.py
+++ b/solution.py
@@ -217,14 +217,23 @@
     )(taps.reshape(1, TAPS), raw)
 
 
-def unplane_kernel(in_ref, out_ref):
+def unplane_kernel(in_ref, out_ref, stage_ref, sems):
     planes = in_ref.shape[2]
+    pair = 2
+    stores = []
     for plane in range(planes):
         for b in range(32):
             xh, row, core, xl = plane_slot(b)
             y = row if plane % 2 == 0 else 3 - row
             start = (plane * 32 + b) * BLK
-            out_ref[:, start : start + BLK] = in_ref[xh, y, plane, core, xl]
+            stage_ref[:, start : start + BLK] = in_ref[xh, y, plane, core, xl]
+        if plane % pair == pair - 1:
+            part = pl.ds((plane + 1 - pair) * 32 * BLK, pair * 32 * BLK)
+            store = pltpu.make_async_copy(stage_ref.at[:, part], out_ref.at[:, part], sems.at[plane // pair])
+            store.start()
+            stores.append(store)
+    for store in stores:
+        store.wait()
 
 
 def unplane(blocks):
@@ -233,8 +242,12 @@
     return pl.pallas_call(
         unplane_kernel,
         in_specs=[VMEM],
-        out_specs=VMEM,
+        out_specs=ANY,
         out_shape=jax.ShapeDtypeStruct((channels, planes * 32 * BLK), F32),
+        scratch_shapes=[
+            pltpu.VMEM((channels, planes * 32 * BLK), F32),
+            pltpu.SemaphoreType.DMA((planes // 2,)),
+        ],
         compiler_params=params(8),
         name="unplane",
     )(blocks)
@@ -320,7 +333,7 @@
 
     for n in range(2):
         loads[n].wait()
-        lax.fori_loop(n * half // 8, (n + 1) * half // 8, tile, 0)
+        lax.fori_loop(n * half // 8, (n + 1) * half // 8, tile, 0, unroll=2)
     second_stage(core_index(), 0, mid_ref, second_ref, own_ref, other_ref)
 
 
@@ -396,7 +409,7 @@
             out_ref[c1, rows, :] = values[c1]
         return carry
 
-    lax.fori_loop(0, ROOT // 8, tile, 0)
+    lax.fori_loop(0, ROOT // 8, tile, 0, unroll=2)
 
 
 def inverse_space(waves, earlier, inv):

time: 188 us -> 188 us (level)
  no operation moved by 1% of the time
where the time goes in v8:
time: 188 us
  waiting for transfers between devices  60.5 us (32%)
  blocking collectives  59.2 us (31%)
  starting transfers between devices  42.8 us (23%)
  Pallas kernels  23.3 us (12%)
    all_to_all x1, blocking collectives, body(): lax.all_to_all(filtered.reshape(256, 16, BLK), AXES, 0, 0, tiled=True)  59.2 us
    all_to_all x1, waiting for transfers between devices, body(): blocks = lax.all_to_all(blocks, AXES, 0, 0, tiled=True)  45 us
    all_to_all x1, starting transfers between devices, body(): blocks = lax.all_to_all(blocks, AXES, 0, 0, tiled=True)  16.7 us
    pallas_call x2, Pallas kernels, time_filter(): pl.pallas_call(functools.partial(time_kernel, chunk == 0), grid=(steps,),...  9.32 us
    ppermute x2, starting transfers between devices, body(): from_cross = lax.ppermute(other, AXES, cross)  8.58 us
    ppermute x2, starting transfers between devices, body(): back_cross = lax.ppermute(far, AXES, flipped(cross))  7.45 us
    ppermute x2, waiting for transfers between devices, body(): back_same = lax.ppermute(halo, AXES, flipped(same))  6.46 us
    ppermute x2, waiting for transfers between devices, body(): from_cross = lax.ppermute(other, AXES, cross)  6.16 us
  transfers between devices with their start and end apart: 14, of which 5 were waited for; matrix products, arithmetic and copies ran while one was open for 0% of the time, Pallas kernels for 9%

profile of v8, /device:TPU:1, one launch (start us, length us, event | category | flops | bytes accessed | tf_op | source)
XLA Modules:
  0.0 187.8 jit_solution(4123062956250089897)
XLA Ops:
  0.0 4.2 %decimate.1 = f32[2,4,8,2,2,16,128]{6,5,4,3,2,1,0:T(8,128)} custom-call(bf16[1,128]{1,0:T(2,128)(2,1)} %bitcast.8, bf16[16,131072]{1,0:T(8,128)(2,1)} %raw_ref.1), custom_call_target="tpu_custom_call" | custom-call | tf_op jit(solution)/shard_map/decimate/pallas_call | solution.py:202
  4.2 16.7 %all-to-all-start = ((f32[256,16,128]{2,1,0:T(8,128)}), f32[256,16,128]{2,1,0:T(8,128)}, u32[]{:S(2)}, u32[]{:S(2)}) async-start(f32[256,16,128]{2,1,0:T(8,128)} %bitcast.7), calls=%async_computation | async-start | bytes 4194304 | tf_op jit(solution)/shard_map/all_to_all | solution.py:571
  20.9 1.6 copy-done.4
  22.5 2.9 %gains.1.refs_4_ = f32[2,16,64,128]{3,2,1,0:T(8,128)} custom-call(f32[8]{0:T(128)S(1)} %copy-done.5, s32[4096,128]{1,0:T(8,128)S(1)} %copy-done.4), custom_call_target="tpu_custom_call" | custom-call | tf_op jit(solution)/shard_map/gains/pallas_call | solution.py:471
  25.4 1.4 collective-permute-start.3
  26.8 45.0 %all-to-all-done = f32[256,16,128]{2,1,0:T(8,128)} async-done(((f32[256,16,128]{2,1,0:T(8,128)}), f32[256,16,128]{2,1,0:T(8,128)}, u32[]{:S(2)}, u32[]{:S(2)}) %all-to-all-start) | async-done | bytes 2097184 | tf_op jit(solution)/shard_map/all_to_all | solution.py:571
  71.8 2.8 %forward_space.1 = (f32[8,128,128]{2,1,0:T(8,128)S(1)}, f32[8,128,128]{2,1,0:T(8,128)S(1)}, f32[32,128,128]{2,1,0:T(8,128)S(1)}) custom-call(f32[64,64,128]{2,1,0:T(8,128)} %bitcast.2.x_hbm, bf16[32,128,384]{2,1,0:T(8,128)(2,1)S(1)} %copy-done), custom_call_target="tpu_custom_call" | custom-call | tf_op jit(solution)/shard_map/forward_space/pallas_call | solution.py:341
  74.6 1.9 %collective-permute-start.8 = (f32[8,128,128]{2,1,0:T(8,128)S(1)}, f32[8,128,128]{2,1,0:T(8,128)S(1)}, u32[]{:S(2)}, u32[]{:S(2)}) collective-permute-start(f32[8,128,128]{2,1,0:T(8,128)S(1)} %get-tuple-element.25.refs_0_), channel_id=1, source_target_pairs={{1,0},{2,3},{128,1},{3,130},{129,128},{130,131},{161,129},{131,163... | collective-permute-start | bytes 1572872 | tf_op jit(solution)/shard_map/ppermute | solution.py:578
  76.5 4.7 %collective-permute-start.9 = (f32[8,128,128]{2,1,0:T(8,128)S(1)}, f32[8,128,128]{2,1,0:T(8,128)S(1)}, u32[]{:S(2)}, u32[]{:S(2)}) collective-permute-start(f32[8,128,128]{2,1,0:T(8,128)S(1)} %get-tuple-element.26), channel_id=1, source_target_pairs={{1,2},{2,1},{128,3},{3,128},{129,130},{130,129},{161,131},{131,161... | collective-permute-start | bytes 1572872 | tf_op jit(solution)/shard_map/ppermute | solution.py:579
  81.9 2.1 %collective-permute-start.1 = (f32[8,128,128]{2,1,0:T(8,128)S(1)}, f32[8,128,128]{2,1,0:T(8,128)S(1)}, u32[]{:S(2)}, u32[]{:S(2)}) collective-permute-start(f32[8,128,128]{2,1,0:T(8,128)S(1)} %get-tuple-element.19.refs_0_), channel_id=1, source_target_pairs={{1,0},{2,3},{128,1},{3,130},{129,128},{130,131},{161,129},{131,163... | collective-permute-start | bytes 1572872 | tf_op jit(solution)/shard_map/ppermute | solution.py:578
  84.1 3.9 %collective-permute-start.2 = (f32[8,128,128]{2,1,0:T(8,128)S(1)}, f32[8,128,128]{2,1,0:T(8,128)S(1)}, u32[]{:S(2)}, u32[]{:S(2)}) collective-permute-start(f32[8,128,128]{2,1,0:T(8,128)S(1)} %get-tuple-element.20), channel_id=1, source_target_pairs={{1,2},{2,1},{128,3},{3,128},{129,130},{130,129},{161,131},{131,161... | collective-permute-start | bytes 1572872 | tf_op jit(solution)/shard_map/ppermute | solution.py:579
  88.1 3.7 %collective-permute-done.9.refs_3_ = f32[8,128,128]{2,1,0:T(8,128)S(1)} collective-permute-done((f32[8,128,128]{2,1,0:T(8,128)S(1)}, f32[8,128,128]{2,1,0:T(8,128)S(1)}, u32[]{:S(2)}, u32[]{:S(2)}) %collective-permute-start.9) | collective-permute-done | bytes 524320 | tf_op jit(solution)/shard_map/ppermute | solution.py:579
  91.7 4.7 %time_filter.3 = (f32[8,128,128]{2,1,0:T(8,128)S(1)}, f32[8,128,128]{2,1,0:T(8,128)S(1)}, f32[8,128,128]{2,1,0:T(8,128)S(1)}, f32[8,128,128]{2,1,0:T(8,128)S(1)}) custom-call(f32[8,128,128]{2,1,0:T(8,128)S(1)} %get-tuple-element.25.refs_0_, f32[8,128,128]{2,1,0:T(8,128)S(1)} %collective-permute-done.7.refs_1_, ...), custom_call_target="tpu_custom_call" | custom-call | tf_op jit(solution)/shard_map/time_filter/pallas_call | solution.py:549
  96.4 1.3 collective-permute-start.10
  98.7 3.9 %collective-permute-start.12 = (f32[8,128,128]{2,1,0:T(8,128)S(1)}, f32[8,128,128]{2,1,0:T(8,128)S(1)}, u32[]{:S(2)}, u32[]{:S(2)}) collective-permute-start(f32[8,128,128]{2,1,0:T(8,128)S(1)} %get-tuple-element.30), channel_id=1, source_target_pairs={{2,1},{1,2},{3,128},{128,3},{130,129},{129,130},{131,161},{161,131... | collective-permute-start | bytes 1572872 | tf_op jit(solution)/shard_map/ppermute | solution.py:586
  102.6 2.5 %collective-permute-done.2.refs_3_ = f32[8,128,128]{2,1,0:T(8,128)S(1)} collective-permute-done((f32[8,128,128]{2,1,0:T(8,128)S(1)}, f32[8,128,128]{2,1,0:T(8,128)S(1)}, u32[]{:S(2)}, u32[]{:S(2)}) %collective-permute-start.2) | collective-permute-done | bytes 524320 | tf_op jit(solution)/shard_map/ppermute | solution.py:579
  105.1 4.7 %time_filter.2 = (f32[8,128,128]{2,1,0:T(8,128)S(1)}, f32[8,128,128]{2,1,0:T(8,128)S(1)}, f32[8,128,128]{2,1,0:T(8,128)S(1)}, f32[8,128,128]{2,1,0:T(8,128)S(1)}) custom-call(f32[8,128,128]{2,1,0:T(8,128)S(1)} %get-tuple-element.19.refs_0_, f32[8,128,128]{2,1,0:T(8,128)S(1)} %collective-permute-done.refs_1_, ...), custom_call_target="tpu_custom_call" | custom-call | tf_op jit(solution)/shard_map/time_filter/pallas_call | solution.py:549
  109.8 1.3 collective-permute-start.4
  112.1 3.5 %collective-permute-start.6 = (f32[8,128,128]{2,1,0:T(8,128)S(1)}, f32[8,128,128]{2,1,0:T(8,128)S(1)}, u32[]{:S(2)}, u32[]{:S(2)}) collective-permute-start(f32[8,128,128]{2,1,0:T(8,128)S(1)} %get-tuple-element.24), channel_id=1, source_target_pairs={{2,1},{1,2},{3,128},{128,3},{130,129},{129,130},{131,161},{161,131... | collective-permute-start | bytes 1572872 | tf_op jit(solution)/shard_map/ppermute | solution.py:586
  116.2 6.5 %collective-permute-done.4.halo_ref = f32[8,128,128]{2,1,0:T(8,128)S(1)} collective-permute-done((f32[8,128,128]{2,1,0:T(8,128)S(1)}, f32[8,128,128]{2,1,0:T(8,128)S(1)}, u32[]{:S(2)}, u32[]{:S(2)}) %collective-permute-start.4) | collective-permute-done | bytes 524320 | tf_op jit(solution)/shard_map/ppermute | solution.py:585
  122.6 2.8 %collective-permute-done.6.cross_ref = f32[8,128,128]{2,1,0:T(8,128)S(1)} collective-permute-done((f32[8,128,128]{2,1,0:T(8,128)S(1)}, f32[8,128,128]{2,1,0:T(8,128)S(1)}, u32[]{:S(2)}, u32[]{:S(2)}) %collective-permute-start.6) | collective-permute-done | bytes 524320 | tf_op jit(solution)/shard_map/ppermute | solution.py:586
  125.4 1.6 inverse_space.1
  127.0 59.2 %all_to_all.10 = f32[256,16,128]{2,1,0:T(8,128)S(1)} all-to-all(f32[256,16,128]{2,1,0:T(8,128)S(1)} %bitcast.6), channel_id=1, replica_groups=mesh['chan'=128,'tile'=2] {'chan','tile'}, dimensions={0} | all-to-all | bytes 4194304 | tf_op jit(solution)/shard_map/all_to_all | solution.py:590
  186.2 1.4 unplane.1
  (26 shorter events, 3.3 us)
Async XLA Ops:
  4.2 16.7 %copy-start.5 = (f32[8]{0:T(128)S(1)}, f32[8]{0:T(128)}, u32[]{:S(2)}) copy-start(f32[8]{0:T(128)} %gain_ref.1) | copy-start | bytes 100
  4.2 67.6 %all-to-all-start = ((f32[256,16,128]{2,1,0:T(8,128)}), f32[256,16,128]{2,1,0:T(8,128)}, u32[]{:S(2)}, u32[]{:S(2)}) async-start(f32[256,16,128]{2,1,0:T(8,128)} %bitcast.7), calls=%async_computation | async-start | bytes 4194304 | tf_op jit(solution)/shard_map/all_to_all | solution.py:571
  20.9 1.6 copy-start.4
  22.4 49.4 %copy-start = (bf16[32,128,384]{2,1,0:T(8,128)(2,1)S(1)}, bf16[32,128,384]{2,1,0:T(8,128)(2,1)}, u32[]{:S(2)}) copy-start(bf16[32,128,384]{2,1,0:T(8,128)(2,1)} %constant.8.clone.second_ref) | copy-start | bytes 9437188
  25.4 58.7 %collective-permute-start.3 = (f32[2,16,64,128]{3,2,1,0:T(8,128)}, f32[2,16,64,128]{3,2,1,0:T(8,128)}, u32[]{:S(2)}, u32[]{:S(2)}) collective-permute-start(f32[2,16,64,128]{3,2,1,0:T(8,128)} %gains.1.refs_4_), channel_id=1, source_target_pairs={{0,1},{1,0},{2,3},{3,2},{4,5},{5,4},{6,7},{7,6},{8,9},{9,8},{10,11... | collective-permute-start | bytes 3145736 | tf_op jit(solution)/shard_map/ppermute | solution.py:566
  74.6 13.4 %collective-permute-start.8 = (f32[8,128,128]{2,1,0:T(8,128)S(1)}, f32[8,128,128]{2,1,0:T(8,128)S(1)}, u32[]{:S(2)}, u32[]{:S(2)}) collective-permute-start(f32[8,128,128]{2,1,0:T(8,128)S(1)} %get-tuple-element.25.refs_0_), channel_id=1, source_target_pairs={{1,0},{2,3},{128,1},{3,130},{129,128},{130,131},{161,129},{131,163... | collective-permute-start | bytes 1572872 | tf_op jit(solution)/shard_map/ppermute | solution.py:578
  76.5 15.2 %collective-permute-start.9 = (f32[8,128,128]{2,1,0:T(8,128)S(1)}, f32[8,128,128]{2,1,0:T(8,128)S(1)}, u32[]{:S(2)}, u32[]{:S(2)}) collective-permute-start(f32[8,128,128]{2,1,0:T(8,128)S(1)} %get-tuple-element.26), channel_id=1, source_target_pairs={{1,2},{2,1},{128,3},{3,128},{129,130},{130,129},{161,131},{131,161... | collective-permute-start | bytes 1572872 | tf_op jit(solution)/shard_map/ppermute | solution.py:579
  81.2 10.5 %collective-permute-start.7 = (f32[8,128,128]{2,1,0:T(8,128)S(1)}, f32[8,128,128]{2,1,0:T(8,128)S(1)}, u32[]{:S(2)}, u32[]{:S(2)}) collective-permute-start(f32[8,128,128]{2,1,0:T(8,128)S(1)} %get-tuple-element.26), channel_id=1, source_target_pairs={{0,2},{2,0},{1,3},{3,1},{128,130},{130,128},{129,131},{131,129},{1... | collective-permute-start | bytes 1572872 | tf_op jit(solution)/shard_map/ppermute | solution.py:577
  81.3 10.4 %copy-start.2 = (bf16[2,512,512]{2,1,0:T(8,128)(2,1)S(1)}, bf16[2,512,512]{2,1,0:T(8,128)(2,1)}, u32[]{:S(2)}) copy-start(bf16[2,512,512]{2,1,0:T(8,128)(2,1)} %constant.11.clone.refs_7_) | copy-start | bytes 3145732
  81.3 10.4 %copy-start.3 = (bf16[2,512,512]{2,1,0:T(8,128)(2,1)S(1)}, bf16[2,512,512]{2,1,0:T(8,128)(2,1)}, u32[]{:S(2)}) copy-start(bf16[2,512,512]{2,1,0:T(8,128)(2,1)} %constant.10.clone.refs_6_) | copy-start | bytes 3145732
  81.9 16.8 %collective-permute-start.1 = (f32[8,128,128]{2,1,0:T(8,128)S(1)}, f32[8,128,128]{2,1,0:T(8,128)S(1)}, u32[]{:S(2)}, u32[]{:S(2)}) collective-permute-start(f32[8,128,128]{2,1,0:T(8,128)S(1)} %get-tuple-element.19.refs_0_), channel_id=1, source_target_pairs={{1,0},{2,3},{128,1},{3,130},{129,128},{130,131},{161,129},{131,163... | collective-permute-start | bytes 1572872 | tf_op jit(solution)/shard_map/ppermute | solution.py:578
  84.1 21.1 %collective-permute-start.2 = (f32[8,128,128]{2,1,0:T(8,128)S(1)}, f32[8,128,128]{2,1,0:T(8,128)S(1)}, u32[]{:S(2)}, u32[]{:S(2)}) collective-permute-start(f32[8,128,128]{2,1,0:T(8,128)S(1)} %get-tuple-element.20), channel_id=1, source_target_pairs={{1,2},{2,1},{128,3},{3,128},{129,130},{130,129},{161,131},{131,161... | collective-permute-start | bytes 1572872 | tf_op jit(solution)/shard_map/ppermute | solution.py:579
  88.0 17.2 %collective-permute-start = (f32[8,128,128]{2,1,0:T(8,128)S(1)}, f32[8,128,128]{2,1,0:T(8,128)S(1)}, u32[]{:S(2)}, u32[]{:S(2)}) collective-permute-start(f32[8,128,128]{2,1,0:T(8,128)S(1)} %get-tuple-element.20), channel_id=1, source_target_pairs={{0,2},{2,0},{1,3},{3,1},{128,130},{130,128},{129,131},{131,129},{1... | collective-permute-start | bytes 1572872 | tf_op jit(solution)/shard_map/ppermute | solution.py:577
  96.4 15.7 %collective-permute-start.10 = (f32[8,128,128]{2,1,0:T(8,128)S(1)}, f32[8,128,128]{2,1,0:T(8,128)S(1)}, u32[]{:S(2)}, u32[]{:S(2)}) collective-permute-start(f32[8,128,128]{2,1,0:T(8,128)S(1)} %get-tuple-element.28), channel_id=1, source_target_pairs={{0,1},{3,2},{1,128},{130,3},{128,129},{131,130},{129,161},{163,131... | collective-permute-start | bytes 1572872 | tf_op jit(solution)/shard_map/ppermute | solution.py:585
  97.7 17.9 %collective-permute-start.11 = (f32[8,128,128]{2,1,0:T(8,128)S(1)}, f32[8,128,128]{2,1,0:T(8,128)S(1)}, u32[]{:S(2)}, u32[]{:S(2)}) collective-permute-start(f32[8,128,128]{2,1,0:T(8,128)S(1)} %get-tuple-element.29), channel_id=1, source_target_pairs={{0,2},{2,0},{1,3},{3,1},{128,130},{130,128},{129,131},{131,129},{1... | collective-permute-start | bytes 1572872 | tf_op jit(solution)/shard_map/ppermute | solution.py:584
  98.7 16.9 %copy-start.1 = (bf16[32,128,384]{2,1,0:T(8,128)(2,1)S(1)}, bf16[32,128,384]{2,1,0:T(8,128)(2,1)}, u32[]{:S(2)}) copy-start(bf16[32,128,384]{2,1,0:T(8,128)(2,1)} %constant.9.clone.inv_ref) | copy-start | bytes 9437188
  98.7 16.9 %collective-permute-start.12 = (f32[8,128,128]{2,1,0:T(8,128)S(1)}, f32[8,128,128]{2,1,0:T(8,128)S(1)}, u32[]{:S(2)}, u32[]{:S(2)}) collective-permute-start(f32[8,128,128]{2,1,0:T(8,128)S(1)} %get-tuple-element.30), channel_id=1, source_target_pairs={{2,1},{1,2},{3,128},{128,3},{130,129},{129,130},{131,161},{161,131... | collective-permute-start | bytes 1572872 | tf_op jit(solution)/shard_map/ppermute | solution.py:586
  109.8 12.8 %collective-permute-start.4 = (f32[8,128,128]{2,1,0:T(8,128)S(1)}, f32[8,128,128]{2,1,0:T(8,128)S(1)}, u32[]{:S(2)}, u32[]{:S(2)}) collective-permute-start(f32[8,128,128]{2,1,0:T(8,128)S(1)} %get-tuple-element.22), channel_id=1, source_target_pairs={{0,1},{3,2},{1,128},{130,3},{128,129},{131,130},{129,161},{163,131... | collective-permute-start | bytes 1572872 | tf_op jit(solution)/shard_map/ppermute | solution.py:585
  111.1 11.5 %collective-permute-start.5 = (f32[8,128,128]{2,1,0:T(8,128)S(1)}, f32[8,128,128]{2,1,0:T(8,128)S(1)}, u32[]{:S(2)}, u32[]{:S(2)}) collective-permute-start(f32[8,128,128]{2,1,0:T(8,128)S(1)} %get-tuple-element.23), channel_id=1, source_target_pairs={{0,2},{2,0},{1,3},{3,1},{128,130},{130,128},{129,131},{131,129},{1... | collective-permute-start | bytes 1572872 | tf_op jit(solution)/shard_map/ppermute | solution.py:584
  112.1 13.4 %collective-permute-start.6 = (f32[8,128,128]{2,1,0:T(8,128)S(1)}, f32[8,128,128]{2,1,0:T(8,128)S(1)}, u32[]{:S(2)}, u32[]{:S(2)}) collective-permute-start(f32[8,128,128]{2,1,0:T(8,128)S(1)} %get-tuple-element.24), channel_id=1, source_target_pairs={{2,1},{1,2},{3,128},{128,3},{130,129},{129,130},{131,161},{161,131... | collective-permute-start | bytes 1572872 | tf_op jit(solution)/shard_map/ppermute | solution.py:586
